TPU v7x, 32 devices: a whole 2x2x4 slice. The times are simulated.
32 devices in a mesh: section: 2 (over core), row: 4 (over z), col: 4 (over y, x).
Axes of the slice: x: 2, y: 2, z: 4, core: 2. Of those that a mesh axis runs over, the one named last changes fastest.
Arguments:
- hidden_in: bfloat16 [2, 4, 1024, 1024], P(None, 'col', 'row'), may hold values from -6 to 6
- doc_ids: int32 [2, 4, 1024], P(None, 'col'), may hold values from 0 to 3, never falling along the last dimension, each value on 1 to 512 neighbouring positions
- qkv_weight: bfloat16 [2, 1024, 3, 1024], P('section', 'col', None, 'row'), may hold values from -0.1875 to 0.1875
- out_weight: bfloat16 [2, 1024, 1024], P('section', 'row', 'col'), may hold values from -1.5 to 1.5
- up_weight: bfloat16 [2, 1024, 4096], P('section', 'col', 'row'), may hold values from -0.1875 to 0.1875
- down_weight: bfloat16 [2, 4096, 1024], P('section', 'row', 'col'), may hold values from -0.09375 to 0.09375
- attn_gain: float32 [2, 1024], P('section', ('row', 'col')), may hold values from 0.5 to 1.5
- attn_shift: float32 [2, 1024], P('section', ('row', 'col')), may hold values from -1.75 to 1.75
- mlp_gain: float32 [2, 1024], P('section', ('row', 'col')), may hold values from 0.5 to 1.5
- mlp_shift: float32 [2, 1024], P('section', ('row', 'col')), may hold values from -1.75 to 1.75
- out_cotangent: bfloat16 [2, 4, 1024, 1024], P(None, 'col', 'row'), may hold values from -6 to 6
Outputs:
- layer_outputs: bfloat16 [2, 2, 4, 1024, 1024], P('section', None, 'col', 'row')
- input_grads: bfloat16 [2, 2, 4, 1024, 1024], P('section', None, 'col', 'row')
- qkv_grad: float32 [2, 1024, 3, 1024], P('section', 'col', None, 'row')
- out_grad: float32 [2, 1024, 1024], P('section', 'row', 'col')
- up_grad: float32 [2, 1024, 4096], P('section', 'col', 'row')
- down_grad: float32 [2, 4096, 1024], P('section', 'row', 'col')
- attn_gain_grad: float32 [2, 1024], P('section', ('row', 'col'))
- attn_shift_grad: float32 [2, 1024], P('section', ('row', 'col'))
- mlp_gain_grad: float32 [2, 1024], P('section', ('row', 'col'))
- mlp_shift_grad: float32 [2, 1024], P('section', ('row', 'col'))
Inputs may be any that keep to these rules, and one draw needn't show every extreme that they name: `doc_ids`: in each sequence the document numbers never fall, every number appears, each document has 1 to 512 tokens and one has exactly 512.
All inputs are finite; a program needn't handle non-finite values.
Results may differ from a plain program's by a relative error of at most 0.02.
Values may be sent and summed in bfloat16 or wider, within the bound.
No kernel may reach another device: no remote copies, remote signals or barrier semaphores. Data moves between devices by JAX's collectives and lax.ppermute only.
A program may use at most 256 MiB of HBM per device.

v0:
```python
from functools import partial
import math

import jax
import jax.numpy as jnp
from jax import lax
from jax.sharding import PartitionSpec as P

HEAD_DIM = 64
ROT = 16


EPSILON = 1e-05
NEG_FILL = -1e30


def from_behind(block, axis, distance):
    devices = range(lax.axis_size(axis))
    route = [(i - distance, i) for i in devices if i - distance in devices]
    return lax.ppermute(block, axis, route)


def positions_of(docs):
    length = docs.shape[0]
    index = jnp.arange(length, dtype=jnp.int32)
    starts = jnp.concatenate([jnp.ones((1,), jnp.bool_), docs[1:] != docs[:-1]])
    first = lax.cummax(jnp.where(starts, index, 0), axis=0)
    return index - first


def rotary_tables(docs):
    half = ROT // 2
    freqs = 10000.0 ** (-2.0 * jnp.arange(half, dtype=jnp.float32) / ROT)
    angles = positions_of(docs).astype(jnp.float32)[:, None] * freqs[None, :]
    return (jnp.cos(angles)[:, None, :], jnp.sin(angles)[:, None, :])


def rotate(values, cosine, sine):
    half = ROT // 2
    front = values[..., :half]
    back = values[..., half:ROT]
    return jnp.concatenate(
        [front * cosine - back * sine, back * cosine + front * sine, values[..., ROT:]], axis=-1
    )


def rotate_back(grads, cosine, sine):
    half = ROT // 2
    front = grads[..., :half]
    back = grads[..., half:ROT]
    return jnp.concatenate(
        [front * cosine + back * sine, back * cosine - front * sine, grads[..., ROT:]], axis=-1
    )


def normalize(full):
    wide = full.astype(jnp.float32)
    center = wide - jnp.mean(wide, axis=-1, keepdims=True)
    scale = lax.rsqrt(jnp.mean(center * center, axis=-1, keepdims=True) + EPSILON)
    return (center * scale, scale)


def block_mask(docs, start, size):
    rows = start + jnp.arange(size, dtype=jnp.int32)
    cols = jnp.arange(docs.shape[0], dtype=jnp.int32)
    row_docs = lax.dynamic_slice_in_dim(docs, start, size)
    return (row_docs[:, None] == docs[None, :]) & (cols[None, :] <= rows[:, None])


def block_scores(query, key, docs, start, block):
    factor = 1.0 / math.sqrt(query.shape[2])
    rows = lax.dynamic_slice_in_dim(query, start, block)
    scores = jnp.einsum("qhd,khd->hqk", rows, key, preferred_element_type=jnp.float32) * factor
    allowed = block_mask(docs, start, block)[None]
    return (rows, jnp.where(allowed, scores, NEG_FILL))


def attend_forward(query, key, value, docs):
    length, heads, width = query.shape
    block = min(512, length)

    def one_block(number):
        start = number * block
        rows, scores = block_scores(query, key, docs, start, block)
        peak = jnp.max(scores, axis=-1, keepdims=True)
        raised = jnp.exp(scores - peak)
        total = jnp.sum(raised, axis=-1, keepdims=True)
        probs = (raised / total).astype(jnp.bfloat16)
        context = jnp.einsum(
            "hqk,khd->qhd", probs, value, preferred_element_type=jnp.float32
        ).astype(jnp.bfloat16)
        return (context, (peak + jnp.log(total))[..., 0])

    context, logsum = lax.map(one_block, jnp.arange(length // block, dtype=jnp.int32))
    return (context.reshape(length, heads, width), logsum)


def attend_backward(query, key, value, docs, logsum, context_grad):
    length, heads, width = query.shape
    block = min(512, length)
    factor = 1.0 / math.sqrt(width)

    def one_block(carry, inputs):
        key_grad, value_grad = carry
        number, block_logsum = inputs
        start = number * block
        rows, scores = block_scores(query, key, docs, start, block)
        rows_grad = lax.dynamic_slice_in_dim(context_grad, start, block)
        probs_full = jnp.exp(scores - block_logsum[:, :, None])
        probs = probs_full.astype(jnp.bfloat16)
        context = jnp.einsum(
            "hqk,khd->qhd", probs, value, preferred_element_type=jnp.float32
        ).astype(jnp.bfloat16)
        probs_grad = jnp.einsum(
            "qhd,khd->hqk", rows_grad, value, preferred_element_type=jnp.float32
        )
        inner = jnp.sum(probs_grad * probs_full, axis=-1, keepdims=True)
        score_grad = (probs_full * (probs_grad - inner)).astype(jnp.bfloat16)
        query_grad = (
            jnp.einsum("hqk,khd->qhd", score_grad, key, preferred_element_type=jnp.float32) * factor
        )
        key_grad = (
            key_grad
            + jnp.einsum("hqk,qhd->khd", score_grad, rows, preferred_element_type=jnp.float32)
            * factor
        )
        value_grad = value_grad + jnp.einsum(
            "hqk,qhd->khd", probs, rows_grad, preferred_element_type=jnp.float32
        )
        return ((key_grad, value_grad), (context, query_grad))

    zeros = jnp.zeros((length, heads, width), jnp.float32)
    numbers = jnp.arange(length // block, dtype=jnp.int32)
    (key_grad, value_grad), (context, query_grad) = lax.scan(
        one_block, (zeros, zeros), (numbers, logsum)
    )
    return (
        context.reshape(length, heads * width),
        query_grad.reshape(length, heads, width),
        key_grad,
        value_grad,
    )


def gather_features(shard):
    return lax.all_gather(shard, "row", axis=0, tiled=True)


def recompute_inputs(full, docs, norms, weights):
    gain_a, shift_a, gain_m, shift_m = norms
    qkv_full = weights[0]
    normed, scale = normalize(full)
    attn_in = (normed * gain_a + shift_a).astype(jnp.bfloat16)
    feed_in = (normed * gain_m + shift_m).astype(jnp.bfloat16)
    length = full.shape[0]
    heads_here = qkv_full.shape[2] // HEAD_DIM
    project = jnp.einsum("td,dke->tke", attn_in, qkv_full, preferred_element_type=jnp.float32)
    cosine, sine = rotary_tables(docs)
    query = rotate(project[:, 0].reshape(length, heads_here, HEAD_DIM), cosine, sine).astype(
        jnp.bfloat16
    )
    key = rotate(project[:, 1].reshape(length, heads_here, HEAD_DIM), cosine, sine).astype(
        jnp.bfloat16
    )
    value = project[:, 2].reshape(length, heads_here, HEAD_DIM).astype(jnp.bfloat16)
    pre = jnp.dot(feed_in, weights[2], preferred_element_type=jnp.float32)
    return (normed, scale, attn_in, feed_in, query, key, value, pre, cosine, sine)


def layer_forward(shard, docs, full, norms, weights):
    normed, scale, attn_in, feed_in, query, key, value, pre, cosine, sine = recompute_inputs(
        full, docs, norms, weights
    )
    length = full.shape[0]
    context, logsum = attend_forward(query, key, value, docs)
    active = jax.nn.gelu(pre, approximate=False).astype(jnp.bfloat16)
    partial_sum = jnp.dot(
        context.reshape(length, -1), weights[1], preferred_element_type=jnp.float32
    )
    partial_sum = partial_sum + jnp.dot(active, weights[3], preferred_element_type=jnp.float32)
    branch = lax.psum_scatter(
        partial_sum.astype(jnp.bfloat16), "row", scatter_dimension=0, tiled=True
    ).astype(jnp.float32)
    return ((shard.astype(jnp.float32) + branch).astype(jnp.bfloat16), logsum)


def layer_backward(docs, full, logsum, upstream, norms, weights):
    gain_a, shift_a, gain_m, shift_m = norms
    qkv_full, out_full, up_full, down_full = weights
    normed, scale, attn_in, feed_in, query, key, value, pre, cosine, sine = recompute_inputs(
        full, docs, norms, weights
    )
    length = full.shape[0]
    heads_here = query.shape[1]
    active = jax.nn.gelu(pre, approximate=False).astype(jnp.bfloat16)
    upstream_full = lax.all_gather(upstream, "row", axis=0, tiled=True)
    down_part = jnp.einsum("tf,td->fd", active, upstream_full, preferred_element_type=jnp.float32)
    act_grad = jnp.einsum("td,fd->tf", upstream_full, down_full, preferred_element_type=jnp.float32)
    pre_grad = jax.vjp(partial(jax.nn.gelu, approximate=False), pre)[1](act_grad)[0].astype(
        jnp.bfloat16
    )
    up_part = jnp.einsum("td,tf->df", feed_in, pre_grad, preferred_element_type=jnp.float32)
    feed_grad = jnp.einsum("tf,df->td", pre_grad, up_full, preferred_element_type=jnp.float32)
    context_grad = jnp.einsum(
        "td,ed->te", upstream_full, out_full, preferred_element_type=jnp.float32
    ).astype(jnp.bfloat16)
    context_grad = context_grad.reshape(length, heads_here, HEAD_DIM)
    context, query_grad, key_grad, value_grad = attend_backward(
        query, key, value, docs, logsum, context_grad
    )
    out_part = jnp.einsum("te,td->ed", context, upstream_full, preferred_element_type=jnp.float32)
    project_grad = jnp.stack(
        [
            rotate_back(query_grad, cosine, sine).reshape(length, -1),
            rotate_back(key_grad, cosine, sine).reshape(length, -1),
            value_grad.reshape(length, -1),
        ],
        axis=1,
    ).astype(jnp.bfloat16)
    qkv_part = jnp.einsum("td,tke->dke", attn_in, project_grad, preferred_element_type=jnp.float32)
    attn_grad = jnp.einsum(
        "tke,dke->td", project_grad, qkv_full, preferred_element_type=jnp.float32
    )
    own_rows = upstream.shape[0]
    offset = lax.axis_index("row") * own_rows
    normed_part = lax.dynamic_slice_in_dim(normed, offset, own_rows, 0)
    scale_part = lax.dynamic_slice_in_dim(scale, offset, own_rows, 0)
    attn_piece, feed_piece = (
        lax.psum_scatter(
            attn_grad.astype(jnp.bfloat16), "row", scatter_dimension=0, tiled=True
        ).astype(jnp.float32),
        lax.psum_scatter(
            feed_grad.astype(jnp.bfloat16), "row", scatter_dimension=0, tiled=True
        ).astype(jnp.float32),
    )
    normed_grad = attn_piece * gain_a + feed_piece * gain_m
    gain_terms = (
        jnp.sum(attn_piece * normed_part, axis=0),
        jnp.sum(attn_piece, axis=0),
        jnp.sum(feed_piece * normed_part, axis=0),
        jnp.sum(feed_piece, axis=0),
    )
    row_sum = jnp.sum(normed_grad, axis=-1)
    cross_sum = jnp.sum(normed_grad * normed_part, axis=-1)
    count = full.shape[1]
    input_grad = upstream.astype(jnp.float32) + scale_part * (
        normed_grad - row_sum[:, None] / count - normed_part * cross_sum[:, None] / count
    )
    return (input_grad, (qkv_part, out_part, up_part, down_part), gain_terms)


def shards(
    hidden_in,
    doc_ids,
    qkv_weight,
    out_weight,
    up_weight,
    down_weight,
    attn_gain,
    attn_shift,
    mlp_gain,
    mlp_shift,
    out_cotangent,
):
    micro = hidden_in.shape[0]
    first_section = lax.axis_index("section") == 0
    norms = (
        lax.all_gather(attn_gain[0], ("row", "col"), axis=0, tiled=True),
        lax.all_gather(attn_shift[0], ("row", "col"), axis=0, tiled=True),
        lax.all_gather(mlp_gain[0], ("row", "col"), axis=0, tiled=True),
        lax.all_gather(mlp_shift[0], ("row", "col"), axis=0, tiled=True),
    )
    weights = (
        lax.all_gather(qkv_weight[0], "col", axis=0, tiled=True),
        lax.all_gather(out_weight[0], "col", axis=1, tiled=True),
        lax.all_gather(up_weight[0], "col", axis=0, tiled=True),
        lax.all_gather(down_weight[0], "col", axis=1, tiled=True),
    )
    received = jnp.zeros_like(hidden_in[0, 0])
    tick_inputs, tick_docs, tick_fulls, tick_outputs, tick_logsums = ([], [], [], [], [])
    for tick in range(micro + 1):
        own = hidden_in[min(tick, micro - 1), 0]
        shard = jnp.where(first_section, own, received)
        docs = jnp.where(
            first_section, doc_ids[min(tick, micro - 1), 0], doc_ids[max(tick - 1, 0), 0]
        )
        full = gather_features(shard)
        result, logsum = layer_forward(shard, docs, full, norms, weights)
        tick_inputs.append(shard)
        tick_docs.append(docs)
        tick_fulls.append(full)
        tick_outputs.append(result)
        tick_logsums.append(logsum)
        if tick < micro:
            received = from_behind(result, "section", 1)
    outputs = jnp.stack(
        [
            jnp.where(first_section, tick_outputs[number], tick_outputs[number + 1])
            for number in range(micro)
        ]
    )
    received = jnp.zeros_like(hidden_in[0, 0])
    matrix_totals = None
    gain_totals = None
    tick_grads = []
    for tick in range(micro + 1):
        early = max(tick - 1, 0)
        later = min(tick + 1, micro)
        if tick < micro:
            given = out_cotangent[tick, 0]
        else:
            given = jnp.zeros_like(out_cotangent[0, 0])
        upstream = jnp.where(first_section, received, given)
        shard = jnp.where(first_section, tick_inputs[early], tick_inputs[later])
        docs = jnp.where(first_section, tick_docs[early], tick_docs[later])
        logsum = jnp.where(first_section, tick_logsums[early], tick_logsums[later])
        full = gather_features(shard)
        input_grad, matrices, gain_terms = layer_backward(
            docs, full, logsum, upstream, norms, weights
        )
        if matrix_totals is None:
            matrix_totals = matrices
            gain_totals = gain_terms
        else:
            matrix_totals = jax.tree.map(jnp.add, matrix_totals, matrices)
            gain_totals = jax.tree.map(jnp.add, gain_totals, gain_terms)
        grad_low = input_grad.astype(jnp.bfloat16)
        tick_grads.append(grad_low)
        if tick < micro:
            received = from_behind(grad_low, "section", -1)
    grads_in = jnp.stack(
        [
            jnp.where(first_section, tick_grads[number + 1], tick_grads[number])
            for number in range(micro)
        ]
    )
    qkv_sum, out_sum, up_sum, down_sum = matrix_totals
    gain_a_sum, shift_a_sum, gain_m_sum, shift_m_sum = gain_totals
    qkv_total, out_total, up_total, down_total = (
        lax.psum_scatter(
            qkv_sum.astype(jnp.bfloat16), "col", scatter_dimension=0, tiled=True
        ).astype(jnp.float32),
        lax.psum_scatter(
            out_sum.astype(jnp.bfloat16), "col", scatter_dimension=1, tiled=True
        ).astype(jnp.float32),
        lax.psum_scatter(
            up_sum.astype(jnp.bfloat16), "col", scatter_dimension=0, tiled=True
        ).astype(jnp.float32),
        lax.psum_scatter(
            down_sum.astype(jnp.bfloat16), "col", scatter_dimension=1, tiled=True
        ).astype(jnp.float32),
    )
    gain_a_total, shift_a_total, gain_m_total, shift_m_total = (
        lax.psum_scatter(gain_a_sum, ("row", "col"), scatter_dimension=0, tiled=True),
        lax.psum_scatter(shift_a_sum, ("row", "col"), scatter_dimension=0, tiled=True),
        lax.psum_scatter(gain_m_sum, ("row", "col"), scatter_dimension=0, tiled=True),
        lax.psum_scatter(shift_m_sum, ("row", "col"), scatter_dimension=0, tiled=True),
    )
    return (
        outputs[None, :, None],
        grads_in[None, :, None],
        qkv_total[None],
        out_total[None],
        up_total[None],
        down_total[None],
        gain_a_total[None],
        shift_a_total[None],
        gain_m_total[None],
        shift_m_total[None],
    )


def solution(mesh):
    placed = (
        P(None, "col", "row", None),
        P(None, "col", None),
        P("section", "col", None, "row"),
        P("section", "row", "col"),
        P("section", "col", "row"),
        P("section", "row", "col"),
        P("section", ("row", "col")),
        P("section", ("row", "col")),
        P("section", ("row", "col")),
        P("section", ("row", "col")),
        P(None, "col", "row", None),
    )
    return jax.shard_map(
        shards,
        mesh=mesh,
        in_specs=placed,
        out_specs=(
            P("section", None, "col", "row", None),
            P("section", None, "col", "row", None),
            P("section", "col", None, "row"),
            P("section", "row", "col"),
            P("section", "col", "row"),
            P("section", "row", "col"),
            P("section", ("row", "col")),
            P("section", ("row", "col")),
            P("section", ("row", "col")),
            P("section", ("row", "col")),
        ),
        check_vma=False,
    )
```

profile of v0, /device:TPU:1, one launch (start us, length us, event | category | flops | bytes accessed | tf_op | source)
XLA Modules:
  0.0 1403.4 jit_solution(10198626544265135634)
XLA Ops:
  18.8 13.1 all-gather.4
  33.7 62.7 %all-reduce.9 = (f32[1024]{0:T(1024)S(1)}, f32[1024]{0:T(1024)S(1)}, f32[1024]{0:T(1024)S(1)}, f32[1024]{0:T(1024)S(1)}) all-reduce(f32[1024]{0:T(1024)S(1)} %bitcast_dynamic-update-slice_fusion.3, f32[1024]{0:T(1024)S(1)} %bitcast_dynamic-update-slice_fusion.4, ...), channel_id=8, replica_groups=mesh['section'=2,'row'=4,'col'=4] {'row','col'}, use_global_device_ids=true, to_apply=%add.3 | all-reduce | flops 4096 | bytes 32768
  108.8 21.2 %while.87 = (s32[]{:T(128)}, bf16[2,512,4,64]{1,3,2,0:T(8,128)(2,1)}, f32[2,4,512]{2,1,0:T(4,128)S(1)}, s32[2]{0:T(128)S(1)}, s32[1024]{0:T(1024)S(1)}, /*index=...) while((s32[]{:T(128)}, ...), condition=%wide.region_7.8_spmd, body=%wide.region_4.7_spmd.sunk | while | flops 563739136 | bytes 31013596 | solution.py:94
  131.7 33.6 %all-gather.43.cloned.1.call-done = bf16[1,1024,1024]{2,1,0:T(8,128)(2,1)} async-done(((bf16[1,1024,256]{2,1,0:T(8,128)(2,1)}), bf16[1,1024,1024]{2,1,0:T(8,128)(2,1)}) %all-gather.43.cloned.1.call-update) | async-done | bytes 2097168 | tf_op jit(solution)/shard_map/all_gather | solution.py:277
  165.3 17.0 %fusion.220 = f32[1024,1024]{1,0:T(8,128)} fusion(bf16[1,1024,1024]{2,1,0:T(8,128)(2,1)} %all-gather.43.cloned.1.call-done, bf16[1,1,1024,1024]{3,2,1,0:T(8,128)(2,1)S(1)} %copy-done.42, bf16[1,1024,1024]{2,1,0:T(8,128)(2,1)} %all-gather.41.cloned.1.call-done, f32[1024]{0:T(1024)S(1)} %get-tuple-element.643, f32[1024]{0:T(1024)S(1)} %get-tuple-element.644, ...), kind=kOutput, calls=%fused_computation.341 | convolution fusion | flops 4369416192 | bytes 10502144 | tf_op jit(solution)/shard_map/dot_general | solution.py:180
  186.8 43.8 %reduce-scatter.14.cloned.1.call-done = bf16[256,1024]{1,0:T(8,128)(2,1)} async-done(((bf16[1024,1024]{1,0:T(8,128)(2,1)}), bf16[256,1024]{1,0:T(8,128)(2,1)}) %reduce-scatter.14.cloned.1.call-update) | async-done | bytes 524304 | tf_op jit(solution)/shard_map/reduce_scatter | solution.py:181
  236.8 45.1 %all-gather.23.cloned.1.call-done = bf16[1024,1024]{1,0:T(8,128)(2,1)} async-done(((bf16[256,1024]{1,0:T(8,128)(2,1)}), bf16[1024,1024]{1,0:T(8,128)(2,1)}) %all-gather.23.cloned.1.call-update) | async-done | bytes 2097168 | tf_op jit(solution)/shard_map/all_gather | solution.py:146
  289.7 18.2 %while.88 = (s32[]{:T(128)}, bf16[2,512,4,64]{1,3,2,0:T(8,128)(2,1)S(1)}, f32[2,4,512]{2,1,0:T(4,128)S(1)}, s32[2]{0:T(128)S(1)}, s32[1024]{0:T(1024)S(1)}, /*in...) while((s32[]{:T(128)}, ...), condition=%wide.region_16.17_spmd, body=%wide.region_13.16_spmd.sunk | while | flops 563739136 | bytes 31013088 | solution.py:94
  309.3 17.6 %fusion.218 = f32[1024,1024]{1,0:T(8,128)} fusion(bf16[1,1024,1024]{2,1,0:T(8,128)(2,1)} %all-gather.43.cloned.1.call-done, bf16[1024,1024]{1,0:T(8,128)(2,1)} %all-gather.23.cloned.1.call-done, bf16[1,1024,1024]{2,1,0:T(8,128)(2,1)} %all-gather.41.cloned.1.call-done, f32[1024]{0:T(1024)S(1)} %get-tuple-element.643, f32[1024]{0:T(1024)S(1)} %get-tuple-element.644, ...), kind=kOutput, calls=%fused_computation.339 | convolution fusion | flops 4369416192 | bytes 10502144 | tf_op jit(solution)/shard_map/dot_general | solution.py:180
  333.3 40.9 %reduce-scatter.16.cloned.1.call-done = bf16[256,1024]{1,0:T(8,128)(2,1)} async-done(((bf16[1024,1024]{1,0:T(8,128)(2,1)}), bf16[256,1024]{1,0:T(8,128)(2,1)}) %reduce-scatter.16.cloned.1.call-update) | async-done | bytes 524304 | tf_op jit(solution)/shard_map/reduce_scatter | solution.py:181
  381.3 40.5 %all-gather.45.cloned.1.call-done = bf16[1,1,1024,1024]{3,2,1,0:T(8,128)(2,1)} async-done(((bf16[1,1,256,1024]{3,2,1,0:T(8,128)(2,1)}), bf16[1,1,1024,1024]{3,2,1,0:T(8,128)(2,1)}) %all-gather.45.cloned.1.call-update) | async-done | bytes 2097168 | tf_op jit(solution)/shard_map/all_gather | solution.py:196
  424.9 43.7 %all-gather.27.cloned.1.call-done = bf16[1024,1024]{1,0:T(8,128)(2,1)} async-done(((bf16[256,1024]{1,0:T(8,128)(2,1)}), bf16[1024,1024]{1,0:T(8,128)(2,1)}) %all-gather.27.cloned.1.call-update) | async-done | bytes 2097168 | tf_op jit(solution)/shard_map/all_gather | solution.py:146
  480.0 34.7 %all-gather.25.cloned.1.call-done = bf16[1024,1024]{1,0:T(8,128)(2,1)} async-done(((bf16[256,1024]{1,0:T(8,128)(2,1)}), bf16[1024,1024]{1,0:T(8,128)(2,1)}) %all-gather.25.cloned.1.call-update) | async-done | bytes 2097168 | tf_op jit(solution)/shard_map/all_gather | solution.py:146
  524.2 21.1 %while.89 = (s32[]{:T(128)}, bf16[2,512,4,64]{1,3,2,0:T(8,128)(2,1)}, f32[2,4,512]{2,1,0:T(4,128)S(1)}, s32[2]{0:T(128)S(1)}, s32[1024]{0:T(1024)S(1)}, /*index=...) while((s32[]{:T(128)}, ...), condition=%wide.region_25.26_spmd, body=%wide.region_22.25_spmd.sunk | while | flops 563739136 | bytes 31013596 | solution.py:94
  547.0 17.6 %fusion.216 = f32[1024,1024]{1,0:T(8,128)} fusion(bf16[1,1024,1024]{2,1,0:T(8,128)(2,1)} %all-gather.43.cloned.1.call-done, bf16[1024,1024]{1,0:T(8,128)(2,1)} %all-gather.25.cloned.1.call-done, bf16[1,1024,1024]{2,1,0:T(8,128)(2,1)} %all-gather.41.cloned.1.call-done, f32[1024]{0:T(1024)S(1)} %get-tuple-element.643, f32[1024]{0:T(1024)S(1)} %get-tuple-element.644, ...), kind=kOutput, calls=%fused_computation.337 | convolution fusion | flops 4369416192 | bytes 10502144 | tf_op jit(solution)/shard_map/dot_general | solution.py:180
  569.1 12.2 fusion.142
  593.6 70.9 %while.90 = (s32[]{:T(128)}, f32[1024,4,64]{0,2,1:T(8,128)S(1)}, f32[1024,4,64]{0,2,1:T(8,128)}, bf16[2,512,4,64]{1,3,2,0:T(8,128)(2,1)}, f32[2,512,4,64]{1,0,3,...) while((s32[]{:T(128)}, f32[1024,4,64]{0,2,1:T(8,128)S(1)}, ...), condition=%wide.region_33.34_spmd.clone, body=%wide.region_31.33_spmd.clone.sunk | while | flops 1653602816 | bytes 176503760 | solution.py:134
  606.6 10.4 dynamic_update_slice.73
  681.9 36.8 %reduce-scatter.20.cloned.1.call-done = bf16[256,1024]{1,0:T(8,128)(2,1)} async-done(((bf16[1024,1024]{1,0:T(8,128)(2,1)}), bf16[256,1024]{1,0:T(8,128)(2,1)}) %reduce-scatter.20.cloned.1.call-update) | async-done | bytes 524304 | tf_op jit(solution)/shard_map/reduce_scatter | solution.py:229
  729.6 36.7 %all-gather.29.cloned.1.call-done = bf16[1024,1024]{1,0:T(8,128)(2,1)} async-done(((bf16[256,1024]{1,0:T(8,128)(2,1)}), bf16[1024,1024]{1,0:T(8,128)(2,1)}) %all-gather.29.cloned.1.call-update) | async-done | bytes 2097168 | tf_op jit(solution)/shard_map/all_gather | solution.py:146
  775.1 37.3 %all-gather.31.cloned.1.call-done = bf16[1024,1024]{1,0:T(8,128)(2,1)} async-done(((bf16[256,1024]{1,0:T(8,128)(2,1)}), bf16[1024,1024]{1,0:T(8,128)(2,1)}) %all-gather.31.cloned.1.call-update) | async-done | bytes 2097168 | tf_op jit(solution)/shard_map/all_gather | solution.py:196
  817.7 70.1 %while.91 = (s32[]{:T(128)}, f32[1024,4,64]{0,2,1:T(8,128)S(1)}, f32[1024,4,64]{0,2,1:T(8,128)}, bf16[2,512,4,64]{1,3,2,0:T(8,128)(2,1)}, f32[2,512,4,64]{1,0,3,...) while((s32[]{:T(128)}, f32[1024,4,64]{0,2,1:T(8,128)S(1)}, ...), condition=%wide.region_44.45_spmd.clone, body=%wide.region_42.44_spmd.clone.sunk | while | flops 1653602816 | bytes 176503760 | solution.py:134
  897.9 12.2 fusion.143
  922.4 17.8 %reduce-scatter.24.cloned.1.call-done = bf16[256,1024]{1,0:T(8,128)(2,1)} async-done(((bf16[1024,1024]{1,0:T(8,128)(2,1)}), bf16[256,1024]{1,0:T(8,128)(2,1)}) %reduce-scatter.24.cloned.1.call-update) | async-done | bytes 524304 | tf_op jit(solution)/shard_map/reduce_scatter | solution.py:229
  940.2 45.4 %reduce-scatter.26.cloned.1.call-done = bf16[256,1024]{1,0:T(8,128)(2,1)} async-done(((bf16[1024,1024]{1,0:T(8,128)(2,1)}), bf16[256,1024]{1,0:T(8,128)(2,1)}) %reduce-scatter.26.cloned.1.call-update) | async-done | bytes 524304 | tf_op jit(solution)/shard_map/reduce_scatter | solution.py:232
  995.2 37.8 %all-gather.33.cloned.1.call-done = bf16[1024,1024]{1,0:T(8,128)(2,1)} async-done(((bf16[256,1024]{1,0:T(8,128)(2,1)}), bf16[1024,1024]{1,0:T(8,128)(2,1)}) %all-gather.33.cloned.1.call-update) | async-done | bytes 2097168 | tf_op jit(solution)/shard_map/all_gather | solution.py:146
  1056.8 27.4 %all-gather.35.cloned.1.call-done = bf16[1024,1024]{1,0:T(8,128)(2,1)} async-done(((bf16[256,1024]{1,0:T(8,128)(2,1)}), bf16[1024,1024]{1,0:T(8,128)(2,1)}) %all-gather.35.cloned.1.call-update) | async-done | bytes 2097168 | tf_op jit(solution)/shard_map/all_gather | solution.py:196
  1089.4 70.7 %while.92 = (s32[]{:T(128)}, f32[1024,4,64]{0,2,1:T(8,128)S(1)}, f32[1024,4,64]{0,2,1:T(8,128)}, bf16[2,512,4,64]{1,3,2,0:T(8,128)(2,1)}, f32[2,512,4,64]{1,0,3,...) while((s32[]{:T(128)}, f32[1024,4,64]{0,2,1:T(8,128)S(1)}, ...), condition=%wide.region_55.56_spmd.clone, body=%wide.region_53.55_spmd.clone.sunk | while | flops 1653602816 | bytes 176503760 | solution.py:134
  1187.4 12.2 fusion.144
  1244.1 27.4 %reduce-scatter.28.cloned.1.call-done = bf16[256,1024]{1,0:T(8,128)(2,1)} async-done(((bf16[1024,1024]{1,0:T(8,128)(2,1)}), bf16[256,1024]{1,0:T(8,128)(2,1)}) %reduce-scatter.28.cloned.1.call-update) | async-done | bytes 524304 | tf_op jit(solution)/shard_map/reduce_scatter | solution.py:229
  1271.5 45.6 %reduce-scatter.30.cloned.1.call-done = bf16[256,1024]{1,0:T(8,128)(2,1)} async-done(((bf16[1024,1024]{1,0:T(8,128)(2,1)}), bf16[256,1024]{1,0:T(8,128)(2,1)}) %reduce-scatter.30.cloned.1.call-update) | async-done | bytes 524304 | tf_op jit(solution)/shard_map/reduce_scatter | solution.py:232
  1319.4 61.9 %all-reduce.8 = (f32[1024]{0:T(1024)S(1)}, f32[1024]{0:T(1024)S(1)}, f32[1024]{0:T(1024)S(1)}, f32[1024]{0:T(1024)S(1)}) all-reduce(f32[1024]{0:T(1024)S(1)} %add_add_fusion.3, f32[1024]{0:T(1024)S(1)} %add_add_fusion.2, f32[1024]{0:T(1024)S(1)} %add_add_fusion.1, ...), channel_id=25, replica_groups=mesh['section'=2,'row'=4,'col'=4] {'row','col'}, use_global_device_ids=true, to_apply=%region_67.68.clone | all-reduce | flops 4096 | bytes 32768
  (844 shorter events, 543.3 us)
Async XLA Ops:
  7.2 90.6 %all-gather.37.cloned.1.call-start = ((), (), s32[]{:S(2)}) async-start(), calls=%async_computation.33 | async-start | bytes 2621440 | tf_op jit(solution)/shard_map/all_gather | solution.py:146
  9.2 93.2 %all-gather.39.cloned.1.call-start = ((), (), s32[]{:S(2)}) async-start(), calls=%async_computation.34 | async-start | bytes 1966080 | tf_op jit(solution)/shard_map/all_gather | solution.py:274
  11.2 120.5 %all-gather.41.cloned.1.call-start = ((), (), s32[]{:S(2)}) async-start(), calls=%async_computation.35 | async-start | bytes 2621440 | tf_op jit(solution)/shard_map/all_gather | solution.py:276
  11.9 153.4 %all-gather.43.cloned.1.call-start = ((), (), s32[]{:S(2)}) async-start(), calls=%async_computation.36 | async-start | bytes 2621440 | tf_op jit(solution)/shard_map/all_gather | solution.py:277
  12.5 218.1 %reduce-scatter.14.cloned.1.call-start = ((), (), s32[]{:S(2)}) async-start(), calls=%async_computation.13 | async-start | bytes 2621440 | tf_op jit(solution)/shard_map/reduce_scatter | solution.py:181
  31.9 532.7 %copy-start.30 = (bf16[1,256,1024]{2,1,0:T(8,128)(2,1)}, bf16[1,256,1024]{2,1,0:T(8,128)(2,1)S(1)}, u32[]{:S(2)}) copy-start(bf16[1,256,1024]{2,1,0:T(8,128)(2,1)S(1)} %all-gather.4) | copy-start | bytes 1572868
  96.4 472.6 %copy-start.110 = (f32[1024]{0:T(1024)}, f32[1024]{0:T(1024)S(1)}, u32[]{:S(2)}) copy-start(f32[1024]{0:T(1024)S(1)} %get-tuple-element.644) | copy-start | bytes 12292
  96.4 472.6 %copy-start.156 = (f32[1024]{0:T(1024)}, f32[1024]{0:T(1024)S(1)}, u32[]{:S(2)}) copy-start(f32[1024]{0:T(1024)S(1)} %get-tuple-element.643) | copy-start | bytes 12292
  186.7 95.1 %all-gather.23.cloned.1.call-start = ((), (), s32[]{:S(2)}) async-start(), calls=%async_computation.14 | async-start | bytes 2621440 | tf_op jit(solution)/shard_map/all_gather | solution.py:146
  231.8 3.8 collective-permute-start
  236.7 137.4 %reduce-scatter.16.cloned.1.call-start = ((), (), s32[]{:S(2)}) async-start(), calls=%async_computation.15 | async-start | bytes 2621440 | tf_op jit(solution)/shard_map/reduce_scatter | solution.py:181
  331.6 90.2 %all-gather.45.cloned.1.call-start = ((), (), s32[]{:S(2)}) async-start(), calls=%async_computation.37 | async-start | bytes 2621440 | tf_op jit(solution)/shard_map/all_gather | solution.py:196
  332.5 136.1 %all-gather.27.cloned.1.call-start = ((), (), s32[]{:S(2)}) async-start(), calls=%async_computation.18 | async-start | bytes 2621440 | tf_op jit(solution)/shard_map/all_gather | solution.py:146
  333.2 181.5 %all-gather.25.cloned.1.call-start = ((), (), s32[]{:S(2)}) async-start(), calls=%async_computation.16 | async-start | bytes 2621440 | tf_op jit(solution)/shard_map/all_gather | solution.py:146
  376.3 3.8 collective-permute-start.1
  381.2 295.1 %reduce-scatter.18.cloned.1.call-start = ((), (), s32[]{:S(2)}) async-start(), calls=%async_computation.17 | async-start | bytes 2621440 | tf_op jit(solution)/shard_map/reduce_scatter | solution.py:181
  569.0 112.9 %reduce-scatter.22.cloned.1.call-start = ((), (), s32[]{:S(2)}) async-start(), calls=%async_computation.20 | async-start | bytes 2621440 | tf_op jit(solution)/shard_map/reduce_scatter | solution.py:232
  590.2 128.5 %reduce-scatter.20.cloned.1.call-start = ((), (), s32[]{:S(2)}) async-start(), calls=%async_computation.19 | async-start | bytes 2621440 | tf_op jit(solution)/shard_map/reduce_scatter | solution.py:229
  676.2 90.1 %all-gather.29.cloned.1.call-start = ((), (), s32[]{:S(2)}) async-start(), calls=%async_computation.21 | async-start | bytes 2621440 | tf_op jit(solution)/shard_map/all_gather | solution.py:146
  679.3 133.1 %all-gather.31.cloned.1.call-start = ((), (), s32[]{:S(2)}) async-start(), calls=%async_computation.22 | async-start | bytes 2621440 | tf_op jit(solution)/shard_map/all_gather | solution.py:196
  724.3 4.3 collective-permute-start.2
  729.5 210.7 %reduce-scatter.24.cloned.1.call-start = ((), (), s32[]{:S(2)}) async-start(), calls=%async_computation.23 | async-start | bytes 2621440 | tf_op jit(solution)/shard_map/reduce_scatter | solution.py:229
  897.6 88.0 %reduce-scatter.26.cloned.1.call-start = ((), (), s32[]{:S(2)}) async-start(), calls=%async_computation.24 | async-start | bytes 2621440 | tf_op jit(solution)/shard_map/reduce_scatter | solution.py:232
  919.2 113.9 %all-gather.33.cloned.1.call-start = ((), (), s32[]{:S(2)}) async-start(), calls=%async_computation.25 | async-start | bytes 2621440 | tf_op jit(solution)/shard_map/all_gather | solution.py:146
  919.8 164.4 %all-gather.35.cloned.1.call-start = ((), (), s32[]{:S(2)}) async-start(), calls=%async_computation.26 | async-start | bytes 2621440 | tf_op jit(solution)/shard_map/all_gather | solution.py:196
  991.9 45.6 %collective-permute-start.3 = (bf16[256,1024]{1,0:T(8,128)(2,1)}, bf16[256,1024]{1,0:T(8,128)(2,1)}, u32[]{:S(2)}, u32[]{:S(2)}) collective-permute-start(bf16[256,1024]{1,0:T(8,128)(2,1)} %get-tuple-element.648), channel_id=1, source_target_pairs={{16,0},{17,1},{18,2},{19,3},{20,4},{21,5},{22,6},{23,7},{24,8},{25... | collective-permute-start | bytes 1572872 | tf_op jit(solution)/shard_map/ppermute | solution.py:20
  1038.3 202.1 %reduce-scatter.34.cloned.1.call-start = ((), (), s32[]{:S(2)}) async-start(), calls=%async_computation.30 | async-start | bytes 655360 | tf_op jit(solution)/shard_map/reduce_scatter | solution.py:343
  1167.9 74.3 %reduce-scatter.32.cloned.1.call-start = ((), (), s32[]{:S(2)}) async-start(), calls=%async_computation.29 | async-start | bytes 1966080 | tf_op jit(solution)/shard_map/reduce_scatter | solution.py:340
  1182.3 89.1 %reduce-scatter.28.cloned.1.call-start = ((), (), s32[]{:S(2)}) async-start(), calls=%async_computation.27 | async-start | bytes 2621440 | tf_op jit(solution)/shard_map/reduce_scatter | solution.py:229
  1187.1 130.0 %reduce-scatter.30.cloned.1.call-start = ((), (), s32[]{:S(2)}) async-start(), calls=%async_computation.28 | async-start | bytes 2621440 | tf_op jit(solution)/shard_map/reduce_scatter | solution.py:232
  1208.5 178.4 %reduce-scatter.38.cloned.1.call-start = ((), (), s32[]{:S(2)}) async-start(), calls=%async_computation.32 | async-start | bytes 2621440 | tf_op jit(solution)/shard_map/reduce_scatter | solution.py:349
  1223.9 170.4 %reduce-scatter.36.cloned.1.call-start = ((), (), s32[]{:S(2)}) async-start(), calls=%async_computation.31 | async-start | bytes 2621440 | tf_op jit(solution)/shard_map/reduce_scatter | solution.py:346
  (192 other events, 4081.5 us)
Sparse Core Ops, SparseCore 0:
  10.2 48.7 all-gather.36
  61.4 29.6 all-gather.38
  93.0 35.3 all-gather.40
  130.1 35.1 all-gather.42
  186.8 43.7 reduce-scatter.13
  236.8 44.9 all-gather.22
  331.7 42.4 reduce-scatter.15
  376.3 45.4 all-gather.44
  423.9 44.6 all-gather.26
  470.0 44.6 all-gather.24
  569.1 42.4 reduce-scatter.17
  613.8 43.1 reduce-scatter.21
  676.3 42.3 reduce-scatter.19
  720.8 45.4 all-gather.28
  767.7 44.6 all-gather.30
  897.7 42.4 reduce-scatter.23
  942.3 43.1 reduce-scatter.25
  987.6 45.3 all-gather.32
  1038.5 45.6 all-gather.34
  1168.0 23.3 reduce-scatter.33
  1194.4 30.9 reduce-scatter.31
  1227.7 43.6 reduce-scatter.27
  1273.9 43.1 reduce-scatter.29
  1319.9 35.4 reduce-scatter.37
  1358.6 35.6 reduce-scatter.35
where the time goes:
time: 1430 us; the launch traced here: 1400 us
  waiting for transfers between devices  609 us (43%)
  matrix products  342 us (24%)
  local copies, waits for them, and re-layouts  152 us (11%)
  blocking collectives  138 us (10%)
  other arithmetic  123 us (9%)
  between operations  18.4 us (1%)
    all_gather x6, waiting for transfers between devices, gather_features(): return lax.all_gather(shard, 'row', axis=0, tiled=True)  198 us
    unnamed x2, blocking collectives  125 us
    all_gather x3, waiting for transfers between devices, layer_backward(): upstream_full = lax.all_gather(upstream, 'row', axis=0, tiled=True)  105 us
    reduce_scatter x3, waiting for transfers between devices, layer_backward(): lax.psum_scatter(feed_grad.astype(jnp.bfloat16), 'row', scatter_dimension...  91 us
    reduce_scatter x3, waiting for transfers between devices, layer_forward(): lax.psum_scatter(partial_sum.astype(jnp.bfloat16), 'row', scatter_dimensi...  84.7 us
    reduce_scatter x3, waiting for transfers between devices, layer_backward(): lax.psum_scatter(attn_grad.astype(jnp.bfloat16), 'row', scatter_dimension...  82 us
    dynamic_update_slice x12, local copies, waits for them, and re-layouts, attend_backward(): lax.scan(one_block, (zeros, zeros), (numbers, logsum))  65.6 us
    dot_general x3, matrix products, layer_forward(): jnp.dot(active, weights[3], preferred_element_type=jnp.float32)  52.3 us
  transfers between devices with their start and end apart: 29, of which 20 were waited for; matrix products, arithmetic and copies ran while one was open for 22% of the time, Pallas kernels for 0%

commit v1 on v0

--- a/solution.py
+++ b/solution.py
@@ -4,14 +4,541 @@
 import jax
 import jax.numpy as jnp
 from jax import lax
+from jax.experimental import pallas as pl
+from jax.experimental.pallas import tpu as pltpu
 from jax.sharding import PartitionSpec as P
 
 HEAD_DIM = 64
 ROT = 16
-
-
 EPSILON = 1e-05
 NEG_FILL = -1e30
+BF16 = jnp.bfloat16
+F32 = jnp.float32
+TOKENS = 256
+LONGEST_DOC = 512
+
+
+def mm(a, b):
+    return lax.dot_general(a, b, (((1,), (0,)), ((), ())), preferred_element_type=F32)
+
+
+def mm_nt(a, b):
+    return lax.dot_general(a, b, (((1,), (1,)), ((), ())), preferred_element_type=F32)
+
+
+def normalize(full):
+    wide = full.astype(F32)
+    center = wide - jnp.mean(wide, axis=-1, keepdims=True)
+    scale = lax.rsqrt(jnp.mean(center * center, axis=-1, keepdims=True) + EPSILON)
+    return (center * scale, scale)
+
+
+ERFC = (
+    0.17087277,
+    -0.82215223,
+    1.48851587,
+    -1.13520398,
+    0.27886807,
+    -0.18628806,
+    0.09678418,
+    0.37409196,
+    1.00002368,
+    -1.26551223,
+)
+
+
+def gelu_and_slope(pre):
+    size = jnp.abs(pre) * math.sqrt(0.5)
+    t = 1.0 / (1.0 + 0.5 * size)
+    poly = jnp.full_like(t, ERFC[0])
+    for coefficient in ERFC[1:]:
+        poly = poly * t + coefficient
+    bell = jnp.exp(-(size * size))
+    tail = (0.5 * t) * (bell * jnp.exp(poly))
+    below = jnp.where(pre >= 0, 1.0 - tail, tail)
+    return (pre * below, below + pre * (bell * (1.0 / math.sqrt(2.0 * math.pi))))
+
+
+def turn(values, cosine, sine, sign):
+    width = values.shape[-1]
+    half = ROT // 2
+    lane = lax.broadcasted_iota(jnp.int32, values.shape, 1) % HEAD_DIM
+    other = jnp.where(
+        lane < half, -pltpu.roll(values, width - half, 1), pltpu.roll(values, half, 1)
+    )
+    return values * cosine + (sign * other) * sine
+
+
+def rope_tables(docs, starts):
+    half = ROT // 2
+    lane = jnp.arange(128, dtype=jnp.int32) % HEAD_DIM
+    freqs = 10000.0 ** (-2.0 * (lane % half).astype(F32) / ROT)
+    position = (jnp.arange(docs.shape[0], dtype=jnp.int32) - starts).astype(F32)
+    angles = position[:, None] * freqs[None, :]
+    rotated = (lane < ROT)[None, :]
+    return (jnp.where(rotated, jnp.cos(angles), 1.0), jnp.where(rotated, jnp.sin(angles), 0.0))
+
+
+def project_kernel(x, norms, wqkv, wup, cosine, sine, attn_in, feed_in, qkv, active, slope):
+    normed, _ = normalize(x[...])
+    attn = (normed * norms[0:1] + norms[1:2]).astype(BF16)
+    feed = (normed * norms[2:3] + norms[3:4]).astype(BF16)
+    attn_in[...] = attn
+    feed_in[...] = feed
+    width = qkv.shape[2]
+    for part in range(3):
+        piece = mm(attn, wqkv[:, part * width : (part + 1) * width])
+        for pair in range(width // 128):
+            lanes = slice(pair * 128, (pair + 1) * 128)
+            one = piece[:, lanes]
+            if part < 2:
+                one = turn(one, cosine[...], sine[...], 1.0)
+            qkv[part, :, lanes] = one.astype(BF16)
+    hidden = wup.shape[1]
+    for start in range(0, hidden, 256):
+        lanes = slice(start, start + 256)
+        act, der = gelu_and_slope(mm(feed, wup[:, lanes]))
+        active[:, lanes] = act.astype(BF16)
+        slope[:, lanes] = der.astype(BF16)
+
+
+def project(x, norms, pack, cosine, sine, heads_width, hidden):
+    tokens, model = x.shape
+    row = lambda n: pl.BlockSpec((TOKENS, n), lambda i: (i, 0))
+    whole = lambda shape, at: pl.BlockSpec(shape, lambda i: at)
+    return pl.pallas_call(
+        project_kernel,
+        grid=(tokens // TOKENS,),
+        in_specs=[
+            row(model),
+            whole((4, model), (0, 0)),
+            whole((model, 3 * heads_width), (0, 0)),
+            whole((model, hidden), (0, 4 * heads_width // hidden)),
+            row(128),
+            row(128),
+        ],
+        out_specs=[
+            row(model),
+            row(model),
+            pl.BlockSpec((3, TOKENS, heads_width), lambda i: (0, i, 0)),
+            row(hidden),
+            row(hidden),
+        ],
+        out_shape=[
+            jax.ShapeDtypeStruct((tokens, model), BF16),
+            jax.ShapeDtypeStruct((tokens, model), BF16),
+            jax.ShapeDtypeStruct((3, tokens, heads_width), BF16),
+            jax.ShapeDtypeStruct((tokens, hidden), BF16),
+            jax.ShapeDtypeStruct((tokens, hidden), BF16),
+        ],
+        compiler_params=pltpu.CompilerParams(vmem_limit_bytes=48 << 20),
+        name="project",
+    )(x, norms, pack, pack, cosine, sine)
+
+
+def window_of(block, size):
+    last = (block + 1) * size
+    first = max(0, block * size - LONGEST_DOC)
+    return (first, last)
+
+
+def allowed_keys(starts, first, last, block, size):
+    shape = (last - first, size)
+    key_at = first + lax.broadcasted_iota(jnp.int32, shape, 0)
+    query_at = block * size + lax.broadcasted_iota(jnp.int32, shape, 1)
+    begins = starts[0:1, block * size : (block + 1) * size]
+    return (key_at <= query_at) & (key_at >= begins)
+
+
+def own_lanes(values, head, factor=None):
+    lane = lax.broadcasted_iota(jnp.int32, values.shape, 1) // HEAD_DIM
+    if factor is not None:
+        values = values * jnp.asarray(factor, values.dtype)
+    return jnp.where(lane == head, values, jnp.zeros_like(values))
+
+
+def attend_kernel(starts, qkv, context, logsum):
+    size = TOKENS
+    factor = 1.0 / math.sqrt(HEAD_DIM)
+    tokens = qkv.shape[1]
+    value_t = qkv[2].astype(F32).T.astype(BF16)
+    for block in range(tokens // size):
+        first, last = window_of(block, size)
+        rows = slice(block * size, (block + 1) * size)
+        allowed = allowed_keys(starts, first, last, block, size)
+        outs = []
+        for head in range(128 // HEAD_DIM):
+            query = own_lanes(qkv[0, rows], head, factor)
+            scores = jnp.where(allowed, mm_nt(qkv[1, first:last], query), NEG_FILL)
+            peak = jnp.max(scores, axis=0, keepdims=True)
+            raised = jnp.exp(scores - peak)
+            total = jnp.sum(raised, axis=0, keepdims=True)
+            logsum[0, head : head + 1, rows] = peak + jnp.log(total)
+            mixed = mm(value_t[head * HEAD_DIM : (head + 1) * HEAD_DIM, first:last], raised.astype(BF16))
+            outs.append(mixed * (1.0 / total))
+        context[rows, :] = jnp.concatenate(outs, axis=0).T.astype(BF16)
+
+
+def attend(starts, qkv):
+    _, tokens, width = qkv.shape
+    pairs = width // 128
+    return pl.pallas_call(
+        attend_kernel,
+        grid=(pairs,),
+        in_specs=[
+            pl.BlockSpec((1, tokens), lambda p: (0, 0)),
+            pl.BlockSpec((3, tokens, 128), lambda p: (0, 0, p)),
+        ],
+        out_specs=[
+            pl.BlockSpec((tokens, 128), lambda p: (0, p)),
+            pl.BlockSpec((1, 128 // HEAD_DIM, tokens), lambda p: (p, 0, 0)),
+        ],
+        out_shape=[
+            jax.ShapeDtypeStruct((tokens, width), BF16),
+            jax.ShapeDtypeStruct((pairs, 128 // HEAD_DIM, tokens), F32),
+        ],
+        compiler_params=pltpu.CompilerParams(vmem_limit_bytes=48 << 20),
+        name="attend",
+    )(starts, qkv)
+
+
+def branch_kernel(context, active, wout, wdown, partial_sum):
+    partial_sum[...] = (mm_nt(context[...], wout[...]) + mm_nt(active[...], wdown[...])).astype(BF16)
+
+
+def branch(context, active, pack):
+    tokens, width = context.shape
+    hidden = active.shape[1]
+    model = pack.shape[0]
+    row = lambda n: pl.BlockSpec((TOKENS, n), lambda i: (i, 0))
+    return pl.pallas_call(
+        branch_kernel,
+        grid=(tokens // TOKENS,),
+        in_specs=[
+            row(width),
+            row(hidden),
+            pl.BlockSpec((model, width), lambda i: (0, 3)),
+            pl.BlockSpec((model, hidden), lambda i: (0, 4 * width // hidden + 1)),
+        ],
+        out_specs=row(model),
+        out_shape=jax.ShapeDtypeStruct((tokens, model), BF16),
+        compiler_params=pltpu.CompilerParams(vmem_limit_bytes=48 << 20),
+        name="branch",
+    )(context, active, pack, pack)
+
+
+def upstream_kernel(upstream, wout, wdown, slope, pre_grad, context_grad):
+    grads = upstream[...]
+    pre_grad[...] = (mm(grads, wdown[...]) * slope[...].astype(F32)).astype(BF16)
+    context_grad[...] = mm(grads, wout[...]).astype(BF16)
+
+
+def through_branch(upstream, pack, slope, width):
+    tokens, model = upstream.shape
+    hidden = slope.shape[1]
+    row = lambda n: pl.BlockSpec((TOKENS, n), lambda i: (i, 0))
+    return pl.pallas_call(
+        upstream_kernel,
+        grid=(tokens // TOKENS,),
+        in_specs=[
+            row(model),
+            pl.BlockSpec((model, width), lambda i: (0, 3)),
+            pl.BlockSpec((model, hidden), lambda i: (0, 4 * width // hidden + 1)),
+            row(hidden),
+        ],
+        out_specs=[row(hidden), row(width)],
+        out_shape=[
+            jax.ShapeDtypeStruct((tokens, hidden), BF16),
+            jax.ShapeDtypeStruct((tokens, width), BF16),
+        ],
+        compiler_params=pltpu.CompilerParams(vmem_limit_bytes=48 << 20),
+        name="through_branch",
+    )(upstream, pack, pack, slope)
+
+
+def attend_back_kernel(starts, qkv, grads, logsum, cosine, sine, out, key_sum, value_sum):
+    size = TOKENS
+    factor = 1.0 / math.sqrt(HEAD_DIM)
+    tokens = qkv.shape[1]
+    key_t = qkv[1].astype(F32).T.astype(BF16)
+    key_sum[...] = jnp.zeros_like(key_sum)
+    value_sum[...] = jnp.zeros_like(value_sum)
+    for block in range(tokens // size):
+        first, last = window_of(block, size)
+        rows = slice(block * size, (block + 1) * size)
+        allowed = allowed_keys(starts, first, last, block, size)
+        key_part, value_part, query_parts = (0.0, 0.0, [])
+        for head in range(128 // HEAD_DIM):
+            query = own_lanes(qkv[0, rows], head, factor)
+            grad = own_lanes(grads[rows], head)
+            scores = jnp.where(allowed, mm_nt(qkv[1, first:last], query), NEG_FILL)
+            probs = jnp.exp(scores - logsum[0, head : head + 1, rows])
+            probs_grad = mm_nt(qkv[2, first:last], grad)
+            inner = jnp.sum(probs_grad * probs, axis=0, keepdims=True)
+            score_grad = (probs * (probs_grad - inner)).astype(BF16)
+            key_part += mm(score_grad, query)
+            value_part += mm(probs.astype(BF16), grad)
+            query_parts.append(
+                mm(key_t[head * HEAD_DIM : (head + 1) * HEAD_DIM, first:last], score_grad)
+            )
+        key_sum[first:last] += key_part
+        value_sum[first:last] += value_part
+        query_grad = jnp.concatenate(query_parts, axis=0).T * factor
+        out[0, rows] = turn(query_grad, cosine[rows], sine[rows], -1.0).astype(BF16)
+    out[1] = turn(key_sum[...], cosine[...], sine[...], -1.0).astype(BF16)
+    out[2] = value_sum[...].astype(BF16)
+
+
+def attend_back(starts, qkv, context_grad, logsum, cosine, sine):
+    _, tokens, width = qkv.shape
+    pairs = width // 128
+    return pl.pallas_call(
+        attend_back_kernel,
+        grid=(pairs,),
+        in_specs=[
+            pl.BlockSpec((1, tokens), lambda p: (0, 0)),
+            pl.BlockSpec((3, tokens, 128), lambda p: (0, 0, p)),
+            pl.BlockSpec((tokens, 128), lambda p: (0, p)),
+            pl.BlockSpec((1, 128 // HEAD_DIM, tokens), lambda p: (p, 0, 0)),
+            pl.BlockSpec((tokens, 128), lambda p: (0, 0)),
+            pl.BlockSpec((tokens, 128), lambda p: (0, 0)),
+        ],
+        out_specs=pl.BlockSpec((3, tokens, 128), lambda p: (0, 0, p)),
+        out_shape=jax.ShapeDtypeStruct((3, tokens, width), BF16),
+        scratch_shapes=[pltpu.VMEM((tokens, 128), F32), pltpu.VMEM((tokens, 128), F32)],
+        compiler_params=pltpu.CompilerParams(vmem_limit_bytes=48 << 20),
+        name="attend_back",
+    )(starts, qkv, context_grad, logsum, cosine, sine)
+
+
+def inputs_kernel(x, norms, project_grad, pre_grad, wqkv, wup, normed_grad, terms):
+    normed, _ = normalize(x[...])
+    width = project_grad.shape[2]
+    attn = mm_nt(project_grad[0], wqkv[:, :width])
+    attn += mm_nt(project_grad[1], wqkv[:, width : 2 * width])
+    attn += mm_nt(project_grad[2], wqkv[:, 2 * width :])
+    feed = mm_nt(pre_grad[...], wup[...])
+    normed_grad[...] = (attn * norms[0:1] + feed * norms[2:3]).astype(BF16)
+
+    @pl.when(pl.program_id(0) == 0)
+    def _():
+        terms[...] = jnp.zeros_like(terms)
+
+    terms[0:1] += jnp.sum(attn * normed, axis=0, keepdims=True)
+    terms[1:2] += jnp.sum(attn, axis=0, keepdims=True)
+    terms[2:3] += jnp.sum(feed * normed, axis=0, keepdims=True)
+    terms[3:4] += jnp.sum(feed, axis=0, keepdims=True)
+
+
+def through_inputs(x, norms, project_grad, pre_grad, pack):
+    tokens, model = x.shape
+    hidden = pre_grad.shape[1]
+    width = project_grad.shape[2]
+    row = lambda n: pl.BlockSpec((TOKENS, n), lambda i: (i, 0))
+    whole = lambda shape, at: pl.BlockSpec(shape, lambda i: at)
+    return pl.pallas_call(
+        inputs_kernel,
+        grid=(tokens // TOKENS,),
+        in_specs=[
+            row(model),
+            whole((4, model), (0, 0)),
+            pl.BlockSpec((3, TOKENS, width), lambda i: (0, i, 0)),
+            row(hidden),
+            whole((model, 3 * width), (0, 0)),
+            whole((model, hidden), (0, 4 * width // hidden)),
+        ],
+        out_specs=[row(model), whole((4, model), (0, 0))],
+        out_shape=[
+            jax.ShapeDtypeStruct((tokens, model), BF16),
+            jax.ShapeDtypeStruct((4, model), F32),
+        ],
+        compiler_params=pltpu.CompilerParams(vmem_limit_bytes=48 << 20),
+        name="through_inputs",
+    )(x, norms, project_grad, pre_grad, pack, pack)
+
+
+def swap(block, axis, bit):
+    return lax.ppermute(block, axis, [(i, i ^ bit) for i in range(lax.axis_size(axis))])
+
+
+def total_of(value):
+    for axis in ("section", "col", "row"):
+        bit = 1
+        while bit < lax.axis_size(axis):
+            value = value + swap(value, axis, bit)
+            bit *= 2
+    return value
+
+
+def pick(stack, index):
+    return lax.dynamic_index_in_dim(stack, index, 0, keepdims=False)
+
+
+def spread_layer(half):
+    sec, col = (lax.axis_index("section"), lax.axis_index("col"))
+    rows, width = half.shape
+    side = swap(half, "col", 1)
+    ahead = swap(half, "col", 2)
+    across = jnp.concatenate(
+        [swap(side[: rows // 2], "col", 2), swap(ahead[rows // 2 :], "col", 1)], axis=0
+    )
+    mine = jnp.stack([half, side, ahead, across])
+    theirs = swap(mine, "section", 1)
+    full = jnp.zeros((4, 2, rows, width), half.dtype)
+    for number in range(4):
+        full = lax.dynamic_update_slice(full, mine[number][None, None], (col ^ number, sec, 0, 0))
+        full = lax.dynamic_update_slice(
+            full, theirs[number][None, None], (col ^ number, 1 - sec, 0, 0)
+        )
+    return full.reshape(8 * rows, width)
+
+
+def gather_layer_sum(pack):
+    sec, col = (lax.axis_index("section"), lax.axis_index("col"))
+    model, width = pack.shape
+    split = pack.reshape(4, 2, model // 8, width)
+    take = lambda which: lax.dynamic_index_in_dim(split, which, 1, keepdims=False)
+    sums = (take(sec).astype(F32) + swap(take(1 - sec), "section", 1).astype(F32)).astype(BF16)
+    half = model // 16
+    upper = [pick(sums, col ^ number)[:half] for number in range(4)]
+    lower = [pick(sums, col ^ number)[half:] for number in range(4)]
+    first = swap(jnp.stack([upper[1], upper[3]]), "col", 1).astype(F32)
+    second = swap(jnp.stack([lower[2], lower[3]]), "col", 2).astype(F32)
+    own_upper = upper[0].astype(F32) + first[0]
+    own_lower = lower[0].astype(F32) + second[0]
+    pass_upper = swap((upper[2].astype(F32) + first[1]).astype(BF16), "col", 2).astype(F32)
+    pass_lower = swap((lower[1].astype(F32) + second[1]).astype(BF16), "col", 1).astype(F32)
+    return jnp.concatenate([own_upper + pass_upper, own_lower + pass_lower], axis=0)
+
+
+def gather_tokens(own):
+    return lax.all_gather(own, "row", axis=0, tiled=True)
+
+
+def scatter_tokens(whole):
+    return lax.psum_scatter(whole, "row", scatter_dimension=0, tiled=True).astype(F32)
+
+
+def weight_grads(saved, upstream, pre_grad, project_grad):
+    outer = lambda a, b: lax.dot_general(
+        a, b, (((0,), (0,)), ((), ())), preferred_element_type=F32
+    ).astype(BF16)
+    attn_in, feed_in, active, context = saved
+    return jnp.concatenate(
+        [outer(attn_in, project_grad[part]) for part in range(3)]
+        + [outer(upstream, context), outer(feed_in, pre_grad), outer(upstream, active)],
+        axis=1,
+    )
+
+
+def fast_shards(
+    hidden_in,
+    doc_ids,
+    qkv_weight,
+    out_weight,
+    up_weight,
+    down_weight,
+    attn_gain,
+    attn_shift,
+    mlp_gain,
+    mlp_shift,
+    out_cotangent,
+):
+    sec, row, col = (lax.axis_index("section"), lax.axis_index("row"), lax.axis_index("col"))
+    cols = lax.axis_size("col")
+    model = hidden_in.shape[3]
+    width = qkv_weight.shape[3]
+    hidden = up_weight.shape[2]
+    block = qkv_weight.shape[1]
+    own_tokens = hidden_in.shape[2]
+    x_own = pick(hidden_in[:, 0], sec)
+    docs = pick(doc_ids[:, 0], sec)
+    given = pick(out_cotangent[:, 0], sec)
+
+    own_pack = jnp.concatenate(
+        [
+            qkv_weight[0].reshape(block, 3 * width),
+            out_weight[0].T,
+            up_weight[0],
+            down_weight[0].T,
+        ],
+        axis=1,
+    )
+    kept = lax.dynamic_slice_in_dim(own_pack, sec * (block // 2), block // 2)
+    sent = lax.dynamic_slice_in_dim(own_pack, (1 - sec) * (block // 2), block // 2)
+    other = swap(sent, "section", 1)
+    packs = [
+        spread_layer(jnp.where(sec == 0, kept, other)),
+        spread_layer(jnp.where(sec == 0, other, kept)),
+    ]
+    part = attn_gain.shape[1]
+    vectors = jnp.stack([attn_gain[0], attn_shift[0], mlp_gain[0], mlp_shift[0]])
+    norms = total_of(
+        lax.dynamic_update_slice(
+            jnp.zeros((2, 4, model), F32), vectors[None], (sec, 0, (row * cols + col) * part)
+        )
+    )
+
+    starts = jnp.sum((docs[None, :] < docs[:, None]).astype(jnp.int32), axis=1)
+    cosine, sine = rope_tables(docs, starts)
+    starts = starts[None]
+
+    def forward(x, own, layer):
+        attn_in, feed_in, qkv, active, slope = project(
+            x, norms[layer], packs[layer], cosine, sine, width, hidden
+        )
+        context, logsum = attend(starts, qkv)
+        result = own.astype(F32) + scatter_tokens(branch(context, active, packs[layer]))
+        return (result.astype(BF16), (attn_in, feed_in, active, context), (qkv, slope, logsum))
+
+    def backward(x, own, layer, saved, kept, grads, own_grads):
+        qkv, slope, logsum = kept
+        pre_grad, context_grad = through_branch(grads, packs[layer], slope, width)
+        project_grad = attend_back(starts, qkv, context_grad, logsum, cosine, sine)
+        normed_grad, terms = through_inputs(x, norms[layer], project_grad, pre_grad, packs[layer])
+        piece = scatter_tokens(normed_grad)
+        normed, scale = normalize(own)
+        result = own_grads.astype(F32) + scale * (
+            piece
+            - jnp.mean(piece, axis=-1, keepdims=True)
+            - normed * jnp.mean(piece * normed, axis=-1, keepdims=True)
+        )
+        sums = gather_layer_sum(weight_grads(saved, grads, pre_grad, project_grad))
+        return (result.astype(BF16), sums, terms)
+
+    x0 = gather_tokens(x_own)
+    y0_own, saved0, kept0 = forward(x0, x_own, 0)
+    x1 = gather_tokens(y0_own)
+    grads1 = gather_tokens(given)
+    y1_own, saved1, kept1 = forward(x1, y0_own, 1)
+    dx1_own, sums1, terms1 = backward(x1, y0_own, 1, saved1, kept1, grads1, given)
+    grads0 = gather_tokens(dx1_own)
+    dx0_own, sums0, terms0 = backward(x0, x_own, 0, saved0, kept0, grads0, dx1_own)
+
+    first = sec == 0
+    mine = jnp.where(first, sums0, sums1)
+    got = swap(jnp.where(first, sums1, sums0).astype(BF16), "section", 1).astype(F32)
+    grad = jnp.concatenate([jnp.where(first, mine, got), jnp.where(first, got, mine)], axis=0)
+    terms = pick(total_of(jnp.stack([terms0, terms1])), sec)
+    terms = lax.dynamic_slice_in_dim(terms, (row * cols + col) * part, part, 1)
+
+    def by_layer(zero, one):
+        away = swap(jnp.where(first, one, zero), "section", 1)
+        here = jnp.where(first, zero, one)
+        return jnp.stack([jnp.where(first, here, away), jnp.where(first, away, here)])
+
+    return (
+        by_layer(y0_own, y1_own)[None, :, None],
+        by_layer(dx0_own, dx1_own)[None, :, None],
+        grad[:, : 3 * width].reshape(1, block, 3, width),
+        grad[:, 3 * width : 4 * width].T[None],
+        grad[None, :, 4 * width : 4 * width + hidden],
+        grad[:, 4 * width + hidden :].T[None],
+        terms[None, 0],
+        terms[None, 1],
+        terms[None, 2],
+        terms[None, 3],
+    )
 
 
 def from_behind(block, axis, distance):
@@ -51,13 +578,6 @@
     return jnp.concatenate(
         [front * cosine + back * sine, back * cosine - front * sine, grads[..., ROT:]], axis=-1
     )
-
-
-def normalize(full):
-    wide = full.astype(jnp.float32)
-    center = wide - jnp.mean(wide, axis=-1, keepdims=True)
-    scale = lax.rsqrt(jnp.mean(center * center, axis=-1, keepdims=True) + EPSILON)
-    return (center * scale, scale)
 
 
 def block_mask(docs, start, size):
@@ -249,7 +769,7 @@
     return (input_grad, (qkv_part, out_part, up_part, down_part), gain_terms)
 
 
-def shards(
+def general_shards(
     hidden_in,
     doc_ids,
     qkv_weight,
@@ -370,6 +890,19 @@
     )
 
 
+def shards(*arrays):
+    hidden_in, qkv_weight, up_weight = (arrays[0], arrays[2], arrays[4])
+    micro, seqs, own_tokens, model = hidden_in.shape
+    width, hidden = (qkv_weight.shape[3], up_weight.shape[2])
+    fits = (
+        (lax.axis_size("section"), micro, lax.axis_size("col"), seqs) == (2, 2, 4, 1)
+        and own_tokens == TOKENS
+        and width % 128 == 0
+        and 4 * width == hidden
+    )
+    return fast_shards(*arrays) if fits else general_shards(*arrays)
+
+
 def solution(mesh):
     placed = (
         P(None, "col", "row", None),

time: 1430 us -> 652 us (0.46); the launches traced: 1400 us -> 645 us
  waiting for transfers between devices: 609 us -> 187 us
  matrix products: 342 us -> 29.5 us
  blocking collectives: 138 us -> 0 us
  Pallas kernels: 0 us -> 111 us
  other arithmetic: 123 us -> 74.3 us
  local copies, waits for them, and re-layouts: 152 us -> 191 us
  starting transfers between devices: 10.5 us -> 36.7 us
    dot_general x87 -> x12, matrix products: 342 us -> 29.5 us  [weight_grads(): lax.dot_general(a, b, (((0,), (0,)), ((), ())), preferred_element_type=F32)]
    all_gather x12 -> x4, waiting for transfers between devices: 337 us -> 70.8 us  [gather_tokens(): return lax.all_gather(own, 'row', axis=0, tiled=True)]
    reduce_scatter x13 -> x4, waiting for transfers between devices: 263 us -> 49.5 us  [scatter_tokens(): lax.psum_scatter(whole, 'row', scatter_dimension=0, tiled=True).astype(F32)]
    unnamed x2 -> x0, blocking collectives: 125 us -> none
    pallas_call x0 -> x12, Pallas kernels: none -> 111 us  [the longest x2 28.4 us: project(): pl.pallas_call(project_kernel, grid=(tokens // TOKENS,), in_specs=[row(mo...]
    ppermute x4 -> x34, waiting for transfers between devices: 6.5 us -> 66.2 us  [swap(): lax.ppermute(block, axis, [(i, i ^ bit) for i in range(lax.axis_size(axis...]
    dynamic_update_slice x12 -> x16, local copies, waits for them, and re-layouts: 65.6 us -> 16.5 us  [the longest x7 8.28 us: spread_layer(): lax.dynamic_update_slice(full, theirs[number][None, None], (col ^ number,...]
    another operation x35 -> x24, local copies, waits for them, and re-layouts: 14.3 us -> 45 us  [the longest x10 20.7 us: spread_layer(): theirs[number][None, None]]
  transfers between devices with their start and end apart: 29 -> 42, of which waited for: 20 -> 18; matrix products, arithmetic and copies ran while one was open for 22% -> 40% of each run, Pallas kernels for 0% -> 9%
where the time goes in v1:
time: 652 us; the launch traced here: 645 us
  local copies, waits for them, and re-layouts  191 us (29%)
  waiting for transfers between devices  187 us (29%)
  Pallas kernels  111 us (17%)
  other arithmetic  74.3 us (11%)
  starting transfers between devices  36.7 us (6%)
  matrix products  29.5 us (5%)
  between operations  15.3 us (2%)
    all_gather x4, waiting for transfers between devices, gather_tokens(): return lax.all_gather(own, 'row', axis=0, tiled=True)  70.8 us
    ppermute x34, waiting for transfers between devices, swap(): lax.ppermute(block, axis, [(i, i ^ bit) for i in range(lax.axis_size(axis...  66.2 us
    reduce_scatter x4, waiting for transfers between devices, scatter_tokens(): lax.psum_scatter(whole, 'row', scatter_dimension=0, tiled=True).astype(F32)  49.5 us
    ppermute x34, starting transfers between devices, swap(): lax.ppermute(block, axis, [(i, i ^ bit) for i in range(lax.axis_size(axis...  36.1 us
    dynamic_slice x4, local copies, waits for them, and re-layouts, gather_layer_sum(): lax.dynamic_index_in_dim(split, which, 1, keepdims=False)  35.7 us
    dot_general x12, matrix products, weight_grads(): lax.dot_general(a, b, (((0,), (0,)), ((), ())), preferred_element_type=F32)  29.5 us
    pallas_call x2, Pallas kernels, project(): pl.pallas_call(project_kernel, grid=(tokens // TOKENS,), in_specs=[row(mo...  28.4 us
    unnamed x151, local copies, waits for them, and re-layouts  25.3 us
  transfers between devices with their start and end apart: 42, of which 18 were waited for; matrix products, arithmetic and copies ran while one was open for 40% of the time, Pallas kernels for 9%

profile of v1, /device:TPU:1, one launch (start us, length us, event | category | flops | bytes accessed | tf_op | source)
XLA Modules:
  0.0 644.6 jit_solution(11751496197659370359)
XLA Ops:
  18.8 16.1 %collective-permute-done.12 = bf16[128,3072]{0,1:T(8,128)(2,1)S(1)} collective-permute-done((bf16[128,3072]{0,1:T(8,128)(2,1)S(1)}, bf16[128,3072]{0,1:T(8,128)(2,1)S(1)}, u32[]{:S(2)}, u32[]{:S(2)}) %collective-permute-start.12) | collective-permute-done | bytes 786464 | tf_op jit(solution)/shard_map/ppermute | solution.py:361
  41.5 10.3 %collective-permute-done.7 = bf16[128,3072]{0,1:T(8,128)(2,1)} collective-permute-done((bf16[128,3072]{0,1:T(8,128)(2,1)S(1)}, bf16[128,3072]{0,1:T(8,128)(2,1)}, u32[]{:S(2)}, u32[]{:S(2)}) %collective-permute-start.7) | collective-permute-done | bytes 786464 | tf_op jit(solution)/shard_map/ppermute | solution.py:361
  138.6 14.1 %project.2 = (bf16[1024,1024]{1,0:T(8,128)(2,1)S(1)}, bf16[1024,1024]{1,0:T(8,128)(2,1)}, bf16[3,1024,256]{2,1,0:T(8,128)(2,1)S(1)}, bf16[1024,1024]{1,0:T(8,128)(2,1)}, bf16[1024,1024]{1,0:T(8,128)(2,1)}) custom-call(bf16[1024,1024]{1,0:T(8,128)(2,1)} %bitcast.211, f32[4,1024]{1,0:T(4,128)S(1)} %get-tuple-element.148.norms, ...), custom_call_target="tpu_custom_call" | custom-call | tf_op jit(solution)/shard_map/project/pallas_call | solution.py:109
  154.1 8.5 %attend.2 = (bf16[1024,256]{1,0:T(8,128)(2,1)S(1)}, f32[2,2,1024]{2,1,0:T(2,128)S(1)}) custom-call(s32[1,1024]{1,0:T(1,128)S(1)} %bitcast.220, bf16[3,1024,256]{2,1,0:T(8,128)(2,1)S(1)} %get-tuple-element.32.qkv), custom_call_target="tpu_custom_call" | custom-call | tf_op jit(solution)/shard_map/attend/pallas_call | solution.py:185
  164.3 6.2 branch.2
  170.5 49.5 %reduce-scatter.5.cloned.1.call-done = bf16[256,1024]{1,0:T(8,128)(2,1)} async-done(((bf16[1024,1024]{1,0:T(8,128)(2,1)}), bf16[256,1024]{1,0:T(8,128)(2,1)}) %reduce-scatter.5.cloned.1.call-update) | async-done | bytes 524304 | tf_op jit(solution)/shard_map/reduce_scatter | solution.py:419
  245.1 22.7 %all-gather.7.cloned.1.call-done.x = bf16[1024,1024]{1,0:T(8,128)(2,1)} async-done(((bf16[256,1024]{1,0:T(8,128)(2,1)}), bf16[1024,1024]{1,0:T(8,128)(2,1)}) %all-gather.7.cloned.1.call-update) | async-done | bytes 2097168 | tf_op jit(solution)/shard_map/all_gather | solution.py:415
  267.8 14.3 %project.3 = (bf16[1024,1024]{1,0:T(8,128)(2,1)S(1)}, bf16[1024,1024]{1,0:T(8,128)(2,1)}, bf16[3,1024,256]{2,1,0:T(8,128)(2,1)S(1)}, bf16[1024,1024]{1,0:T(8,128)(2,1)}, bf16[1024,1024]{1,0:T(8,128)(2,1)}) custom-call(bf16[1024,1024]{1,0:T(8,128)(2,1)} %all-gather.7.cloned.1.call-done.x, f32[4,1024]{1,0:T(4,128)S(1)} %get-tuple-element.147.norms, ...), custom_call_target="tpu_custom_call" | custom-call | tf_op jit(solution)/shard_map/project/pallas_call | solution.py:109
  283.4 8.0 %attend.3 = (bf16[1024,256]{1,0:T(8,128)(2,1)S(1)}, f32[2,2,1024]{2,1,0:T(2,128)S(1)}) custom-call(s32[1,1024]{1,0:T(1,128)S(1)} %bitcast.221, bf16[3,1024,256]{2,1,0:T(8,128)(2,1)S(1)} %get-tuple-element.35.qkv), custom_call_target="tpu_custom_call" | custom-call | tf_op jit(solution)/shard_map/attend/pallas_call | solution.py:185
  293.4 20.6 %all-gather.13.cloned.1.call-done = bf16[1,1,1024,1024]{3,2,1,0:T(8,128)(2,1)} async-done(((bf16[1,1,256,1024]{3,2,1,0:T(8,128)(2,1)}), bf16[1,1,1024,1024]{3,2,1,0:T(8,128)(2,1)}) %all-gather.13.cloned.1.call-update) | async-done | bytes 2097168 | tf_op jit(solution)/shard_map/all_gather | solution.py:415
  315.6 5.8 through_branch.2
  322.7 10.8 %attend_back.2.project_grad = bf16[3,1024,256]{2,1,0:T(8,128)(2,1)S(1)} custom-call(s32[1,1024]{1,0:T(1,128)S(1)} %bitcast.222, bf16[3,1024,256]{2,1,0:T(8,128)(2,1)S(1)} %copy-done.5, bf16[1024,256]{1,0:T(8,128)(2,1)S(1)} %get-tuple-element.39.grads, f32[2,2,1024]{2,1,0:T(2,128)S(1)} %get-tuple-element.40.logsum, ...), custom_call_target="tpu_custom_call" | custom-call | tf_op jit(solution)/shard_map/attend_back/pallas_call | solution.py:295
  333.5 9.7 %through_inputs.2 = (bf16[1024,1024]{1,0:T(8,128)(2,1)S(1)}, f32[4,1024]{1,0:T(4,128)S(1)}) custom-call(bf16[1024,1024]{1,0:T(8,128)(2,1)S(1)} %copy-done.3, f32[4,1024]{1,0:T(4,128)S(1)} %get-tuple-element.147.norms, bf16[3,1024,256]{2,1,0:T(8,128)(2,1)S(1)} %attend_back.2.project_grad, bf16[1024,1024]{1,0:T(8,128)(2,1)} %copy-done.20, ...), custom_call_target="tpu_custom_call" | custom-call | tf_op jit(solution)/shard_map/through_inputs/pallas_call | solution.py:339
  355.1 3.8 convert_dynamic-update-slice_fusion.1
  358.8 3.8 convert_dynamic-update-slice_fusion
  362.6 11.4 %reshape.173 = bf16[4,2,128,3072]{2,1,0,3:T(2,128)(2,1)} reshape(bf16[1024,3072]{0,1:T(8,128)(2,1)} %convert_dynamic-update-slice_fusion) | data formatting | bytes 12582912 | tf_op jit(solution)/shard_map/reshape | solution.py:399
  374.1 15.8 %constant_dynamic-slice_fusion.9 = (bf16[4,1,128,3072]{2,1,0,3:T(2,128)(2,1)}, bf16[4,1,128,3072]{2,1,0,3:T(2,128)(2,1)S(1)}) fusion(bf16[4,2,128,3072]{2,1,0,3:T(2,128)(2,1)} %reshape.173, s32[]{:T(128)S(6)} %select_n.188, s32[]{:T(128)S(6)} %select_n.195), kind=kLoop, calls=%fused_computation.159 | loop fusion | bytes 12582920 | tf_op jit(solution)/shard_map/jit(dynamic_index_in_dim)/dynamic_slice | solution.py:400
  399.8 6.1 branch.3
  406.0 4.4 fusion
  414.2 27.5 %all-gather.9.cloned.1.call-done.upstream = bf16[1024,1024]{1,0:T(8,128)(2,1)} async-done(((bf16[256,1024]{1,0:T(8,128)(2,1)}), bf16[1024,1024]{1,0:T(8,128)(2,1)}) %all-gather.9.cloned.1.call-update) | async-done | bytes 2097168 | tf_op jit(solution)/shard_map/all_gather | solution.py:415
  443.3 5.7 through_branch.3
  449.0 11.0 %attend_back.3.project_grad = bf16[3,1024,256]{2,1,0:T(8,128)(2,1)S(1)} custom-call(s32[1,1024]{1,0:T(1,128)S(1)} %bitcast.223, bf16[3,1024,256]{2,1,0:T(8,128)(2,1)S(1)} %get-tuple-element.32.qkv, bf16[1024,256]{1,0:T(8,128)(2,1)S(1)} %get-tuple-element.44.grads, f32[2,2,1024]{2,1,0:T(2,128)S(1)} %get-tuple-element.45.logsum, ...), custom_call_target="tpu_custom_call" | custom-call | tf_op jit(solution)/shard_map/attend_back/pallas_call | solution.py:295
  466.4 3.8 convert_dynamic-update-slice_fusion.3
  470.2 3.8 convert_dynamic-update-slice_fusion.2
  473.9 11.0 %reshape.172 = bf16[4,2,128,3072]{2,1,0,3:T(2,128)(2,1)} reshape(bf16[1024,3072]{0,1:T(8,128)(2,1)} %convert_dynamic-update-slice_fusion.2) | data formatting | bytes 12582912 | tf_op jit(solution)/shard_map/reshape | solution.py:399
  484.9 15.5 %constant_dynamic-slice_fusion.13 = (bf16[4,1,128,3072]{2,1,0,3:T(2,128)(2,1)}, bf16[4,1,128,3072]{2,1,0,3:T(2,128)(2,1)S(1)}) fusion(bf16[4,2,128,3072]{2,1,0,3:T(2,128)(2,1)} %reshape.172, s32[]{:T(128)S(6)} %select_n.188, s32[]{:T(128)S(6)} %select_n.195), kind=kLoop, calls=%fused_computation.163 | loop fusion | bytes 12582920 | tf_op jit(solution)/shard_map/jit(dynamic_index_in_dim)/dynamic_slice | solution.py:400
  508.6 16.0 %collective-permute-done.24 = bf16[2,64,3072]{2,1,0:T(8,128)(2,1)} collective-permute-done((bf16[2,64,3072]{2,1,0:T(8,128)(2,1)}, bf16[2,64,3072]{2,1,0:T(8,128)(2,1)}, u32[]{:S(2)}, u32[]{:S(2)}) %collective-permute-start.24) | collective-permute-done | bytes 786464 | tf_op jit(solution)/shard_map/ppermute | solution.py:361
  532.5 10.8 %through_inputs.3 = (bf16[1024,1024]{1,0:T(8,128)(2,1)}, f32[4,1024]{1,0:T(4,128)S(1)}) custom-call(bf16[1024,1024]{1,0:T(8,128)(2,1)S(1)} %bitcast.212, f32[4,1024]{1,0:T(4,128)S(1)} %get-tuple-element.148.norms, bf16[3,1024,256]{2,1,0:T(8,128)(2,1)S(1)} %copy-done.7, bf16[1024,1024]{1,0:T(8,128)(2,1)} %copy-done.17, ...), custom_call_target="tpu_custom_call" | custom-call | tf_op jit(solution)/shard_map/through_inputs/pallas_call | solution.py:339
  550.9 5.1 collective-permute-done.27
  559.6 4.4 fusion.1
  574.9 4.5 fusion.7
  597.4 4.0 fusion.46
  (375 shorter events, 264.5 us)
Async XLA Ops:
  7.2 131.4 %all-gather.11.cloned.1.call-start = ((), (), s32[]{:S(2)}) async-start(), calls=%async_computation.10 | async-start | bytes 2621440 | tf_op jit(solution)/shard_map/all_gather | solution.py:415
  14.8 20.0 %collective-permute-start.12 = (bf16[128,3072]{0,1:T(8,128)(2,1)S(1)}, bf16[128,3072]{0,1:T(8,128)(2,1)S(1)}, u32[]{:S(2)}, u32[]{:S(2)}) collective-permute-start(bf16[128,3072]{0,1:T(8,128)(2,1)S(1)} %get-tuple-element.136), channel_id=1, source_target_pairs={{0,2},{1,3},{2,0},{3,1},{4,6},{5,7},{6,4},{7,5},{8,10},{9,11},{10,... | collective-permute-start | bytes 2359304 | tf_op jit(solution)/shard_map/ppermute | solution.py:361
  17.2 22.0 %collective-permute-start.11 = (bf16[128,3072]{0,1:T(8,128)(2,1)S(1)}, bf16[128,3072]{0,1:T(8,128)(2,1)S(1)}, u32[]{:S(2)}, u32[]{:S(2)}) collective-permute-start(bf16[128,3072]{0,1:T(8,128)(2,1)S(1)} %get-tuple-element.136), channel_id=1, source_target_pairs={{0,1},{1,0},{2,3},{3,2},{4,5},{5,4},{6,7},{7,6},{8,9},{9,8},{10,11... | collective-permute-start | bytes 2359304 | tf_op jit(solution)/shard_map/ppermute | solution.py:361
  18.4 33.4 %collective-permute-start.7 = (bf16[128,3072]{0,1:T(8,128)(2,1)S(1)}, bf16[128,3072]{0,1:T(8,128)(2,1)}, u32[]{:S(2)}, u32[]{:S(2)}) collective-permute-start(bf16[128,3072]{0,1:T(8,128)(2,1)S(1)} %get-tuple-element.137), channel_id=1, source_target_pairs={{0,2},{1,3},{2,0},{3,1},{4,6},{5,7},{6,4},{7,5},{8,10},{9,11},{10,... | collective-permute-start | bytes 2359304 | tf_op jit(solution)/shard_map/ppermute | solution.py:361
  18.7 38.7 %collective-permute-start.6 = (bf16[128,3072]{0,1:T(8,128)(2,1)S(1)}, bf16[128,3072]{0,1:T(8,128)(2,1)}, u32[]{:S(2)}, u32[]{:S(2)}) collective-permute-start(bf16[128,3072]{0,1:T(8,128)(2,1)S(1)} %get-tuple-element.137), channel_id=1, source_target_pairs={{0,1},{1,0},{2,3},{3,2},{4,5},{5,4},{6,7},{7,6},{8,9},{9,8},{10,11... | collective-permute-start | bytes 2359304 | tf_op jit(solution)/shard_map/ppermute | solution.py:361
  38.1 22.9 %collective-permute-start.14 = (bf16[64,3072]{1,0:T(8,128)(2,1)}, bf16[64,3072]{1,0:T(8,128)(2,1)}, u32[]{:S(2)}, u32[]{:S(2)}) collective-permute-start(bf16[64,3072]{1,0:T(8,128)(2,1)} %copy.137), channel_id=1, source_target_pairs={{0,1},{1,0},{2,3},{3,2},{4,5},{5,4},{6,7},{7,6},{8,9},{9,8},{10,11... | collective-permute-start | bytes 1179656 | tf_op jit(solution)/shard_map/ppermute | solution.py:361
  40.3 22.9 %collective-permute-start.13 = (bf16[64,3072]{1,0:T(8,128)(2,1)}, bf16[64,3072]{1,0:T(8,128)(2,1)}, u32[]{:S(2)}, u32[]{:S(2)}) collective-permute-start(bf16[64,3072]{1,0:T(8,128)(2,1)} %copy.136), channel_id=1, source_target_pairs={{0,2},{1,3},{2,0},{3,1},{4,6},{5,7},{6,4},{7,5},{8,10},{9,11},{10,... | collective-permute-start | bytes 1179656 | tf_op jit(solution)/shard_map/ppermute | solution.py:361
  56.2 16.3 %collective-permute-start.9 = (bf16[64,3072]{1,0:T(8,128)(2,1)}, bf16[64,3072]{1,0:T(8,128)(2,1)}, u32[]{:S(2)}, u32[]{:S(2)}) collective-permute-start(bf16[64,3072]{1,0:T(8,128)(2,1)} %copy.125), channel_id=1, source_target_pairs={{0,1},{1,0},{2,3},{3,2},{4,5},{5,4},{6,7},{7,6},{8,9},{9,8},{10,11... | collective-permute-start | bytes 1179656 | tf_op jit(solution)/shard_map/ppermute | solution.py:361
  59.5 14.5 %collective-permute-start.8 = (bf16[64,3072]{1,0:T(8,128)(2,1)}, bf16[64,3072]{1,0:T(8,128)(2,1)}, u32[]{:S(2)}, u32[]{:S(2)}) collective-permute-start(bf16[64,3072]{1,0:T(8,128)(2,1)} %copy.124), channel_id=1, source_target_pairs={{0,2},{1,3},{2,0},{3,1},{4,6},{5,7},{6,4},{7,5},{8,10},{9,11},{10,... | collective-permute-start | bytes 1179656 | tf_op jit(solution)/shard_map/ppermute | solution.py:361
  69.9 46.5 %collective-permute-start.15 = (bf16[4,128,3072]{1,2,0:T(8,128)(2,1)}, bf16[4,128,3072]{1,2,0:T(8,128)(2,1)}, u32[]{:S(2)}, u32[]{:S(2)}) collective-permute-start(bf16[4,128,3072]{1,2,0:T(8,128)(2,1)} %pad_maximum_fusion.1), channel_id=1, source_target_pairs={{0,16},{16,0},{1,17},{17,1},{2,18},{18,2},{3,19},{19,3},{4,20},{20... | collective-permute-start | bytes 9437192 | tf_op jit(solution)/shard_map/ppermute | solution.py:361
  81.7 39.2 %collective-permute-start.10 = (bf16[4,128,3072]{1,2,0:T(8,128)(2,1)}, bf16[4,128,3072]{1,2,0:T(8,128)(2,1)}, u32[]{:S(2)}, u32[]{:S(2)}) collective-permute-start(bf16[4,128,3072]{1,2,0:T(8,128)(2,1)} %pad_maximum_fusion), channel_id=1, source_target_pairs={{0,16},{16,0},{1,17},{17,1},{2,18},{18,2},{3,19},{19,3},{4,20},{20... | collective-permute-start | bytes 9437192 | tf_op jit(solution)/shard_map/ppermute | solution.py:361
  84.4 135.6 %reduce-scatter.5.cloned.1.call-start = ((), (), s32[]{:S(2)}) async-start(), calls=%async_computation.4 | async-start | bytes 2621440 | tf_op jit(solution)/shard_map/reduce_scatter | solution.py:419
  170.5 97.3 %all-gather.7.cloned.1.call-start = ((), (), s32[]{:S(2)}) async-start(), calls=%async_computation.5 | async-start | bytes 2621440 | tf_op jit(solution)/shard_map/all_gather | solution.py:415
  222.2 91.8 %all-gather.13.cloned.1.call-start = ((), (), s32[]{:S(2)}) async-start(), calls=%async_computation.11 | async-start | bytes 2621440 | tf_op jit(solution)/shard_map/all_gather | solution.py:415
  224.2 167.9 %reduce-scatter.9.cloned.1.call-start = ((), (), s32[]{:S(2)}) async-start(), calls=%async_computation.7 | async-start | bytes 2621440 | tf_op jit(solution)/shard_map/reduce_scatter | solution.py:419
  344.6 97.1 %all-gather.9.cloned.1.call-start = ((), (), s32[]{:S(2)}) async-start(), calls=%async_computation.8 | async-start | bytes 2621440 | tf_op jit(solution)/shard_map/all_gather | solution.py:415
  396.3 151.6 %reduce-scatter.7.cloned.1.call-start = ((), (), s32[]{:S(2)}) async-start(), calls=%async_computation.6 | async-start | bytes 2621440 | tf_op jit(solution)/shard_map/reduce_scatter | solution.py:419
  396.4 9.6 %collective-permute-start.23 = (bf16[4,128,3072]{1,2,0:T(8,128)(2,1)}, bf16[4,128,3072]{1,2,0:T(8,128)(2,1)}, u32[]{:S(2)}, u32[]{:S(2)}) collective-permute-start(bf16[4,128,3072]{1,2,0:T(8,128)(2,1)} %bitcast.241), channel_id=1, source_target_pairs={{0,16},{16,0},{1,17},{17,1},{2,18},{18,2},{3,19},{19,3},{4,20},{20... | collective-permute-start | bytes 9437192 | tf_op jit(solution)/shard_map/ppermute | solution.py:361
  405.9 200.3 %reduce-scatter.11.cloned.1.call-start = ((), (), s32[]{:S(2)}) async-start(), calls=%async_computation.9 | async-start | bytes 2621440 | tf_op jit(solution)/shard_map/reduce_scatter | solution.py:419
  502.7 56.9 %collective-permute-start.18 = (bf16[4,128,3072]{1,2,0:T(8,128)(2,1)}, bf16[4,128,3072]{1,2,0:T(8,128)(2,1)}, u32[]{:S(2)}, u32[]{:S(2)}) collective-permute-start(bf16[4,128,3072]{1,2,0:T(8,128)(2,1)} %bitcast.208), channel_id=1, source_target_pairs={{0,16},{16,0},{1,17},{17,1},{2,18},{18,2},{3,19},{19,3},{4,20},{20... | collective-permute-start | bytes 9437192 | tf_op jit(solution)/shard_map/ppermute | solution.py:361
  505.1 19.5 %collective-permute-start.24 = (bf16[2,64,3072]{2,1,0:T(8,128)(2,1)}, bf16[2,64,3072]{2,1,0:T(8,128)(2,1)}, u32[]{:S(2)}, u32[]{:S(2)}) collective-permute-start(bf16[2,64,3072]{2,1,0:T(8,128)(2,1)} %copy.159), channel_id=1, source_target_pairs={{0,1},{1,0},{2,3},{3,2},{4,5},{5,4},{6,7},{7,6},{8,9},{9,8},{10,11... | collective-permute-start | bytes 2359304 | tf_op jit(solution)/shard_map/ppermute | solution.py:361
  507.3 20.9 %collective-permute-start.26 = (bf16[2,64,3072]{2,1,0:T(8,128)(2,1)S(1)}, bf16[2,64,3072]{2,1,0:T(8,128)(2,1)S(1)}, u32[]{:S(2)}, u32[]{:S(2)}) collective-permute-start(bf16[2,64,3072]{2,1,0:T(8,128)(2,1)S(1)} %copy.163), channel_id=1, source_target_pairs={{0,2},{1,3},{2,0},{3,1},{4,6},{5,7},{6,4},{7,5},{8,10},{9,11},{10,... | collective-permute-start | bytes 2359304 | tf_op jit(solution)/shard_map/ppermute | solution.py:361
  545.2 10.8 %collective-permute-start.27 = (bf16[64,3072]{1,0:T(8,128)(2,1)S(1)}, bf16[64,3072]{1,0:T(8,128)(2,1)S(1)}, u32[]{:S(2)}, u32[]{:S(2)}) collective-permute-start(bf16[64,3072]{1,0:T(8,128)(2,1)S(1)} %copy.165), channel_id=1, source_target_pairs={{0,1},{1,0},{2,3},{3,2},{4,5},{5,4},{6,7},{7,6},{8,9},{9,8},{10,11... | collective-permute-start | bytes 1179656 | tf_op jit(solution)/shard_map/ppermute | solution.py:361
  546.5 10.7 %collective-permute-start.25 = (bf16[64,3072]{1,0:T(8,128)(2,1)S(1)}, bf16[64,3072]{1,0:T(8,128)(2,1)S(1)}, u32[]{:S(2)}, u32[]{:S(2)}) collective-permute-start(bf16[64,3072]{1,0:T(8,128)(2,1)S(1)} %copy.161), channel_id=1, source_target_pairs={{0,2},{1,3},{2,0},{3,1},{4,6},{5,7},{6,4},{7,5},{8,10},{9,11},{10,... | collective-permute-start | bytes 1179656 | tf_op jit(solution)/shard_map/ppermute | solution.py:361
  547.6 10.7 %collective-permute-start.30 = (f32[2,4,1024]{2,1,0:T(4,128)S(1)}, f32[2,4,1024]{2,1,0:T(4,128)S(1)}, u32[]{:S(2)}, u32[]{:S(2)}) collective-permute-start(f32[2,4,1024]{2,1,0:T(4,128)S(1)} %fusion.69), channel_id=1, source_target_pairs={{0,1},{1,0},{2,3},{3,2},{4,5},{5,4},{6,7},{7,6},{8,9},{9,8},{10,11... | collective-permute-start | bytes 98312 | tf_op jit(solution)/shard_map/ppermute | solution.py:361
  550.0 29.4 %collective-permute-start.16 = (bf16[256,1024]{1,0:T(8,128)(2,1)}, bf16[256,1024]{1,0:T(8,128)(2,1)}, u32[]{:S(2)}, u32[]{:S(2)}) collective-permute-start(bf16[256,1024]{1,0:T(8,128)(2,1)} %fusion.51), channel_id=1, source_target_pairs={{0,16},{16,0},{1,17},{17,1},{2,18},{18,2},{3,19},{19,3},{4,20},{20... | collective-permute-start | bytes 1572872 | tf_op jit(solution)/shard_map/ppermute | solution.py:361
  558.4 21.0 %collective-permute-start.31 = (f32[2,4,1024]{2,1,0:T(4,128)S(1)}, f32[2,4,1024]{2,1,0:T(4,128)S(1)}, u32[]{:S(2)}, u32[]{:S(2)}) collective-permute-start(f32[2,4,1024]{2,1,0:T(4,128)S(1)} %fusion.88), channel_id=1, source_target_pairs={{0,2},{1,3},{2,0},{3,1},{4,6},{5,7},{6,4},{7,5},{8,10},{9,11},{10,... | collective-permute-start | bytes 98312 | tf_op jit(solution)/shard_map/ppermute | solution.py:361
  567.9 17.6 %collective-permute-start.19 = (bf16[2,64,3072]{2,1,0:T(8,128)(2,1)}, bf16[2,64,3072]{2,1,0:T(8,128)(2,1)}, u32[]{:S(2)}, u32[]{:S(2)}) collective-permute-start(bf16[2,64,3072]{2,1,0:T(8,128)(2,1)} %copy.149), channel_id=1, source_target_pairs={{0,1},{1,0},{2,3},{3,2},{4,5},{5,4},{6,7},{7,6},{8,9},{9,8},{10,11... | collective-permute-start | bytes 2359304 | tf_op jit(solution)/shard_map/ppermute | solution.py:361
  574.6 17.7 %collective-permute-start.21 = (bf16[2,64,3072]{2,1,0:T(8,128)(2,1)}, bf16[2,64,3072]{2,1,0:T(8,128)(2,1)}, u32[]{:S(2)}, u32[]{:S(2)}) collective-permute-start(bf16[2,64,3072]{2,1,0:T(8,128)(2,1)} %copy.153), channel_id=1, source_target_pairs={{0,2},{1,3},{2,0},{3,1},{4,6},{5,7},{6,4},{7,5},{8,10},{9,11},{10,... | collective-permute-start | bytes 2359304 | tf_op jit(solution)/shard_map/ppermute | solution.py:361
  584.7 42.2 %collective-permute-start.33 = (f32[2,4,1024]{2,1,0:T(4,128)S(1)}, f32[2,4,1024]{2,1,0:T(4,128)S(1)}, u32[]{:S(2)}, u32[]{:S(2)}) collective-permute-start(f32[2,4,1024]{2,1,0:T(4,128)S(1)} %add.286), channel_id=1, source_target_pairs={{0,8},{4,12},{8,0},{12,4},{1,9},{5,13},{9,1},{13,5},{2,10},{6,14},... | collective-permute-start | bytes 98312 | tf_op jit(solution)/shard_map/ppermute | solution.py:361
  605.6 10.5 %collective-permute-start.20 = (bf16[64,3072]{1,0:T(8,128)(2,1)}, bf16[64,3072]{1,0:T(8,128)(2,1)}, u32[]{:S(2)}, u32[]{:S(2)}) collective-permute-start(bf16[64,3072]{1,0:T(8,128)(2,1)} %copy.151), channel_id=1, source_target_pairs={{0,2},{1,3},{2,0},{3,1},{4,6},{5,7},{6,4},{7,5},{8,10},{9,11},{10,... | collective-permute-start | bytes 1179656 | tf_op jit(solution)/shard_map/ppermute | solution.py:361
  610.9 16.7 %collective-permute-start.17 = (bf16[256,1024]{1,0:T(8,128)(2,1)}, bf16[256,1024]{1,0:T(8,128)(2,1)}, u32[]{:S(2)}, u32[]{:S(2)}) collective-permute-start(bf16[256,1024]{1,0:T(8,128)(2,1)} %get-tuple-element.98), channel_id=1, source_target_pairs={{0,16},{16,0},{1,17},{17,1},{2,18},{18,2},{3,19},{19,3},{4,20},{20... | collective-permute-start | bytes 1572872 | tf_op jit(solution)/shard_map/ppermute | solution.py:361
  (84 other events, 462.0 us)
Sparse Core Ops, SparseCore 0:
  84.5 47.1 all-gather.10
  170.6 49.3 reduce-scatter.4
  222.3 45.4 all-gather.6
  269.3 44.6 all-gather.12
  344.7 42.4 reduce-scatter.8
  396.5 45.1 all-gather.8
  444.0 42.3 reduce-scatter.6
  558.4 44.1 reduce-scatter.10

commit v2 on v0

--- a/solution.py
+++ b/solution.py
@@ -4,14 +4,729 @@
 import jax
 import jax.numpy as jnp
 from jax import lax
+from jax.experimental import pallas as pl
+from jax.experimental.pallas import tpu as pltpu
 from jax.sharding import PartitionSpec as P
 
 HEAD_DIM = 64
 ROT = 16
-
-
 EPSILON = 1e-05
 NEG_FILL = -1e30
+BF16 = jnp.bfloat16
+F32 = jnp.float32
+TOKENS = 256
+LONGEST_DOC = 512
+
+
+def mm(a, b):
+    return lax.dot_general(a, b, (((1,), (0,)), ((), ())), preferred_element_type=F32)
+
+
+def mm_nt(a, b):
+    return lax.dot_general(a, b, (((1,), (1,)), ((), ())), preferred_element_type=F32)
+
+
+def normalize(full):
+    wide = full.astype(F32)
+    center = wide - jnp.mean(wide, axis=-1, keepdims=True)
+    scale = lax.rsqrt(jnp.mean(center * center, axis=-1, keepdims=True) + EPSILON)
+    return (center * scale, scale)
+
+
+ERFC = (
+    0.17087277,
+    -0.82215223,
+    1.48851587,
+    -1.13520398,
+    0.27886807,
+    -0.18628806,
+    0.09678418,
+    0.37409196,
+    1.00002368,
+    -1.26551223,
+)
+
+
+def gelu_and_slope(pre):
+    size = jnp.abs(pre) * math.sqrt(0.5)
+    t = 1.0 / (1.0 + 0.5 * size)
+    poly = jnp.full_like(t, ERFC[0])
+    for coefficient in ERFC[1:]:
+        poly = poly * t + coefficient
+    bell = jnp.exp(-(size * size))
+    tail = (0.5 * t) * (bell * jnp.exp(poly))
+    below = jnp.where(pre >= 0, 1.0 - tail, tail)
+    return (pre * below, below + pre * (bell * (1.0 / math.sqrt(2.0 * math.pi))))
+
+
+def turn(values, cosine, sine, sign):
+    width = values.shape[-1]
+    half = ROT // 2
+    lane = lax.broadcasted_iota(jnp.int32, values.shape, 1) % HEAD_DIM
+    other = jnp.where(
+        lane < half, -pltpu.roll(values, width - half, 1), pltpu.roll(values, half, 1)
+    )
+    return values * cosine + (sign * other) * sine
+
+
+def rope_tables(docs, starts):
+    half = ROT // 2
+    lane = jnp.arange(128, dtype=jnp.int32) % HEAD_DIM
+    freqs = 10000.0 ** (-2.0 * (lane % half).astype(F32) / ROT)
+    position = (jnp.arange(docs.shape[0], dtype=jnp.int32) - starts).astype(F32)
+    angles = position[:, None] * freqs[None, :]
+    rotated = (lane < ROT)[None, :]
+    return (jnp.where(rotated, jnp.cos(angles), 1.0), jnp.where(rotated, jnp.sin(angles), 0.0))
+
+
+def params(mib=24):
+    return pltpu.CompilerParams(vmem_limit_bytes=mib << 20)
+
+
+def chunk_call(body, name, index, outs, inputs, kept=()):
+    given = len(inputs)
+
+    def kernel(number, *refs):
+        body(number, *refs[:given], *refs[given + len(kept) :])
+
+    spec = lambda block, at: pl.BlockSpec(block, lambda i, number: at(number[0]))
+    return pl.pallas_call(
+        kernel,
+        grid_spec=pltpu.PrefetchScalarGridSpec(
+            num_scalar_prefetch=1,
+            grid=(1,),
+            in_specs=[spec(block, at) for _, block, at in inputs]
+            + [pl.BlockSpec(memory_space=pl.ANY) for _ in kept],
+            out_specs=[spec(block, at) for _, _, block, at in outs],
+        ),
+        out_shape=[jax.ShapeDtypeStruct(shape, dtype) for shape, dtype, _, _ in outs],
+        input_output_aliases={1 + given + i: i for i in range(len(kept))},
+        compiler_params=params(),
+        name=name,
+    )(index.reshape(1).astype(jnp.int32), *[array for array, _, _ in inputs], *kept)
+
+
+HERE = lambda i: (0, 0)
+ROWS = lambda i: (i, 0)
+LANES = lambda i: (0, i)
+
+
+def added(refs):
+    whole = refs[0][...]
+    for ref in refs[1:]:
+        whole = whole + ref[...]
+    return whole
+
+
+def project_body(ways, number, *refs):
+    norms, wqkv, wup, cosine, sine, attn_in, feed_in, qkv, value_t, active, slope = refs[ways:]
+    normed, _ = normalize(added(refs[:ways]))
+    attn = (normed * norms[0:1] + norms[1:2]).astype(BF16)
+    feed = (normed * norms[2:3] + norms[3:4]).astype(BF16)
+    attn_in[...] = attn
+    feed_in[...] = feed
+    width = qkv.shape[2]
+    for part in range(3):
+        piece = mm(attn, wqkv[:, part * width : (part + 1) * width])
+        for pair in range(width // 128):
+            lanes = slice(pair * 128, (pair + 1) * 128)
+            one = piece[:, lanes]
+            if part < 2:
+                one = turn(one, cosine[...], sine[...], 1.0)
+            else:
+                value_t[lanes, :] = one.T.astype(BF16)
+            qkv[part, :, lanes] = one.astype(BF16)
+    hidden = wup.shape[1]
+    for start in range(0, hidden, 256):
+        lanes = slice(start, start + 256)
+        act, der = gelu_and_slope(mm(feed, wup[:, lanes]))
+        active[:, lanes] = act.astype(BF16)
+        slope[:, lanes] = der.astype(BF16)
+
+
+def project(chunk, index, tokens, norms, pack, tables, width, hidden, kept):
+    model = pack.shape[0]
+    return chunk_call(
+        partial(project_body, len(chunk)),
+        "project",
+        index,
+        [
+            ((tokens, model), BF16, (TOKENS, model), ROWS),
+            ((tokens, model), BF16, (TOKENS, model), ROWS),
+            ((3, tokens, width), BF16, (3, TOKENS, width), lambda i: (0, i, 0)),
+            ((width, tokens), BF16, (width, TOKENS), LANES),
+            ((tokens, hidden), BF16, (TOKENS, hidden), ROWS),
+            ((tokens, hidden), BF16, (TOKENS, hidden), ROWS),
+        ],
+        [(way, (TOKENS, model), HERE) for way in chunk]
+        + [
+            (norms, (4, model), HERE),
+            (pack, (model, 3 * width), HERE),
+            (pack, (model, hidden), lambda i: (0, 1)),
+            (tables[0], (TOKENS, 128), ROWS),
+            (tables[1], (TOKENS, 128), ROWS),
+        ],
+        kept,
+    )
+
+
+def own_lanes(values, head, factor=None):
+    lane = lax.broadcasted_iota(jnp.int32, values.shape, 1) // HEAD_DIM
+    if factor is not None:
+        values = values * jnp.asarray(factor, values.dtype)
+    return jnp.where(lane == head, values, jnp.zeros_like(values))
+
+
+def attend_body(number, starts, qkv, value_t, active, wout, wdown, context, logsum, partial_sum):
+    index = number[0]
+    tokens, width = (qkv.shape[1], qkv.shape[2])
+    reach = min(tokens, TOKENS + LONGEST_DOC)
+    first = pl.multiple_of(jnp.maximum(index * TOKENS + TOKENS - reach, 0), TOKENS)
+    at = pl.multiple_of(index * TOKENS, TOKENS)
+    key_at = first + lax.broadcasted_iota(jnp.int32, (reach, TOKENS), 0)
+    query_at = at + lax.broadcasted_iota(jnp.int32, (reach, TOKENS), 1)
+    allowed = (key_at <= query_at) & (key_at >= starts[0:1, pl.ds(at, TOKENS)])
+    outs, sums = ([], [])
+    for pair in range(width // 128):
+        lanes = slice(pair * 128, (pair + 1) * 128)
+        keys = qkv[1, pl.ds(first, reach), lanes]
+        queries = qkv[0, pl.ds(at, TOKENS), lanes]
+        for head in range(128 // HEAD_DIM):
+            query = own_lanes(queries, head, 1.0 / math.sqrt(HEAD_DIM))
+            scores = jnp.where(allowed, mm_nt(keys, query), NEG_FILL)
+            peak = jnp.max(scores, axis=0, keepdims=True)
+            raised = jnp.exp(scores - peak)
+            total = jnp.sum(raised, axis=0, keepdims=True)
+            sums.append(peak + jnp.log(total))
+            begin = pair * 128 + head * HEAD_DIM
+            values = value_t[begin : begin + HEAD_DIM, pl.ds(first, reach)]
+            outs.append(mm(values, raised.astype(BF16)) * (1.0 / total))
+    mixed = jnp.concatenate(outs, axis=0).T.astype(BF16)
+    context[...] = mixed
+    for head, one in enumerate(sums):
+        logsum[head : head + 1, :] = one
+    partial_sum[...] = (mm_nt(mixed, wout[...]) + mm_nt(active[...], wdown[...])).astype(BF16)
+
+
+def attend(index, starts, qkv, value_t, active, pack, kept):
+    _, tokens, width = qkv.shape
+    hidden = active.shape[1]
+    model = pack.shape[0]
+    heads = width // HEAD_DIM
+    return chunk_call(
+        attend_body,
+        "attend",
+        index,
+        [
+            ((tokens, width), BF16, (TOKENS, width), ROWS),
+            ((heads, tokens), F32, (heads, TOKENS), LANES),
+            ((TOKENS, model), BF16, (TOKENS, model), HERE),
+        ],
+        [
+            (starts, (1, tokens), HERE),
+            (qkv, (3, tokens, width), lambda i: (0, 0, 0)),
+            (value_t, (width, tokens), HERE),
+            (active, (TOKENS, hidden), ROWS),
+            (pack, (model, width), lambda i: (0, 3)),
+            (pack, (model, hidden), lambda i: (0, 2)),
+        ],
+        kept,
+    )
+
+
+def through_branch_body(ways, number, *refs):
+    wout, wdown, slope, pre_grad, context_grad, copied = refs[ways:]
+    grads = added(refs[:ways])
+    copied[...] = grads
+    pre_grad[...] = (mm(grads, wdown[...]) * slope[...].astype(F32)).astype(BF16)
+    context_grad[...] = mm(grads, wout[...]).astype(BF16)
+
+
+def through_branch(chunk, index, pack, slope, width, kept):
+    tokens, hidden = slope.shape
+    model = pack.shape[0]
+    return chunk_call(
+        partial(through_branch_body, len(chunk)),
+        "through_branch",
+        index,
+        [
+            ((tokens, hidden), BF16, (TOKENS, hidden), ROWS),
+            ((tokens, width), BF16, (TOKENS, width), ROWS),
+            ((tokens, model), BF16, (TOKENS, model), ROWS),
+        ],
+        [(way, (TOKENS, model), HERE) for way in chunk]
+        + [
+            (pack, (model, width), lambda i: (0, 3)),
+            (pack, (model, hidden), lambda i: (0, 2)),
+            (slope, (TOKENS, hidden), ROWS),
+        ],
+        kept,
+    )
+
+
+def window_of(block, size):
+    return (max(0, block * size - LONGEST_DOC), (block + 1) * size)
+
+
+def attend_back_kernel(starts, qkv, grads, logsum, cosine, sine, out, key_sum, value_sum):
+    size = TOKENS
+    factor = 1.0 / math.sqrt(HEAD_DIM)
+    tokens = qkv.shape[1]
+    heads = 128 // HEAD_DIM
+    key_t = qkv[1].astype(F32).T.astype(BF16)
+    key_sum[...] = jnp.zeros_like(key_sum)
+    value_sum[...] = jnp.zeros_like(value_sum)
+    for block in range(tokens // size):
+        first, last = window_of(block, size)
+        rows = slice(block * size, (block + 1) * size)
+        shape = (last - first, size)
+        key_at = first + lax.broadcasted_iota(jnp.int32, shape, 0)
+        query_at = block * size + lax.broadcasted_iota(jnp.int32, shape, 1)
+        allowed = (key_at <= query_at) & (key_at >= starts[0:1, rows])
+        key_part, value_part, query_parts = (0.0, 0.0, [])
+        for head in range(heads):
+            query = own_lanes(qkv[0, rows], head, factor)
+            grad = own_lanes(grads[rows], head)
+            scores = jnp.where(allowed, mm_nt(qkv[1, first:last], query), NEG_FILL)
+            probs = jnp.exp(scores - logsum[0, head : head + 1, rows])
+            probs_grad = mm_nt(qkv[2, first:last], grad)
+            inner = jnp.sum(probs_grad * probs, axis=0, keepdims=True)
+            score_grad = (probs * (probs_grad - inner)).astype(BF16)
+            key_part += mm(score_grad, query)
+            value_part += mm(probs.astype(BF16), grad)
+            query_parts.append(
+                mm(key_t[head * HEAD_DIM : (head + 1) * HEAD_DIM, first:last], score_grad)
+            )
+        key_sum[first:last] += key_part
+        value_sum[first:last] += value_part
+        query_grad = jnp.concatenate(query_parts, axis=0).T * factor
+        out[0, rows] = turn(query_grad, cosine[rows], sine[rows], -1.0).astype(BF16)
+    out[1] = turn(key_sum[...], cosine[...], sine[...], -1.0).astype(BF16)
+    out[2] = value_sum[...].astype(BF16)
+
+
+def attend_back(starts, qkv, context_grad, logsum, tables):
+    _, tokens, width = qkv.shape
+    pairs = width // 128
+    heads = 128 // HEAD_DIM
+    return pl.pallas_call(
+        attend_back_kernel,
+        grid=(pairs,),
+        in_specs=[
+            pl.BlockSpec((1, tokens), lambda p: (0, 0)),
+            pl.BlockSpec((3, tokens, 128), lambda p: (0, 0, p)),
+            pl.BlockSpec((tokens, 128), lambda p: (0, p)),
+            pl.BlockSpec((1, heads, tokens), lambda p: (p, 0, 0)),
+            pl.BlockSpec((tokens, 128), lambda p: (0, 0)),
+            pl.BlockSpec((tokens, 128), lambda p: (0, 0)),
+        ],
+        out_specs=pl.BlockSpec((3, tokens, 128), lambda p: (0, 0, p)),
+        out_shape=jax.ShapeDtypeStruct((3, tokens, width), BF16),
+        scratch_shapes=[pltpu.VMEM((tokens, 128), F32), pltpu.VMEM((tokens, 128), F32)],
+        compiler_params=params(),
+        name="attend_back",
+    )(starts, qkv, context_grad, logsum.reshape(pairs, heads, tokens), *tables)
+
+
+def through_inputs_body(ways, number, *refs):
+    norms, project_grad, pre_grad, wqkv, wup, normed_grad, terms = refs[ways:]
+    normed, _ = normalize(added(refs[:ways]))
+    width = project_grad.shape[2]
+    attn = mm_nt(project_grad[0], wqkv[:, :width])
+    attn += mm_nt(project_grad[1], wqkv[:, width : 2 * width])
+    attn += mm_nt(project_grad[2], wqkv[:, 2 * width :])
+    feed = mm_nt(pre_grad[...], wup[...])
+    normed_grad[...] = (attn * norms[0:1] + feed * norms[2:3]).astype(BF16)
+    terms[0:1] = jnp.sum(attn * normed, axis=0, keepdims=True)
+    terms[1:2] = jnp.sum(attn, axis=0, keepdims=True)
+    terms[2:3] = jnp.sum(feed * normed, axis=0, keepdims=True)
+    terms[3:4] = jnp.sum(feed, axis=0, keepdims=True)
+
+
+def through_inputs(chunk, index, norms, project_grad, pre_grad, pack):
+    model = pack.shape[0]
+    hidden = pre_grad.shape[1]
+    width = project_grad.shape[2]
+    return chunk_call(
+        partial(through_inputs_body, len(chunk)),
+        "through_inputs",
+        index,
+        [
+            ((TOKENS, model), BF16, (TOKENS, model), HERE),
+            ((4, model), F32, (4, model), HERE),
+        ],
+        [(way, (TOKENS, model), HERE) for way in chunk]
+        + [
+            (norms, (4, model), HERE),
+            (project_grad, (3, TOKENS, width), lambda i: (0, i, 0)),
+            (pre_grad, (TOKENS, hidden), ROWS),
+            (pack, (model, 3 * width), HERE),
+            (pack, (model, hidden), lambda i: (0, 1)),
+        ],
+    )
+
+
+def outer_kernel(blocks, attn_in, feed_in, upstream, project_grad, context, pre_grad, active, out):
+    step = pl.program_id(0)
+
+    def fill(left, right):
+        for number in range(4):
+            lanes = pl.ds(pl.multiple_of(blocks[number] * 128, 128), 128)
+            out[number] = lax.dot_general(
+                left[:, lanes], right, (((0,), (0,)), ((), ())), preferred_element_type=F32
+            ).astype(BF16)
+
+    @pl.when(step < 3)
+    def _():
+        fill(attn_in, project_grad[0])
+
+    @pl.when(step == 3)
+    def _():
+        fill(upstream, context[...])
+
+    @pl.when((step >= 4) & (step < 8))
+    def _():
+        fill(feed_in, pre_grad[...])
+
+    @pl.when(step >= 8)
+    def _():
+        fill(upstream, active[...])
+
+
+def weight_grads(blocks, saved, upstream, pre_grad, project_grad):
+    attn_in, feed_in, active, context = saved
+    tokens, model = attn_in.shape
+    width = context.shape[1]
+    steps = 4 + 2 * active.shape[1] // width
+    whole = pl.BlockSpec((tokens, model), lambda j, blocks: (0, 0))
+    return pl.pallas_call(
+        outer_kernel,
+        grid_spec=pltpu.PrefetchScalarGridSpec(
+            num_scalar_prefetch=1,
+            grid=(steps,),
+            in_specs=[
+                whole,
+                whole,
+                whole,
+                pl.BlockSpec((1, tokens, width), lambda j, blocks: (jnp.minimum(j, 2), 0, 0)),
+                pl.BlockSpec((tokens, width), lambda j, blocks: (0, 0)),
+                pl.BlockSpec((tokens, width), lambda j, blocks: (0, jnp.clip(j - 4, 0, 3))),
+                pl.BlockSpec((tokens, width), lambda j, blocks: (0, jnp.clip(j - 8, 0, 3))),
+            ],
+            out_specs=pl.BlockSpec((4, model // 8, width), lambda j, blocks: (0, 0, j)),
+        ),
+        out_shape=jax.ShapeDtypeStruct((4, model // 8, steps * width), BF16),
+        compiler_params=params(32),
+        name="weight_grads",
+    )(blocks.astype(jnp.int32), attn_in, feed_in, upstream, project_grad, context, pre_grad, active)
+
+
+def fold_kernel(kept, came, side, ahead, rest):
+    half = kept.shape[1] // 2
+    both = (kept[...].astype(F32) + came[...].astype(F32)).astype(BF16)
+    side[0] = both[1, :half]
+    side[1] = both[3, :half]
+    ahead[0] = both[2, half:]
+    ahead[1] = both[3, half:]
+    rest[0] = both[0, :half]
+    rest[1] = both[2, :half]
+    rest[2] = both[0, half:]
+    rest[3] = both[1, half:]
+
+
+def fold(kept, came):
+    _, rows, width = kept.shape
+    step = width // 6
+    block = lambda n, r: pl.BlockSpec((n, r, step), lambda j: (0, 0, j))
+    shape = lambda n: jax.ShapeDtypeStruct((n, rows // 2, width), BF16)
+    return pl.pallas_call(
+        fold_kernel,
+        grid=(6,),
+        in_specs=[block(4, rows), block(4, rows)],
+        out_specs=[block(2, rows // 2), block(2, rows // 2), block(4, rows // 2)],
+        out_shape=[shape(2), shape(2), shape(4)],
+        compiler_params=params(),
+        name="fold",
+    )(kept, came)
+
+
+def assemble_kernel(place, *refs):
+    pieces, whole = (refs[:-1], refs[-1])
+    rows = pieces[0].shape[0]
+    for order, piece in enumerate(pieces):
+        core, number, part = (order // 8, (order % 8) // 2, order % 2)
+        at = ((place[1] ^ number) * 2 + (place[0] ^ core)) * (2 * rows) + part * rows
+        whole[pl.ds(pl.multiple_of(at, rows), rows), :] = piece[...]
+
+
+def assemble(place, pieces):
+    rows, width = pieces[0].shape
+    step = width // 6
+    return pl.pallas_call(
+        assemble_kernel,
+        grid_spec=pltpu.PrefetchScalarGridSpec(
+            num_scalar_prefetch=1,
+            grid=(6,),
+            in_specs=[pl.BlockSpec((rows, step), lambda j, place: (0, j)) for _ in pieces],
+            out_specs=pl.BlockSpec((len(pieces) * rows, step), lambda j, place: (0, j)),
+        ),
+        out_shape=jax.ShapeDtypeStruct((len(pieces) * rows, width), BF16),
+        compiler_params=params(),
+        name="assemble",
+    )(place.astype(jnp.int32), *pieces)
+
+
+def unpack_kernel(place, upper, lower, came, qkv, out, up, down):
+    width, hidden = (out.shape[0], up.shape[1])
+    half = came.shape[0]
+    own = jnp.concatenate([upper[...], lower[...]], axis=0)
+    for core, block in ((place[0], own), (1 - place[0], came[...].astype(F32))):
+        rows = pl.ds(pl.multiple_of(core * half, half), half)
+        qkv[rows, :] = block[:, : 3 * width]
+        out[:, rows] = block[:, 3 * width : 4 * width].T
+        up[rows, :] = block[:, 4 * width : 4 * width + hidden]
+        down[:, rows] = block[:, 4 * width + hidden :].T
+
+
+def unpack(sec, upper, lower, came, width, hidden):
+    half = came.shape[0]
+    shapes = [(2 * half, 3 * width), (width, 2 * half), (2 * half, hidden), (hidden, 2 * half)]
+    return pl.pallas_call(
+        unpack_kernel,
+        grid_spec=pltpu.PrefetchScalarGridSpec(
+            num_scalar_prefetch=1,
+            grid=(1,),
+            in_specs=[
+                pl.BlockSpec(array.shape, lambda i, place: (0, 0)) for array in (upper, lower, came)
+            ],
+            out_specs=[pl.BlockSpec(shape, lambda i, place: (0, 0)) for shape in shapes],
+        ),
+        out_shape=[jax.ShapeDtypeStruct(shape, F32) for shape in shapes],
+        compiler_params=params(32),
+        name="unpack",
+    )(sec.reshape(1).astype(jnp.int32), upper, lower, came)
+
+
+def swap(block, axis, bit):
+    return lax.ppermute(block, axis, [(i, i ^ bit) for i in range(lax.axis_size(axis))])
+
+
+def after(values, *earlier):
+    flat, tree = jax.tree.flatten(values)
+    held = lax.optimization_barrier((*flat, *earlier))
+    return jax.tree.unflatten(tree, held[: len(flat)])
+
+
+def total_of(value):
+    for axis in ("section", "col", "row"):
+        bit = 1
+        while bit < lax.axis_size(axis):
+            value = value + swap(value, axis, bit)
+            bit *= 2
+    return value
+
+
+def pick(stack, index):
+    return lax.dynamic_index_in_dim(stack, index, 0, keepdims=False)
+
+
+def spread_layer(parts, meanwhile):
+    upper, lower = parts
+    side = [swap(part, "col", 1) for part in parts]
+    ahead = [swap(part, "col", 2) for part in parts]
+    if meanwhile is not None:
+        side, ahead = after((side, ahead), meanwhile)
+    across = [swap(side[0], "col", 2), swap(ahead[1], "col", 1)]
+    mine = [*parts, *side, *ahead, *across]
+    theirs = [swap(piece, "section", 1) for piece in mine]
+    return (mine + theirs, across)
+
+
+def sum_layer(sec, col, saved, upstream, pre_grad, project_grad):
+    order = col ^ jnp.arange(4, dtype=jnp.int32)
+    leaving = weight_grads(order * 2 + 1 - sec, saved, upstream, pre_grad, project_grad)
+    came = swap(leaving, "section", 1)
+    kept = weight_grads(order * 2 + sec, saved, upstream, pre_grad, project_grad)
+    side, ahead, rest = fold(kept, came)
+    first = swap(side, "col", 1)
+    second = swap(ahead, "col", 2)
+    add = lambda a, b: a.astype(F32) + b.astype(F32)
+    upper = swap(add(rest[1], first[1]).astype(BF16), "col", 2)
+    lower = swap(add(rest[3], second[1]).astype(BF16), "col", 1)
+    return (add(add(rest[0], first[0]), upper), add(add(rest[2], second[0]), lower))
+
+
+def along_row(block, pairs):
+    return lax.ppermute(block, "row", pairs)
+
+
+ONE_OVER = [(0, 1), (1, 0), (2, 3), (3, 2)]
+TWO_OVER = [(0, 2), (2, 0), (1, 3), (3, 1)]
+MIDDLE = [(1, 2), (2, 1)]
+OUTWARD = [(1, 0), (2, 3)]
+INWARD = [(0, 1), (3, 2)]
+
+
+def gather_tokens(own):
+    far = along_row(own, TWO_OVER)
+    near = along_row(own, ONE_OVER)
+    middle = along_row(own, MIDDLE)
+    passed = along_row(far, OUTWARD)
+    return [(own,), (near,), (far,), (middle, passed)]
+
+
+def scatter_tokens(chunk_of):
+    last = chunk_of(3)
+    passed = along_row(last, INWARD)
+    middle = along_row(last, MIDDLE)
+    far = chunk_of(2)
+    near = along_row(chunk_of(1), ONE_OVER)
+    far = along_row((far.astype(F32) + passed.astype(F32)).astype(BF16), TWO_OVER)
+    own = chunk_of(0)
+    return (own.astype(F32) + near.astype(F32)) + (middle.astype(F32) + far.astype(F32))
+
+
+def fast_shards(
+    hidden_in,
+    doc_ids,
+    qkv_weight,
+    out_weight,
+    up_weight,
+    down_weight,
+    attn_gain,
+    attn_shift,
+    mlp_gain,
+    mlp_shift,
+    out_cotangent,
+):
+    sec, row, col = (lax.axis_index("section"), lax.axis_index("row"), lax.axis_index("col"))
+    cols, rows = (lax.axis_size("col"), lax.axis_size("row"))
+    model = hidden_in.shape[3]
+    tokens = doc_ids.shape[2]
+    width = qkv_weight.shape[3]
+    hidden = up_weight.shape[2]
+    block = qkv_weight.shape[1]
+    first = sec == 0
+    x_own = pick(hidden_in[:, 0], sec)
+    docs = pick(doc_ids[:, 0], sec)
+    given = pick(out_cotangent[:, 0], sec)
+
+    own_pack = jnp.concatenate(
+        [
+            qkv_weight[0].reshape(block, 3 * width),
+            out_weight[0].T,
+            up_weight[0],
+            down_weight[0].T,
+        ],
+        axis=1,
+    )
+    quarter = block // 4
+    part_of = lambda core, part: lax.dynamic_slice_in_dim(
+        own_pack, core * (block // 2) + part * quarter, quarter
+    )
+    own_parts = [part_of(sec, part) for part in range(2)]
+    other_parts = [swap(part_of(1 - sec, part), "section", 1) for part in range(2)]
+    parts0 = [jnp.where(first, a, b) for a, b in zip(own_parts, other_parts)]
+    parts1 = [jnp.where(first, b, a) for a, b in zip(own_parts, other_parts)]
+    share = attn_gain.shape[1]
+    vectors = jnp.stack([attn_gain[0], attn_shift[0], mlp_gain[0], mlp_shift[0]])
+    norms = total_of(
+        lax.dynamic_update_slice(
+            jnp.zeros((2, 4, model), F32), vectors[None], (sec, 0, (row * cols + col) * share)
+        )
+    )
+    chunks_x0 = gather_tokens(x_own)
+    pieces0, across0 = spread_layer(parts0, norms)
+    pieces1, _ = spread_layer(after(parts1, *across0), None)
+    place = jnp.stack([sec, col])
+    packs = [assemble(place, pieces0), assemble(place, pieces1)]
+
+    starts = jnp.sum((docs[None, :] < docs[:, None]).astype(jnp.int32), axis=1)
+    tables = rope_tables(docs, starts)
+    starts = starts[None]
+
+    def forward(chunks, own, layer):
+        kept = ()
+        for number, chunk in enumerate(chunks):
+            kept = project(
+                chunk, row ^ number, tokens, norms[layer], packs[layer], tables, width, hidden, kept
+            )
+        attn_in, feed_in, qkv, value_t, active, slope = kept
+        results = []
+
+        def chunk_of(number):
+            *now, share_of = attend(
+                row ^ number, starts, qkv, value_t, active, packs[layer], tuple(results)
+            )
+            results[:] = now
+            return share_of
+
+        result = own.astype(F32) + scatter_tokens(chunk_of)
+        context, logsum = results
+        return (result.astype(BF16), (attn_in, feed_in, active, context), (qkv, slope, logsum))
+
+    def backward(chunks, own, layer, saved, held, chunks_grads, own_grads):
+        qkv, slope, logsum = held
+        kept = ()
+        for number, chunk in enumerate(chunks_grads):
+            kept = through_branch(chunk, row ^ number, packs[layer], slope, width, kept)
+        pre_grad, context_grad, grads = kept
+        project_grad = attend_back(starts, qkv, context_grad, logsum, tables)
+        terms, pieces = ([], [])
+
+        def chunk_of(number):
+            piece, term = through_inputs(
+                chunks[number], row ^ number, norms[layer], project_grad, pre_grad, packs[layer]
+            )
+            terms.append(term)
+            pieces.append(piece)
+            return piece
+
+        total = scatter_tokens(chunk_of)
+        normed, scale = normalize(own)
+        result = own_grads.astype(F32) + scale * (
+            total
+            - jnp.mean(total, axis=-1, keepdims=True)
+            - normed * jnp.mean(total * normed, axis=-1, keepdims=True)
+        )
+        pre_grad, project_grad = after((pre_grad, project_grad), *pieces)
+        sums = sum_layer(sec, col, saved, grads, pre_grad, project_grad)
+        return (result.astype(BF16), sums, sum(terms))
+
+    y0_own, saved0, held0 = forward(chunks_x0, x_own, 0)
+    chunks_x1 = gather_tokens(y0_own)
+    chunks_g1 = gather_tokens(after(given, chunks_x0[3][1]))
+    y1_own, saved1, held1 = forward(chunks_x1, y0_own, 1)
+    dx1_own, sums1, terms1 = backward(chunks_x1, y0_own, 1, saved1, held1, chunks_g1, given)
+    chunks_g0 = gather_tokens(dx1_own)
+    dx0_own, sums0, terms0 = backward(chunks_x0, x_own, 0, saved0, held0, chunks_g0, dx1_own)
+
+    choose = lambda here, there: jnp.where(first, here, there)
+    leaving = jnp.concatenate([choose(b, a) for a, b in zip(sums0, sums1)]).astype(BF16)
+    upper, lower = [choose(a, b) for a, b in zip(sums0, sums1)]
+    qkv_grad, out_grad, up_grad, down_grad = unpack(
+        sec, upper, lower, swap(leaving, "section", 1), width, hidden
+    )
+    terms = pick(total_of(jnp.stack([terms0, terms1])), sec)
+    terms = lax.dynamic_slice_in_dim(terms, (row * cols + col) * share, share, 1)
+
+    def by_layer(zero, one):
+        away = swap(choose(one, zero), "section", 1)
+        here = choose(zero, one)
+        return jnp.stack([choose(here, away), choose(away, here)])
+
+    return (
+        by_layer(y0_own, y1_own)[None, :, None],
+        by_layer(dx0_own, dx1_own)[None, :, None],
+        qkv_grad.reshape(1, block, 3, width),
+        out_grad[None],
+        up_grad[None],
+        down_grad[None],
+        terms[None, 0],
+        terms[None, 1],
+        terms[None, 2],
+        terms[None, 3],
+    )
 
 
 def from_behind(block, axis, distance):
@@ -51,13 +766,6 @@
     return jnp.concatenate(
         [front * cosine + back * sine, back * cosine - front * sine, grads[..., ROT:]], axis=-1
     )
-
-
-def normalize(full):
-    wide = full.astype(jnp.float32)
-    center = wide - jnp.mean(wide, axis=-1, keepdims=True)
-    scale = lax.rsqrt(jnp.mean(center * center, axis=-1, keepdims=True) + EPSILON)
-    return (center * scale, scale)
 
 
 def block_mask(docs, start, size):
@@ -249,7 +957,7 @@
     return (input_grad, (qkv_part, out_part, up_part, down_part), gain_terms)
 
 
-def shards(
+def general_shards(
     hidden_in,
     doc_ids,
     qkv_weight,
@@ -370,6 +1078,20 @@
     )
 
 
+def shards(*arrays):
+    hidden_in, qkv_weight, up_weight = (arrays[0], arrays[2], arrays[4])
+    micro, seqs, own_tokens, model = hidden_in.shape
+    width, hidden = (qkv_weight.shape[3], up_weight.shape[2])
+    sizes = tuple(lax.axis_size(axis) for axis in ("section", "row", "col"))
+    fits = (
+        sizes == (2, 4, 4) and (micro, seqs) == (2, 1)
+        and own_tokens == TOKENS
+        and width % 128 == 0
+        and 4 * width == hidden
+    )
+    return fast_shards(*arrays) if fits else general_shards(*arrays)
+
+
 def solution(mesh):
     placed = (
         P(None, "col", "row", None),

time: 1430 us -> 541 us (0.38); the launches traced: 1400 us -> 533 us
  waiting for transfers between devices: 609 us -> 184 us
  matrix products: 342 us -> 0 us
  Pallas kernels: 0 us -> 162 us
  blocking collectives: 138 us -> 0 us
  local copies, waits for them, and re-layouts: 152 us -> 53.1 us
  other arithmetic: 123 us -> 24.7 us
  starting transfers between devices: 10.5 us -> 107 us
  between operations: 18.4 us -> 2.86 us
    dot_general x87 -> x0, matrix products: 342 us -> none  [the longest x3 52.3 us: layer_forward(): jnp.dot(active, weights[3], preferred_element_type=jnp.float32)]
    all_gather x12 -> x0, waiting for transfers between devices: 337 us -> none  [the longest x6 198 us: gather_features(): return lax.all_gather(shard, 'row', axis=0, tiled=True)]
    reduce_scatter x13 -> x0, waiting for transfers between devices: 263 us -> none  [the longest x3 91 us: layer_backward(): lax.psum_scatter(feed_grad.astype(jnp.bfloat16), 'row', scatter_dimension...]
    ppermute x4 -> x85, waiting for transfers between devices: 6.5 us -> 184 us  [the longest x32 103 us: along_row(): return lax.ppermute(block, 'row', pairs)]
    pallas_call x0 -> x43, Pallas kernels: none -> 162 us  [the longest x32 85.9 us: chunk_call(): pl.pallas_call(kernel, grid_spec=pltpu.PrefetchScalarGridSpec(num_scalar_...]
    unnamed x2 -> x0, blocking collectives: 125 us -> none
    ppermute x4 -> x85, starting transfers between devices: 8.67 us -> 107 us  [the longest x53 54.7 us: swap(): lax.ppermute(block, axis, [(i, i ^ bit) for i in range(lax.axis_size(axis...]
    dynamic_update_slice x12 -> x1, local copies, waits for them, and re-layouts: 65.6 us -> 0.17 us  [fast_shards(): lax.dynamic_update_slice(jnp.zeros((2, 4, model), F32), vectors[None], (s...]
  transfers between devices with their start and end apart: 29 -> 85, of which waited for: 20 -> 28; matrix products, arithmetic and copies ran while one was open for 22% -> 5% of each run, Pallas kernels for 0% -> 27%
where the time goes in v2:
time: 541 us; the launch traced here: 533 us
  waiting for transfers between devices  184 us (34%)
  Pallas kernels  162 us (30%)
  starting transfers between devices  107 us (20%)
  local copies, waits for them, and re-layouts  53.1 us (10%)
  other arithmetic  24.7 us (5%)
    ppermute x32, waiting for transfers between devices, along_row(): return lax.ppermute(block, 'row', pairs)  103 us
    pallas_call x32, Pallas kernels, chunk_call(): pl.pallas_call(kernel, grid_spec=pltpu.PrefetchScalarGridSpec(num_scalar_...  85.9 us
    ppermute x53, waiting for transfers between devices, swap(): lax.ppermute(block, axis, [(i, i ^ bit) for i in range(lax.axis_size(axis...  80.3 us
    ppermute x53, starting transfers between devices, swap(): lax.ppermute(block, axis, [(i, i ^ bit) for i in range(lax.axis_size(axis...  54.7 us
    ppermute x32, starting transfers between devices, along_row(): return lax.ppermute(block, 'row', pairs)  51.8 us
    unnamed x260, local copies, waits for them, and re-layouts  49.9 us
    pallas_call x4, Pallas kernels, weight_grads(): pl.pallas_call(outer_kernel, grid_spec=pltpu.PrefetchScalarGridSpec(num_s...  36.1 us
    pallas_call x2, Pallas kernels, attend_back(): pl.pallas_call(attend_back_kernel, grid=(pairs,), in_specs=[pl.BlockSpec(...  22.1 us
  transfers between devices with their start and end apart: 85, of which 28 were waited for; matrix products, arithmetic and copies ran while one was open for 5% of the time, Pallas kernels for 27%

profile of v2, /device:TPU:1, one launch (start us, length us, event | category | flops | bytes accessed | tf_op | source)
XLA Modules:
  0.0 533.0 jit_solution(17174422481011777237)
XLA Ops:
  25.6 20.0 %collective-permute-done.7 = f32[2,4,1024]{2,1,0:T(4,128)S(1)} collective-permute-done((f32[2,4,1024]{2,1,0:T(4,128)S(1)}, f32[2,4,1024]{2,1,0:T(4,128)S(1)}, u32[]{:S(2)}, u32[]{:S(2)}) %collective-permute-start.7) | collective-permute-done | bytes 32800 | tf_op jit(solution)/shard_map/ppermute | solution.py:511
  50.5 4.8 collective-permute-done.12.refs_4_
  66.5 4.7 collective-permute-done.15.refs_7_
  87.1 4.8 assemble.2.refs_2_.refs_3_.refs_4_.refs_5_.refs_1_.refs_6_
  91.9 4.2 project.8
  96.1 3.9 project.9
  103.0 3.9 project.11
  128.1 4.0 collective-permute-done.33.refs_3_
  142.1 26.1 %collective-permute-done.28 = bf16[256,1024]{1,0:T(8,128)(2,1)S(1)} collective-permute-done((bf16[256,1024]{1,0:T(8,128)(2,1)S(1)}, bf16[256,1024]{1,0:T(8,128)(2,1)S(1)}, u32[]{:S(2)}, u32[]{:S(2)}) %collective-permute-start.28) | collective-permute-done | bytes 524320 | tf_op jit(solution)/shard_map/ppermute | solution.py:560
  177.0 20.8 %collective-permute-done.30.refs_0_ = bf16[256,1024]{1,0:T(8,128)(2,1)S(1)} collective-permute-done((bf16[256,1024]{1,0:T(8,128)(2,1)S(1)}, bf16[256,1024]{1,0:T(8,128)(2,1)S(1)}, u32[]{:S(2)}, u32[]{:S(2)}) %collective-permute-start.30) | collective-permute-done | bytes 524320 | tf_op jit(solution)/shard_map/ppermute | solution.py:560
  255.7 10.9 %attend_back.2.refs_2_.refs_3_.project_grad = bf16[3,1024,256]{2,1,0:T(8,128)(2,1)S(1)} custom-call(s32[1,1024]{1,0:T(1,128)S(1)} %bitcast.107, bf16[3,1024,256]{2,1,0:T(8,128)(2,1)S(1)} %copy-done.25, bf16[1024,256]{1,0:T(8,128)(2,1)S(1)} %get-tuple-element.222.grads, f32[2,2,1024]{2,1,0:T(2,128)S(1)} %reshape.189.logsum, ...), custom_call_target="tpu_custom_call" | custom-call | tf_op jit(solution)/shard_map/attend_back/pallas_call | solution.py:312
  270.4 4.9 collective-permute-start.58
  280.3 4.8 collective-permute-done.58
  289.8 6.6 %collective-permute-done.56 = bf16[256,1024]{1,0:T(8,128)(2,1)S(1)} collective-permute-done((bf16[256,1024]{1,0:T(8,128)(2,1)S(1)}, bf16[256,1024]{1,0:T(8,128)(2,1)S(1)}, u32[]{:S(2)}, u32[]{:S(2)}) %collective-permute-start.56) | collective-permute-done | bytes 524320 | tf_op jit(solution)/shard_map/ppermute | solution.py:560
  296.4 11.3 %collective-permute-done.59 = bf16[256,1024]{1,0:T(8,128)(2,1)S(1)} collective-permute-done((bf16[256,1024]{1,0:T(8,128)(2,1)S(1)}, bf16[256,1024]{1,0:T(8,128)(2,1)S(1)}, u32[]{:S(2)}, u32[]{:S(2)}) %collective-permute-start.59) | collective-permute-done | bytes 524320 | tf_op jit(solution)/shard_map/ppermute | solution.py:560
  312.8 9.4 %weight_grads.7 = bf16[4,128,3072]{2,1,0:T(8,128)(2,1)} custom-call(s32[4]{0:T(128)S(1)} %add_subtract_fusion.blocks, bf16[1024,1024]{1,0:T(8,128)(2,1)S(1)} %copy-done.37, bf16[1024,1024]{1,0:T(8,128)(2,1)S(1)} %copy-done.40, bf16[1024,1024]{1,0:T(8,128)(2,1)S(1)} %copy-done.45, bf16[3,1024,256]{2,1,0:T(8,128)(2,1)S(1)} %attend_back.2.refs_2_.refs_3_.project_grad, ...), custom_call_target="tpu_custom_call" | custom-call | tf_op jit(solution)/shard_map/weight_grads/pallas_call | solution.py:402
  328.3 6.8 %collective-permute-done.61.refs_0_ = bf16[256,1024]{1,0:T(8,128)(2,1)} collective-permute-done((bf16[256,1024]{1,0:T(8,128)(2,1)}, bf16[256,1024]{1,0:T(8,128)(2,1)}, u32[]{:S(2)}, u32[]{:S(2)}) %collective-permute-start.61) | collective-permute-done | bytes 524320 | tf_op jit(solution)/shard_map/ppermute | solution.py:560
  336.4 4.8 collective-permute-start.49
  353.9 5.3 collective-permute-done.62.refs_1_
  361.4 11.2 %attend_back.3.refs_2_.refs_3_.project_grad = bf16[3,1024,256]{2,1,0:T(8,128)(2,1)S(1)} custom-call(s32[1,1024]{1,0:T(1,128)S(1)} %bitcast.108, bf16[3,1024,256]{2,1,0:T(8,128)(2,1)S(1)} %copy-done.23, bf16[1024,256]{1,0:T(8,128)(2,1)S(1)} %get-tuple-element.239.grads, f32[2,2,1024]{2,1,0:T(2,128)S(1)} %reshape.190.logsum, ...), custom_call_target="tpu_custom_call" | custom-call | tf_op jit(solution)/shard_map/attend_back/pallas_call | solution.py:312
  384.9 9.5 %weight_grads.5 = bf16[4,128,3072]{2,1,0:T(8,128)(2,1)} custom-call(s32[4]{0:T(128)S(1)} %add_subtract_fusion.blocks, bf16[1024,1024]{1,0:T(8,128)(2,1)S(1)} %copy-done.31, bf16[1024,1024]{1,0:T(8,128)(2,1)S(1)} %copy-done.34, bf16[1024,1024]{1,0:T(8,128)(2,1)S(1)} %get-tuple-element.248.upstream, ...), custom_call_target="tpu_custom_call" | custom-call | tf_op jit(solution)/shard_map/weight_grads/pallas_call | solution.py:402
  395.4 4.8 collective-permute-done.80
  405.5 20.0 %collective-permute-done.50 = bf16[256,1024]{1,0:T(8,128)(2,1)S(1)} collective-permute-done((bf16[256,1024]{1,0:T(8,128)(2,1)S(1)}, bf16[256,1024]{1,0:T(8,128)(2,1)S(1)}, u32[]{:S(2)}, u32[]{:S(2)}) %collective-permute-start.50) | collective-permute-done | bytes 524320 | tf_op jit(solution)/shard_map/ppermute | solution.py:560
  447.0 8.5 %weight_grads.6.kept = bf16[4,128,3072]{2,1,0:T(8,128)(2,1)S(1)} custom-call(s32[4]{0:T(128)S(1)} %fusion.36.blocks, bf16[1024,1024]{1,0:T(8,128)(2,1)S(1)} %copy-done.38, bf16[1024,1024]{1,0:T(8,128)(2,1)S(1)} %copy-done.41, bf16[1024,1024]{1,0:T(8,128)(2,1)S(1)} %copy-done.46, bf16[3,1024,256]{2,1,0:T(8,128)(2,1)S(1)} %copy-done.27, ...), custom_call_target="tpu_custom_call" | custom-call | tf_op jit(solution)/shard_map/weight_grads/pallas_call | solution.py:402
  455.6 4.9 fold.3
  462.2 8.6 %weight_grads.4.kept = bf16[4,128,3072]{2,1,0:T(8,128)(2,1)S(1)} custom-call(s32[4]{0:T(128)S(1)} %fusion.36.blocks, bf16[1024,1024]{1,0:T(8,128)(2,1)S(1)} %copy-done.32, bf16[1024,1024]{1,0:T(8,128)(2,1)S(1)} %copy-done.35, bf16[1024,1024]{1,0:T(8,128)(2,1)S(1)} %copy-done.48, bf16[3,1024,256]{2,1,0:T(8,128)(2,1)S(1)} %copy-done.29, ...), custom_call_target="tpu_custom_call" | custom-call | tf_op jit(solution)/shard_map/weight_grads/pallas_call | solution.py:402
  474.2 4.0 fold.2
  481.2 13.2 %collective-permute-done.70 = bf16[2,64,3072]{2,1,0:T(8,128)(2,1)S(1)} collective-permute-done((bf16[2,64,3072]{2,1,0:T(8,128)(2,1)S(1)}, bf16[2,64,3072]{2,1,0:T(8,128)(2,1)S(1)}, u32[]{:S(2)}, u32[]{:S(2)}) %collective-permute-start.70) | collective-permute-done | bytes 786464 | tf_op jit(solution)/shard_map/ppermute | solution.py:511
  498.7 6.6 %collective-permute-start.68 = (bf16[256,1024]{1,0:T(8,128)(2,1)S(1)}, bf16[256,1024]{1,0:T(8,128)(2,1)S(1)}, u32[]{:S(2)}, u32[]{:S(2)}) collective-permute-start(bf16[256,1024]{1,0:T(8,128)(2,1)S(1)} %get-tuple-element.310), channel_id=1, source_target_pairs={{0,16},{16,0},{1,17},{17,1},{2,18},{18,2},{3,19},{19,3},{4,20},{20... | collective-permute-start | bytes 1572872 | tf_op jit(solution)/shard_map/ppermute | solution.py:511
  506.8 4.5 collective-permute-done.76
  511.6 4.4 collective-permute-done.74
  516.0 8.4 %collective-permute-done.71 = bf16[64,3072]{1,0:T(8,128)(2,1)S(1)} collective-permute-done((bf16[64,3072]{1,0:T(8,128)(2,1)S(1)}, bf16[64,3072]{1,0:T(8,128)(2,1)S(1)}, u32[]{:S(2)}, u32[]{:S(2)}) %collective-permute-start.71) | collective-permute-done | bytes 393248 | tf_op jit(solution)/shard_map/ppermute | solution.py:511
  (508 shorter events, 259.7 us)
Async XLA Ops:
  18.4 28.4 %collective-permute-start.1 = (bf16[256,1024]{1,0:T(8,128)(2,1)}, bf16[256,1024]{1,0:T(8,128)(2,1)S(1)}, u32[]{:S(2)}, u32[]{:S(2)}) collective-permute-start(bf16[256,1024]{1,0:T(8,128)(2,1)} %get-tuple-element.313.refs_0_), channel_id=1, source_target_pairs={{0,8},{8,0},{4,12},{12,4},{1,9},{9,1},{5,13},{13,5},{2,10},{10,2},... | collective-permute-start | bytes 1572872 | tf_op jit(solution)/shard_map/ppermute | solution.py:560
  20.9 27.1 %collective-permute-start.11 = (bf16[64,3072]{1,0:T(8,128)(2,1)S(1)}, bf16[64,3072]{1,0:T(8,128)(2,1)S(1)}, u32[]{:S(2)}, u32[]{:S(2)}) collective-permute-start(bf16[64,3072]{1,0:T(8,128)(2,1)S(1)} %get-tuple-element.323.refs_1_), channel_id=1, source_target_pairs={{0,1},{1,0},{2,3},{3,2},{4,5},{5,4},{6,7},{7,6},{8,9},{9,8},{10,11... | collective-permute-start | bytes 1179656 | tf_op jit(solution)/shard_map/ppermute | solution.py:511
  22.2 26.9 %collective-permute-start.13 = (bf16[64,3072]{1,0:T(8,128)(2,1)S(1)}, bf16[64,3072]{1,0:T(8,128)(2,1)}, u32[]{:S(2)}, u32[]{:S(2)}) collective-permute-start(bf16[64,3072]{1,0:T(8,128)(2,1)S(1)} %get-tuple-element.323.refs_1_), channel_id=1, source_target_pairs={{0,2},{1,3},{2,0},{3,1},{4,6},{5,7},{6,4},{7,5},{8,10},{9,11},{10,... | collective-permute-start | bytes 1179656 | tf_op jit(solution)/shard_map/ppermute | solution.py:511
  66.5 29.6 %collective-permute-start.24 = (bf16[256,1024]{1,0:T(8,128)(2,1)}, bf16[256,1024]{1,0:T(8,128)(2,1)}, u32[]{:S(2)}, u32[]{:S(2)}) collective-permute-start(bf16[256,1024]{1,0:T(8,128)(2,1)} %get-tuple-element.313.refs_0_), channel_id=1, source_target_pairs={{0,4},{4,0},{8,12},{12,8},{1,5},{5,1},{9,13},{13,9},{2,6},{6,2},{1... | collective-permute-start | bytes 1572872 | tf_op jit(solution)/shard_map/ppermute | solution.py:560
  71.2 31.8 %collective-permute-start = (bf16[256,1024]{1,0:T(8,128)(2,1)}, bf16[256,1024]{1,0:T(8,128)(2,1)}, u32[]{:S(2)}, u32[]{:S(2)}) collective-permute-start(bf16[256,1024]{1,0:T(8,128)(2,1)} %get-tuple-element.313.refs_0_), channel_id=1, source_target_pairs={{4,8},{8,4},{5,9},{9,5},{6,10},{10,6},{7,11},{11,7},{20,24},{24,20... | collective-permute-start | bytes 1572872 | tf_op jit(solution)/shard_map/ppermute | solution.py:560
  79.4 35.9 %collective-permute-start.53 = (bf16[256,1024]{1,0:T(8,128)(2,1)}, bf16[256,1024]{1,0:T(8,128)(2,1)}, u32[]{:S(2)}, u32[]{:S(2)}) collective-permute-start(bf16[256,1024]{1,0:T(8,128)(2,1)} %dynamic-slice_bitcast_fusion.refs_0_), channel_id=1, source_target_pairs={{0,8},{8,0},{4,12},{12,4},{1,9},{9,1},{5,13},{13,5},{2,10},{10,2},... | collective-permute-start | bytes 1572872 | tf_op jit(solution)/shard_map/ppermute | solution.py:560
  133.2 35.0 %collective-permute-start.28 = (bf16[256,1024]{1,0:T(8,128)(2,1)S(1)}, bf16[256,1024]{1,0:T(8,128)(2,1)S(1)}, u32[]{:S(2)}, u32[]{:S(2)}) collective-permute-start(bf16[256,1024]{1,0:T(8,128)(2,1)S(1)} %add_convert_fusion.3), channel_id=1, source_target_pairs={{0,8},{8,0},{4,12},{12,4},{1,9},{9,1},{5,13},{13,5},{2,10},{10,2},... | collective-permute-start | bytes 1572872 | tf_op jit(solution)/shard_map/ppermute | solution.py:560
  134.9 37.5 %collective-permute-start.36 = (bf16[64,3072]{1,0:T(8,128)(2,1)S(1)}, bf16[64,3072]{1,0:T(8,128)(2,1)S(1)}, u32[]{:S(2)}, u32[]{:S(2)}) collective-permute-start(bf16[64,3072]{1,0:T(8,128)(2,1)S(1)} %collective-permute-done.32.refs_2_), channel_id=1, source_target_pairs={{0,2},{1,3},{2,0},{3,1},{4,6},{5,7},{6,4},{7,5},{8,10},{9,11},{10,... | collective-permute-start | bytes 1179656 | tf_op jit(solution)/shard_map/ppermute | solution.py:511
  135.1 37.3 %collective-permute-start.37 = (bf16[64,3072]{1,0:T(8,128)(2,1)S(1)}, bf16[64,3072]{1,0:T(8,128)(2,1)S(1)}, u32[]{:S(2)}, u32[]{:S(2)}) collective-permute-start(bf16[64,3072]{1,0:T(8,128)(2,1)S(1)} %collective-permute-done.35.refs_5_), channel_id=1, source_target_pairs={{0,1},{1,0},{2,3},{3,2},{4,5},{5,4},{6,7},{7,6},{8,9},{9,8},{10,11... | collective-permute-start | bytes 1179656 | tf_op jit(solution)/shard_map/ppermute | solution.py:511
  139.7 34.8 %collective-permute-start.40 = (bf16[64,3072]{1,0:T(8,128)(2,1)S(1)}, bf16[64,3072]{1,0:T(8,128)(2,1)S(1)}, u32[]{:S(2)}, u32[]{:S(2)}) collective-permute-start(bf16[64,3072]{1,0:T(8,128)(2,1)S(1)} %collective-permute-done.32.refs_2_), channel_id=1, source_target_pairs={{0,16},{16,0},{1,17},{17,1},{2,18},{18,2},{3,19},{19,3},{4,20},{20... | collective-permute-start | bytes 1179656 | tf_op jit(solution)/shard_map/ppermute | solution.py:511
  142.0 33.0 %collective-permute-start.41 = (bf16[64,3072]{1,0:T(8,128)(2,1)S(1)}, bf16[64,3072]{1,0:T(8,128)(2,1)S(1)}, u32[]{:S(2)}, u32[]{:S(2)}) collective-permute-start(bf16[64,3072]{1,0:T(8,128)(2,1)S(1)} %collective-permute-done.33.refs_3_), channel_id=1, source_target_pairs={{0,16},{16,0},{1,17},{17,1},{2,18},{18,2},{3,19},{19,3},{4,20},{20... | collective-permute-start | bytes 1179656 | tf_op jit(solution)/shard_map/ppermute | solution.py:511
  172.5 30.5 %collective-permute-start.46 = (bf16[256,1024]{1,0:T(8,128)(2,1)S(1)}, bf16[256,1024]{1,0:T(8,128)(2,1)S(1)}, u32[]{:S(2)}, u32[]{:S(2)}) collective-permute-start(bf16[256,1024]{1,0:T(8,128)(2,1)S(1)} %get-tuple-element.315.refs_0_), channel_id=1, source_target_pairs={{0,4},{4,0},{8,12},{12,8},{1,5},{5,1},{9,13},{13,9},{2,6},{6,2},{1... | collective-permute-start | bytes 1572872 | tf_op jit(solution)/shard_map/ppermute | solution.py:560
  175.1 26.3 %collective-permute-start.45 = (bf16[64,3072]{1,0:T(8,128)(2,1)S(1)}, bf16[64,3072]{1,0:T(8,128)(2,1)S(1)}, u32[]{:S(2)}, u32[]{:S(2)}) collective-permute-start(bf16[64,3072]{1,0:T(8,128)(2,1)S(1)} %collective-permute-done.37.refs_7_), channel_id=1, source_target_pairs={{0,16},{16,0},{1,17},{17,1},{2,18},{18,2},{3,19},{19,3},{4,20},{20... | collective-permute-start | bytes 1179656 | tf_op jit(solution)/shard_map/ppermute | solution.py:511
  176.4 39.4 %collective-permute-start.29 = (bf16[256,1024]{1,0:T(8,128)(2,1)S(1)}, bf16[256,1024]{1,0:T(8,128)(2,1)S(1)}, u32[]{:S(2)}, u32[]{:S(2)}) collective-permute-start(bf16[256,1024]{1,0:T(8,128)(2,1)S(1)} %get-tuple-element.315.refs_0_), channel_id=1, source_target_pairs={{4,8},{8,4},{5,9},{9,5},{6,10},{10,6},{7,11},{11,7},{20,24},{24,20... | collective-permute-start | bytes 1572872 | tf_op jit(solution)/shard_map/ppermute | solution.py:560
  199.2 41.6 %collective-permute-start.55 = (bf16[256,1024]{1,0:T(8,128)(2,1)}, bf16[256,1024]{1,0:T(8,128)(2,1)}, u32[]{:S(2)}, u32[]{:S(2)}) collective-permute-start(bf16[256,1024]{1,0:T(8,128)(2,1)} %dynamic-slice_bitcast_fusion.refs_0_), channel_id=1, source_target_pairs={{0,4},{4,0},{8,12},{12,8},{1,5},{5,1},{9,13},{13,9},{2,6},{6,2},{1... | collective-permute-start | bytes 1572872 | tf_op jit(solution)/shard_map/ppermute | solution.py:560
  201.3 52.0 %collective-permute-start.52 = (bf16[256,1024]{1,0:T(8,128)(2,1)}, bf16[256,1024]{1,0:T(8,128)(2,1)}, u32[]{:S(2)}, u32[]{:S(2)}) collective-permute-start(bf16[256,1024]{1,0:T(8,128)(2,1)} %dynamic-slice_bitcast_fusion.refs_0_), channel_id=1, source_target_pairs={{4,8},{8,4},{5,9},{9,5},{6,10},{10,6},{7,11},{11,7},{20,24},{24,20... | collective-permute-start | bytes 1572872 | tf_op jit(solution)/shard_map/ppermute | solution.py:560
  203.0 50.4 %collective-permute-start.54 = (bf16[256,1024]{1,0:T(8,128)(2,1)}, bf16[256,1024]{1,0:T(8,128)(2,1)}, u32[]{:S(2)}, u32[]{:S(2)}) collective-permute-start(bf16[256,1024]{1,0:T(8,128)(2,1)} %collective-permute-done.53.refs_0_), channel_id=1, source_target_pairs={{4,0},{8,12},{5,1},{9,13},{6,2},{10,14},{7,3},{11,15},{20,16},{24,... | collective-permute-start | bytes 1572872 | tf_op jit(solution)/shard_map/ppermute | solution.py:560
  309.6 25.4 %collective-permute-start.61 = (bf16[256,1024]{1,0:T(8,128)(2,1)}, bf16[256,1024]{1,0:T(8,128)(2,1)}, u32[]{:S(2)}, u32[]{:S(2)}) collective-permute-start(bf16[256,1024]{1,0:T(8,128)(2,1)} %fusion.17.refs_0_), channel_id=1, source_target_pairs={{0,8},{8,0},{4,12},{12,4},{1,9},{9,1},{5,13},{13,5},{2,10},{10,2},... | collective-permute-start | bytes 1572872 | tf_op jit(solution)/shard_map/ppermute | solution.py:560
  322.2 113.2 %collective-permute-start.72 = (bf16[4,128,3072]{2,1,0:T(8,128)(2,1)}, bf16[4,128,3072]{2,1,0:T(8,128)(2,1)}, u32[]{:S(2)}, u32[]{:S(2)}) collective-permute-start(bf16[4,128,3072]{2,1,0:T(8,128)(2,1)} %weight_grads.7), channel_id=1, source_target_pairs={{0,16},{16,0},{1,17},{17,1},{2,18},{18,2},{3,19},{19,3},{4,20},{20... | collective-permute-start | bytes 9437192 | tf_op jit(solution)/shard_map/ppermute | solution.py:511
  326.8 25.9 %collective-permute-start.60 = (bf16[256,1024]{1,0:T(8,128)(2,1)}, bf16[256,1024]{1,0:T(8,128)(2,1)}, u32[]{:S(2)}, u32[]{:S(2)}) collective-permute-start(bf16[256,1024]{1,0:T(8,128)(2,1)} %fusion.17.refs_0_), channel_id=1, source_target_pairs={{4,8},{8,4},{5,9},{9,5},{6,10},{10,6},{7,11},{11,7},{20,24},{24,20... | collective-permute-start | bytes 1572872 | tf_op jit(solution)/shard_map/ppermute | solution.py:560
  336.4 58.8 %collective-permute-start.49 = (bf16[256,1024]{1,0:T(8,128)(2,1)}, bf16[256,1024]{1,0:T(8,128)(2,1)S(1)}, u32[]{:S(2)}, u32[]{:S(2)}) collective-permute-start(bf16[256,1024]{1,0:T(8,128)(2,1)} %copy-done.103), channel_id=1, source_target_pairs={{0,4},{12,8},{1,5},{13,9},{2,6},{14,10},{3,7},{15,11},{16,20},{28,... | collective-permute-start | bytes 1572872 | tf_op jit(solution)/shard_map/ppermute | solution.py:560
  348.0 56.2 %collective-permute-start.48 = (bf16[256,1024]{1,0:T(8,128)(2,1)S(1)}, bf16[256,1024]{1,0:T(8,128)(2,1)S(1)}, u32[]{:S(2)}, u32[]{:S(2)}) collective-permute-start(bf16[256,1024]{1,0:T(8,128)(2,1)S(1)} %copy-done.104), channel_id=1, source_target_pairs={{4,8},{8,4},{5,9},{9,5},{6,10},{10,6},{7,11},{11,7},{20,24},{24,20... | collective-permute-start | bytes 1572872 | tf_op jit(solution)/shard_map/ppermute | solution.py:560
  352.7 47.6 %collective-permute-start.47 = (bf16[256,1024]{1,0:T(8,128)(2,1)S(1)}, bf16[256,1024]{1,0:T(8,128)(2,1)S(1)}, u32[]{:S(2)}, u32[]{:S(2)}) collective-permute-start(bf16[256,1024]{1,0:T(8,128)(2,1)S(1)} %copy-done.106), channel_id=1, source_target_pairs={{0,4},{4,0},{8,12},{12,8},{1,5},{5,1},{9,13},{13,9},{2,6},{6,2},{1... | collective-permute-start | bytes 1572872 | tf_op jit(solution)/shard_map/ppermute | solution.py:560
  394.5 79.7 %collective-permute-start.69 = (bf16[4,128,3072]{2,1,0:T(8,128)(2,1)}, bf16[4,128,3072]{2,1,0:T(8,128)(2,1)}, u32[]{:S(2)}, u32[]{:S(2)}) collective-permute-start(bf16[4,128,3072]{2,1,0:T(8,128)(2,1)} %weight_grads.5), channel_id=1, source_target_pairs={{0,16},{16,0},{1,17},{17,1},{2,18},{18,2},{3,19},{19,3},{4,20},{20... | collective-permute-start | bytes 9437192 | tf_op jit(solution)/shard_map/ppermute | solution.py:511
  400.3 29.9 %collective-permute-start.66 = (bf16[256,1024]{1,0:T(8,128)(2,1)}, bf16[256,1024]{1,0:T(8,128)(2,1)S(1)}, u32[]{:S(2)}, u32[]{:S(2)}) collective-permute-start(bf16[256,1024]{1,0:T(8,128)(2,1)} %get-tuple-element.244), channel_id=1, source_target_pairs={{0,4},{12,8},{1,5},{13,9},{2,6},{14,10},{3,7},{15,11},{16,20},{28,... | collective-permute-start | bytes 1572872 | tf_op jit(solution)/shard_map/ppermute | solution.py:560
  430.2 31.7 %collective-permute-start.64 = (bf16[256,1024]{1,0:T(8,128)(2,1)}, bf16[256,1024]{1,0:T(8,128)(2,1)}, u32[]{:S(2)}, u32[]{:S(2)}) collective-permute-start(bf16[256,1024]{1,0:T(8,128)(2,1)} %get-tuple-element.243), channel_id=1, source_target_pairs={{0,4},{4,0},{8,12},{12,8},{1,5},{5,1},{9,13},{13,9},{2,6},{6,2},{1... | collective-permute-start | bytes 1572872 | tf_op jit(solution)/shard_map/ppermute | solution.py:560
  430.2 40.6 %collective-permute-start.65 = (bf16[256,1024]{1,0:T(8,128)(2,1)}, bf16[256,1024]{1,0:T(8,128)(2,1)}, u32[]{:S(2)}, u32[]{:S(2)}) collective-permute-start(bf16[256,1024]{1,0:T(8,128)(2,1)} %get-tuple-element.244), channel_id=1, source_target_pairs={{4,8},{8,4},{5,9},{9,5},{6,10},{10,6},{7,11},{11,7},{20,24},{24,20... | collective-permute-start | bytes 1572872 | tf_op jit(solution)/shard_map/ppermute | solution.py:560
  432.7 27.8 %collective-permute-start.83 = (f32[2,4,1024]{2,1,0:T(4,128)S(1)}, f32[2,4,1024]{2,1,0:T(4,128)S(1)}, u32[]{:S(2)}, u32[]{:S(2)}) collective-permute-start(f32[2,4,1024]{2,1,0:T(4,128)S(1)} %add.322), channel_id=1, source_target_pairs={{0,4},{4,0},{8,12},{12,8},{1,5},{5,1},{9,13},{13,9},{2,6},{6,2},{1... | collective-permute-start | bytes 98312 | tf_op jit(solution)/shard_map/ppermute | solution.py:511
  435.4 36.8 %collective-permute-start.67 = (bf16[256,1024]{1,0:T(8,128)(2,1)}, bf16[256,1024]{1,0:T(8,128)(2,1)}, u32[]{:S(2)}, u32[]{:S(2)}) collective-permute-start(bf16[256,1024]{1,0:T(8,128)(2,1)} %add_convert_fusion), channel_id=1, source_target_pairs={{0,8},{8,0},{4,12},{12,4},{1,9},{9,1},{5,13},{13,5},{2,10},{10,2},... | collective-permute-start | bytes 1572872 | tf_op jit(solution)/shard_map/ppermute | solution.py:560
  470.8 56.0 %collective-permute-start.84 = (f32[2,4,1024]{2,1,0:T(4,128)S(1)}, f32[2,4,1024]{2,1,0:T(4,128)S(1)}, u32[]{:S(2)}, u32[]{:S(2)}) collective-permute-start(f32[2,4,1024]{2,1,0:T(4,128)S(1)} %add.323), channel_id=1, source_target_pairs={{0,8},{4,12},{8,0},{12,4},{1,9},{5,13},{9,1},{13,5},{2,10},{6,14},... | collective-permute-start | bytes 98312 | tf_op jit(solution)/shard_map/ppermute | solution.py:511
  479.9 26.3 %collective-permute-start.78 = (bf16[64,3072]{1,0:T(8,128)(2,1)S(1)}, bf16[64,3072]{1,0:T(8,128)(2,1)S(1)}, u32[]{:S(2)}, u32[]{:S(2)}) collective-permute-start(bf16[64,3072]{1,0:T(8,128)(2,1)S(1)} %get-tuple-element.326), channel_id=1, source_target_pairs={{0,1},{1,0},{2,3},{3,2},{4,5},{5,4},{6,7},{7,6},{8,9},{9,8},{10,11... | collective-permute-start | bytes 1179656 | tf_op jit(solution)/shard_map/ppermute | solution.py:511
  498.7 28.7 %collective-permute-start.68 = (bf16[256,1024]{1,0:T(8,128)(2,1)S(1)}, bf16[256,1024]{1,0:T(8,128)(2,1)S(1)}, u32[]{:S(2)}, u32[]{:S(2)}) collective-permute-start(bf16[256,1024]{1,0:T(8,128)(2,1)S(1)} %get-tuple-element.310), channel_id=1, source_target_pairs={{0,16},{16,0},{1,17},{17,1},{2,18},{18,2},{3,19},{19,3},{4,20},{20... | collective-permute-start | bytes 1572872 | tf_op jit(solution)/shard_map/ppermute | solution.py:511
  (181 other events, 2099.4 us)

commit v3 on v2

--- a/solution.py
+++ b/solution.py
@@ -83,8 +83,11 @@
     return pltpu.CompilerParams(vmem_limit_bytes=mib << 20)
 
 
-def chunk_call(body, name, index, outs, inputs, kept=()):
+def chunk_call(body, name, index, outs, inputs, kept=(), place=None):
     given = len(inputs)
+    number = index.reshape(1).astype(jnp.int32)
+    if place is not None:
+        number = jnp.concatenate([number, place])
 
     def kernel(number, *refs):
         body(number, *refs[:given], *refs[given + len(kept) :])
@@ -103,7 +106,7 @@
         input_output_aliases={1 + given + i: i for i in range(len(kept))},
         compiler_params=params(),
         name=name,
-    )(index.reshape(1).astype(jnp.int32), *[array for array, _, _ in inputs], *kept)
+    )(number, *[array for array, _, _ in inputs], *kept)
 
 
 HERE = lambda i: (0, 0)
@@ -118,13 +121,22 @@
     return whole
 
 
+def keep_by_owner(kept, place, values):
+    blocks = values.shape[1] // 128
+    for block in range(blocks):
+        at = (place[0] ^ (block % 2)) * (blocks // 2) + (place[1] ^ (block // 2))
+        lanes = pl.ds(pl.multiple_of(at * 128, 128), 128)
+        kept[:, lanes] = values[:, block * 128 : (block + 1) * 128]
+
+
 def project_body(ways, number, *refs):
     norms, wqkv, wup, cosine, sine, attn_in, feed_in, qkv, value_t, active, slope = refs[ways:]
     normed, _ = normalize(added(refs[:ways]))
     attn = (normed * norms[0:1] + norms[1:2]).astype(BF16)
     feed = (normed * norms[2:3] + norms[3:4]).astype(BF16)
-    attn_in[...] = attn
-    feed_in[...] = feed
+    place = (number[1], number[2])
+    keep_by_owner(attn_in, place, attn)
+    keep_by_owner(feed_in, place, feed)
     width = qkv.shape[2]
     for part in range(3):
         piece = mm(attn, wqkv[:, part * width : (part + 1) * width])
@@ -144,7 +156,7 @@
         slope[:, lanes] = der.astype(BF16)
 
 
-def project(chunk, index, tokens, norms, pack, tables, width, hidden, kept):
+def project(chunk, index, place, tokens, norms, pack, tables, width, hidden, kept):
     model = pack.shape[0]
     return chunk_call(
         partial(project_body, len(chunk)),
@@ -167,6 +179,7 @@
             (tables[1], (TOKENS, 128), ROWS),
         ],
         kept,
+        place,
     )
 
 
@@ -237,12 +250,12 @@
 def through_branch_body(ways, number, *refs):
     wout, wdown, slope, pre_grad, context_grad, copied = refs[ways:]
     grads = added(refs[:ways])
-    copied[...] = grads
+    keep_by_owner(copied, (number[1], number[2]), grads)
     pre_grad[...] = (mm(grads, wdown[...]) * slope[...].astype(F32)).astype(BF16)
     context_grad[...] = mm(grads, wout[...]).astype(BF16)
 
 
-def through_branch(chunk, index, pack, slope, width, kept):
+def through_branch(chunk, index, place, pack, slope, width, kept):
     tokens, hidden = slope.shape
     model = pack.shape[0]
     return chunk_call(
@@ -261,6 +274,7 @@
             (slope, (TOKENS, hidden), ROWS),
         ],
         kept,
+        place,
     )
 
 
@@ -366,59 +380,53 @@
     )
 
 
-def outer_kernel(blocks, attn_in, feed_in, upstream, project_grad, context, pre_grad, active, out):
+def outer_kernel(attn_in, feed_in, upstream, project_grad, context, pre_grad, active, out):
     step = pl.program_id(0)
 
-    def fill(left, right):
-        for number in range(4):
-            lanes = pl.ds(pl.multiple_of(blocks[number] * 128, 128), 128)
-            out[number] = lax.dot_general(
-                left[:, lanes], right, (((0,), (0,)), ((), ())), preferred_element_type=F32
-            ).astype(BF16)
-
-    @pl.when(step < 3)
+    def fill(left, right, start=0):
+        width = right.shape[1]
+        out[:, :, start : start + width] = (
+            lax.dot_general(left[...], right, (((0,), (0,)), ((), ())), preferred_element_type=F32)
+            .astype(BF16)
+            .reshape(*out.shape[:2], width)
+        )
+
+    @pl.when(step == 0)
     def _():
         fill(attn_in, project_grad[0])
-
-    @pl.when(step == 3)
+        fill(attn_in, project_grad[1], context.shape[1])
+
+    @pl.when(step == 1)
     def _():
-        fill(upstream, context[...])
-
-    @pl.when((step >= 4) & (step < 8))
-    def _():
-        fill(feed_in, pre_grad[...])
-
-    @pl.when(step >= 8)
-    def _():
-        fill(upstream, active[...])
-
-
-def weight_grads(blocks, saved, upstream, pre_grad, project_grad):
+        fill(attn_in, project_grad[2])
+        fill(upstream, context[...], context.shape[1])
+
+    pl.when((step == 2) | (step == 3))(lambda: fill(feed_in, pre_grad[...]))
+    pl.when(step >= 4)(lambda: fill(upstream, active[...]))
+
+
+def weight_grads(half, saved, upstream, pre_grad, project_grad):
     attn_in, feed_in, active, context = saved
     tokens, model = attn_in.shape
     width = context.shape[1]
-    steps = 4 + 2 * active.shape[1] // width
-    whole = pl.BlockSpec((tokens, model), lambda j, blocks: (0, 0))
+    left = pl.BlockSpec((tokens, model // 2), lambda j: (0, half))
     return pl.pallas_call(
         outer_kernel,
-        grid_spec=pltpu.PrefetchScalarGridSpec(
-            num_scalar_prefetch=1,
-            grid=(steps,),
-            in_specs=[
-                whole,
-                whole,
-                whole,
-                pl.BlockSpec((1, tokens, width), lambda j, blocks: (jnp.minimum(j, 2), 0, 0)),
-                pl.BlockSpec((tokens, width), lambda j, blocks: (0, 0)),
-                pl.BlockSpec((tokens, width), lambda j, blocks: (0, jnp.clip(j - 4, 0, 3))),
-                pl.BlockSpec((tokens, width), lambda j, blocks: (0, jnp.clip(j - 8, 0, 3))),
-            ],
-            out_specs=pl.BlockSpec((4, model // 8, width), lambda j, blocks: (0, 0, j)),
-        ),
-        out_shape=jax.ShapeDtypeStruct((4, model // 8, steps * width), BF16),
-        compiler_params=params(32),
+        grid=(6,),
+        in_specs=[
+            left,
+            left,
+            left,
+            pl.BlockSpec((3, tokens, width), lambda j: (0, 0, 0)),
+            pl.BlockSpec((tokens, width), lambda j: (0, 0)),
+            pl.BlockSpec((tokens, 2 * width), lambda j: (0, jnp.clip(j - 2, 0, 1))),
+            pl.BlockSpec((tokens, 2 * width), lambda j: (0, jnp.clip(j - 4, 0, 1))),
+        ],
+        out_specs=pl.BlockSpec((4, model // 8, 2 * width), lambda j: (0, 0, j)),
+        out_shape=jax.ShapeDtypeStruct((4, model // 8, 12 * width), BF16),
+        compiler_params=params(58),
         name="weight_grads",
-    )(blocks.astype(jnp.int32), attn_in, feed_in, upstream, project_grad, context, pre_grad, active)
+    )(attn_in, feed_in, upstream, project_grad, context, pre_grad, active)
 
 
 def fold_kernel(kept, came, side, ahead, rest):
@@ -453,10 +461,12 @@
 def assemble_kernel(place, *refs):
     pieces, whole = (refs[:-1], refs[-1])
     rows = pieces[0].shape[0]
+    each = len(pieces) // 2
     for order, piece in enumerate(pieces):
-        core, number, part = (order // 8, (order % 8) // 2, order % 2)
-        at = ((place[1] ^ number) * 2 + (place[0] ^ core)) * (2 * rows) + part * rows
-        whole[pl.ds(pl.multiple_of(at, rows), rows), :] = piece[...]
+        core, number = (order // each, min(order % each, 3))
+        at = ((place[1] ^ number) * 2 + (place[0] ^ core)) * rows
+        at = at + (rows // 2 if order % each == 4 else 0)
+        whole[pl.ds(pl.multiple_of(at, rows // 2), piece.shape[0]), :] = piece[...]
 
 
 def assemble(place, pieces):
@@ -467,13 +477,13 @@
         grid_spec=pltpu.PrefetchScalarGridSpec(
             num_scalar_prefetch=1,
             grid=(6,),
-            in_specs=[pl.BlockSpec((rows, step), lambda j, place: (0, j)) for _ in pieces],
-            out_specs=pl.BlockSpec((len(pieces) * rows, step), lambda j, place: (0, j)),
+            in_specs=[pl.BlockSpec((piece.shape[0], step), lambda j, place: (0, j)) for piece in pieces],
+            out_specs=pl.BlockSpec((8 * rows, step), lambda j, place: (0, j)),
         ),
-        out_shape=jax.ShapeDtypeStruct((len(pieces) * rows, width), BF16),
-        compiler_params=params(),
+        out_shape=jax.ShapeDtypeStruct((8 * rows, width), BF16),
+        compiler_params=params(58),
         name="assemble",
-    )(place.astype(jnp.int32), *pieces)
+    )(place, *pieces)
 
 
 def unpack_kernel(place, upper, lower, came, qkv, out, up, down):
@@ -511,49 +521,31 @@
     return lax.ppermute(block, axis, [(i, i ^ bit) for i in range(lax.axis_size(axis))])
 
 
-def after(values, *earlier):
+def join(*values):
     flat, tree = jax.tree.flatten(values)
-    held = lax.optimization_barrier((*flat, *earlier))
-    return jax.tree.unflatten(tree, held[: len(flat)])
-
-
-def total_of(value):
-    for axis in ("section", "col", "row"):
-        bit = 1
-        while bit < lax.axis_size(axis):
-            value = value + swap(value, axis, bit)
-            bit *= 2
-    return value
+    return jax.tree.unflatten(tree, lax.optimization_barrier(tuple(flat)))
+
+
+def sum_over(value, axis):
+    others = [swap(value, axis, bit) for bit in range(1, lax.axis_size(axis))]
+    return sum(others, start=value)
 
 
 def pick(stack, index):
     return lax.dynamic_index_in_dim(stack, index, 0, keepdims=False)
 
 
-def spread_layer(parts, meanwhile):
-    upper, lower = parts
-    side = [swap(part, "col", 1) for part in parts]
-    ahead = [swap(part, "col", 2) for part in parts]
-    if meanwhile is not None:
-        side, ahead = after((side, ahead), meanwhile)
-    across = [swap(side[0], "col", 2), swap(ahead[1], "col", 1)]
-    mine = [*parts, *side, *ahead, *across]
-    theirs = [swap(piece, "section", 1) for piece in mine]
-    return (mine + theirs, across)
-
-
-def sum_layer(sec, col, saved, upstream, pre_grad, project_grad):
-    order = col ^ jnp.arange(4, dtype=jnp.int32)
-    leaving = weight_grads(order * 2 + 1 - sec, saved, upstream, pre_grad, project_grad)
-    came = swap(leaving, "section", 1)
-    kept = weight_grads(order * 2 + sec, saved, upstream, pre_grad, project_grad)
-    side, ahead, rest = fold(kept, came)
-    first = swap(side, "col", 1)
-    second = swap(ahead, "col", 2)
-    add = lambda a, b: a.astype(F32) + b.astype(F32)
-    upper = swap(add(rest[1], first[1]).astype(BF16), "col", 2)
-    lower = swap(add(rest[3], second[1]).astype(BF16), "col", 1)
-    return (add(add(rest[0], first[0]), upper), add(add(rest[2], second[0]), lower))
+def send_sides(half):
+    return (swap(half, "col", 1), swap(half, "col", 2))
+
+
+def send_corner(side, ahead):
+    rows = side.shape[0] // 2
+    return [swap(side[:rows], "col", 2), swap(ahead[rows:], "col", 1)]
+
+
+def add(a, b):
+    return a.astype(F32) + b.astype(F32)
 
 
 def along_row(block, pairs):
@@ -567,23 +559,20 @@
 INWARD = [(0, 1), (3, 2)]
 
 
-def gather_tokens(own):
-    far = along_row(own, TWO_OVER)
-    near = along_row(own, ONE_OVER)
-    middle = along_row(own, MIDDLE)
-    passed = along_row(far, OUTWARD)
-    return [(own,), (near,), (far,), (middle, passed)]
-
-
-def scatter_tokens(chunk_of):
-    last = chunk_of(3)
-    passed = along_row(last, INWARD)
-    middle = along_row(last, MIDDLE)
-    far = chunk_of(2)
-    near = along_row(chunk_of(1), ONE_OVER)
-    far = along_row((far.astype(F32) + passed.astype(F32)).astype(BF16), TWO_OVER)
-    own = chunk_of(0)
-    return (own.astype(F32) + near.astype(F32)) + (middle.astype(F32) + far.astype(F32))
+def send_own(own):
+    return (along_row(own, TWO_OVER), along_row(own, ONE_OVER))
+
+
+def pass_on(own, far):
+    return (along_row(far, OUTWARD), along_row(own, MIDDLE))
+
+
+def send_last(share):
+    return (along_row(share, INWARD), along_row(share, MIDDLE))
+
+
+def send_sums(far, passed, near):
+    return (along_row(add(far, passed).astype(BF16), TWO_OVER), along_row(near, ONE_OVER))
 
 
 def fast_shards(
@@ -611,6 +600,51 @@
     docs = pick(doc_ids[:, 0], sec)
     given = pick(out_cotangent[:, 0], sec)
 
+    place = jnp.stack([sec, col]).astype(jnp.int32)
+    share = attn_gain.shape[1]
+
+    def enter(kept, chunk, number, layer):
+        return project(
+            chunk,
+            row ^ number,
+            place,
+            tokens,
+            norms[layer],
+            packs[layer],
+            tables,
+            width,
+            hidden,
+            kept,
+        )
+
+    def leave(kept, entered, number, layer):
+        _, _, qkv, value_t, active, _ = entered
+        *kept, share_of = attend(row ^ number, starts, qkv, value_t, active, packs[layer], kept)
+        return (tuple(kept), share_of)
+
+    def back_branch(kept, chunk, number, slope, layer):
+        return through_branch(chunk, row ^ number, place, packs[layer], slope, width, kept)
+
+    def back_inputs(chunks, number, layer, project_grad, pre_grad):
+        return through_inputs(
+            chunks[number], row ^ number, norms[layer], project_grad, pre_grad, packs[layer]
+        )
+
+    def input_grad(total, own, own_grads):
+        normed, scale = normalize(own)
+        result = own_grads.astype(F32) + scale * (
+            total
+            - jnp.mean(total, axis=-1, keepdims=True)
+            - normed * jnp.mean(total * normed, axis=-1, keepdims=True)
+        )
+        return result.astype(BF16)
+
+
+    vectors = jnp.stack([attn_gain[0], attn_shift[0], mlp_gain[0], mlp_shift[0]])
+    norms = lax.dynamic_update_slice(
+        jnp.zeros((2, 4, model), F32), vectors[None], (sec, 0, (row * cols + col) * share)
+    )
+    norms = sum_over(norms, "row")
     own_pack = jnp.concatenate(
         [
             qkv_weight[0].reshape(block, 3 * width),
@@ -620,86 +654,182 @@
         ],
         axis=1,
     )
-    quarter = block // 4
-    part_of = lambda core, part: lax.dynamic_slice_in_dim(
-        own_pack, core * (block // 2) + part * quarter, quarter
-    )
-    own_parts = [part_of(sec, part) for part in range(2)]
-    other_parts = [swap(part_of(1 - sec, part), "section", 1) for part in range(2)]
-    parts0 = [jnp.where(first, a, b) for a, b in zip(own_parts, other_parts)]
-    parts1 = [jnp.where(first, b, a) for a, b in zip(own_parts, other_parts)]
-    share = attn_gain.shape[1]
-    vectors = jnp.stack([attn_gain[0], attn_shift[0], mlp_gain[0], mlp_shift[0]])
-    norms = total_of(
-        lax.dynamic_update_slice(
-            jnp.zeros((2, 4, model), F32), vectors[None], (sec, 0, (row * cols + col) * share)
-        )
-    )
-    chunks_x0 = gather_tokens(x_own)
-    pieces0, across0 = spread_layer(parts0, norms)
-    pieces1, _ = spread_layer(after(parts1, *across0), None)
-    place = jnp.stack([sec, col])
-    packs = [assemble(place, pieces0), assemble(place, pieces1)]
-
+    half_of = lambda core: lax.dynamic_slice_in_dim(own_pack, core * (block // 2), block // 2)
+    staying, leaving = (half_of(sec), half_of(1 - sec))
+    norms, staying, leaving = join(norms, staying, leaving)
+
+    came = swap(leaving, "section", 1)
+    norms = sum_over(norms, "section")
+    half0, half1 = (jnp.where(first, staying, came), jnp.where(first, came, staying))
+    norms, half0, half1 = join(norms, half0, half1)
+
+    norms = sum_over(norms, "col")
+    side0, ahead0 = send_sides(half0)
+    far_x0, near_x0 = send_own(x_own)
     starts = jnp.sum((docs[None, :] < docs[:, None]).astype(jnp.int32), axis=1)
     tables = rope_tables(docs, starts)
     starts = starts[None]
-
-    def forward(chunks, own, layer):
-        kept = ()
-        for number, chunk in enumerate(chunks):
-            kept = project(
-                chunk, row ^ number, tokens, norms[layer], packs[layer], tables, width, hidden, kept
-            )
-        attn_in, feed_in, qkv, value_t, active, slope = kept
-        results = []
-
-        def chunk_of(number):
-            *now, share_of = attend(
-                row ^ number, starts, qkv, value_t, active, packs[layer], tuple(results)
-            )
-            results[:] = now
-            return share_of
-
-        result = own.astype(F32) + scatter_tokens(chunk_of)
-        context, logsum = results
-        return (result.astype(BF16), (attn_in, feed_in, active, context), (qkv, slope, logsum))
-
-    def backward(chunks, own, layer, saved, held, chunks_grads, own_grads):
-        qkv, slope, logsum = held
-        kept = ()
-        for number, chunk in enumerate(chunks_grads):
-            kept = through_branch(chunk, row ^ number, packs[layer], slope, width, kept)
-        pre_grad, context_grad, grads = kept
-        project_grad = attend_back(starts, qkv, context_grad, logsum, tables)
-        terms, pieces = ([], [])
-
-        def chunk_of(number):
-            piece, term = through_inputs(
-                chunks[number], row ^ number, norms[layer], project_grad, pre_grad, packs[layer]
-            )
-            terms.append(term)
-            pieces.append(piece)
-            return piece
-
-        total = scatter_tokens(chunk_of)
-        normed, scale = normalize(own)
-        result = own_grads.astype(F32) + scale * (
-            total
-            - jnp.mean(total, axis=-1, keepdims=True)
-            - normed * jnp.mean(total * normed, axis=-1, keepdims=True)
-        )
-        pre_grad, project_grad = after((pre_grad, project_grad), *pieces)
-        sums = sum_layer(sec, col, saved, grads, pre_grad, project_grad)
-        return (result.astype(BF16), sums, sum(terms))
-
-    y0_own, saved0, held0 = forward(chunks_x0, x_own, 0)
-    chunks_x1 = gather_tokens(y0_own)
-    chunks_g1 = gather_tokens(after(given, chunks_x0[3][1]))
-    y1_own, saved1, held1 = forward(chunks_x1, y0_own, 1)
-    dx1_own, sums1, terms1 = backward(chunks_x1, y0_own, 1, saved1, held1, chunks_g1, given)
-    chunks_g0 = gather_tokens(dx1_own)
-    dx0_own, sums0, terms0 = backward(chunks_x0, x_own, 0, saved0, held0, chunks_g0, dx1_own)
+    norms, half0, side0, ahead0, starts, tables = join(
+        norms, half0, side0, ahead0, starts, tables
+    )
+
+    across0 = send_corner(side0, ahead0)
+    mine = [half0, side0, ahead0]
+    theirs = [swap(piece, "section", 1) for piece in mine]
+    mine, theirs, across0, far_x0, near_x0 = join(mine, theirs, across0, far_x0, near_x0)
+
+    passed_x0, middle_x0 = pass_on(x_own, far_x0)
+    theirs = theirs + [swap(piece, "section", 1) for piece in across0]
+    packs = [assemble(place, mine + across0 + theirs), None]
+    chunks_x0 = [(x_own,), (near_x0,), (far_x0,), (middle_x0, passed_x0)]
+    packs, given, half1, chunks_x0 = join(packs, given, half1, chunks_x0)
+
+    side1, ahead1 = send_sides(half1)
+    far_g1, near_g1 = send_own(given)
+    entered0 = ()
+    for number in range(4):
+        entered0 = enter(entered0, chunks_x0[number], number, 0)
+    kept, last = leave((), entered0, 3, 0)
+    half1, side1, ahead1, far_g1, near_g1, entered0, kept, last = join(
+        half1, side1, ahead1, far_g1, near_g1, entered0, kept, last
+    )
+
+    passed_y0, middle_y0 = send_last(last)
+    kept, far = leave(kept, entered0, 2, 0)
+    kept, near = leave(kept, entered0, 1, 0)
+    (context0, logsum0), share_of = leave(kept, entered0, 0, 0)
+    passed_y0, middle_y0, far, near, share_of, context0, half1, side1, ahead1 = join(
+        passed_y0, middle_y0, far, near, share_of, context0, half1, side1, ahead1
+    )
+
+    far_y0, near_y0 = send_sums(far, passed_y0, near)
+    across1 = send_corner(side1, ahead1)
+    mine = [half1, side1, ahead1] + across1
+    theirs = [swap(piece, "section", 1) for piece in mine]
+    far_y0, near_y0, mine, theirs, far_g1 = join(far_y0, near_y0, mine, theirs, far_g1)
+    total = add(share_of, near_y0) + add(middle_y0, far_y0)
+    y0_own = (x_own.astype(F32) + total).astype(BF16)
+
+    far_x1, near_x1 = send_own(y0_own)
+    packs[1] = assemble(place, mine + theirs)
+    entered1 = enter((), (y0_own,), 0, 1)
+    branch1 = back_branch((), (given,), 0, entered1[5], 1)
+    far_x1, near_x1, entered1, branch1 = join(far_x1, near_x1, entered1, branch1)
+
+    passed_x1, middle_x1 = pass_on(y0_own, far_x1)
+    entered1 = enter(entered1, (near_x1,), 1, 1)
+    branch1 = back_branch(branch1, (near_g1,), 1, entered1[5], 1)
+    entered1 = enter(entered1, (far_x1,), 2, 1)
+    branch1 = back_branch(branch1, (far_g1,), 2, entered1[5], 1)
+    passed_x1, middle_x1, entered1, branch1, far_g1 = join(
+        passed_x1, middle_x1, entered1, branch1, far_g1
+    )
+
+    chunks_x1 = [(y0_own,), (near_x1,), (far_x1,), (middle_x1, passed_x1)]
+    entered1 = enter(entered1, chunks_x1[3], 3, 1)
+    passed_g1, middle_g1 = pass_on(given, far_g1)
+    kept, last_b1 = leave((), entered1, 3, 1)
+    kept, far_b1 = leave(kept, entered1, 2, 1)
+    kept, near_b1 = leave(kept, entered1, 1, 1)
+    (context1, logsum1), share_b1 = leave(kept, entered1, 0, 1)
+    passed_g1, middle_g1, last_b1, far_b1, near_b1, share_b1, context1, entered1 = join(
+        passed_g1, middle_g1, last_b1, far_b1, near_b1, share_b1, context1, entered1
+    )
+
+    passed_y1, middle_y1 = send_last(last_b1)
+    pre_grad1, context_grad1, grads1 = back_branch(
+        branch1, (middle_g1, passed_g1), 3, entered1[5], 1
+    )
+    saved1 = (entered1[0], entered1[1], entered1[4], context1)
+    project_grad1 = attend_back(starts, entered1[2], context_grad1, logsum1, tables)
+    passed_y1, middle_y1, pre_grad1, project_grad1 = join(
+        passed_y1, middle_y1, pre_grad1, project_grad1
+    )
+
+    last, terms1 = back_inputs(chunks_x1, 3, 1, project_grad1, pre_grad1)
+    last, terms1, project_grad1 = join(last, terms1, project_grad1)
+
+    passed_n1, middle_n1 = send_last(last)
+    others = [back_inputs(chunks_x1, number, 1, project_grad1, pre_grad1) for number in (2, 1, 0)]
+    (far, near, share_of), terms = zip(*others)
+    terms1 = sum(terms, start=terms1)
+    passed_n1, middle_n1, far, near, share_of, terms1, project_grad1 = join(
+        passed_n1, middle_n1, far, near, share_of, terms1, project_grad1
+    )
+
+    far_n1, near_n1 = send_sums(far, passed_n1, near)
+    leaving1 = weight_grads(1, saved1, grads1, pre_grad1, project_grad1)
+    kept1 = weight_grads(0, saved1, grads1, pre_grad1, project_grad1)
+    far_n1, near_n1, leaving1, kept1 = join(far_n1, near_n1, leaving1, kept1)
+    total = add(share_of, near_n1) + add(middle_n1, far_n1)
+    dx1_own = input_grad(total, y0_own, given)
+
+    slope0 = entered0[5]
+    far_g0, near_g0 = send_own(dx1_own)
+    came1 = swap(leaving1, "section", 1)
+    branch0 = back_branch((), (dx1_own,), 0, slope0, 0)
+    far_g0, near_g0, came1, branch0 = join(far_g0, near_g0, came1, branch0)
+
+    passed_g0, middle_g0 = pass_on(dx1_own, far_g0)
+    side1, ahead1, rest1 = fold(kept1, came1)
+    branch0 = back_branch(branch0, (near_g0,), 1, slope0, 0)
+    branch0 = back_branch(branch0, (far_g0,), 2, slope0, 0)
+    passed_g0, middle_g0, branch0, side1, ahead1, rest1, far_b1, near_b1 = join(
+        passed_g0, middle_g0, branch0, side1, ahead1, rest1, far_b1, near_b1
+    )
+
+    first1, second1 = (swap(side1, "col", 1), swap(ahead1, "col", 2))
+    far_y1, near_y1 = send_sums(far_b1, passed_y1, near_b1)
+    pre_grad0, context_grad0, grads0 = back_branch(branch0, (middle_g0, passed_g0), 3, slope0, 0)
+    saved0 = (entered0[0], entered0[1], entered0[4], context0)
+    project_grad0 = attend_back(starts, entered0[2], context_grad0, logsum0, tables)
+    last, terms0 = back_inputs(chunks_x0, 3, 0, project_grad0, pre_grad0)
+    first1, second1, far_y1, near_y1, last, terms0, project_grad0 = join(
+        first1, second1, far_y1, near_y1, last, terms0, project_grad0
+    )
+
+    passed_n0, middle_n0 = send_last(last)
+    passed1 = (
+        swap(add(rest1[1], first1[1]).astype(BF16), "col", 2),
+        swap(add(rest1[3], second1[1]).astype(BF16), "col", 1),
+    )
+    sums1 = (
+        add(add(rest1[0], first1[0]), passed1[0]),
+        add(add(rest1[2], second1[0]), passed1[1]),
+    )
+    others = [back_inputs(chunks_x0, number, 0, project_grad0, pre_grad0) for number in (2, 1, 0)]
+    (far, near, share_of), terms = zip(*others)
+    terms0 = sum(terms, start=terms0)
+    leaving0 = weight_grads(1, saved0, grads0, pre_grad0, project_grad0)
+    passed_n0, middle_n0, far, near, share_of, terms0, leaving0, project_grad0, sums1 = join(
+        passed_n0, middle_n0, far, near, share_of, terms0, leaving0, project_grad0, sums1
+    )
+
+    far_n0, near_n0 = send_sums(far, passed_n0, near)
+    came0 = swap(leaving0, "section", 1)
+    kept0 = weight_grads(0, saved0, grads0, pre_grad0, project_grad0)
+    came0, kept0 = join(came0, kept0)
+
+    side0, ahead0, rest0 = fold(kept0, came0)
+    total = add(share_b1, near_y1) + add(middle_y1, far_y1)
+    y1_own = (y0_own.astype(F32) + total).astype(BF16)
+    terms = sum_over(jnp.stack([terms0, terms1]), "section")
+    side0, ahead0, rest0, terms, y1_own = join(side0, ahead0, rest0, terms, y1_own)
+
+    first0, second0 = (swap(side0, "col", 1), swap(ahead0, "col", 2))
+    terms = sum_over(sum_over(terms, "col"), "row")
+    first0, second0, far_n0, near_n0, terms = join(first0, second0, far_n0, near_n0, terms)
+
+    total = add(share_of, near_n0) + add(middle_n0, far_n0)
+    dx0_own = input_grad(total, x_own, dx1_own)
+    passed0 = (
+        swap(add(rest0[1], first0[1]).astype(BF16), "col", 2),
+        swap(add(rest0[3], second0[1]).astype(BF16), "col", 1),
+    )
+    sums0 = (
+        add(add(rest0[0], first0[0]), passed0[0]),
+        add(add(rest0[2], second0[0]), passed0[1]),
+    )
 
     choose = lambda here, there: jnp.where(first, here, there)
     leaving = jnp.concatenate([choose(b, a) for a, b in zip(sums0, sums1)]).astype(BF16)
@@ -707,7 +837,7 @@
     qkv_grad, out_grad, up_grad, down_grad = unpack(
         sec, upper, lower, swap(leaving, "section", 1), width, hidden
     )
-    terms = pick(total_of(jnp.stack([terms0, terms1])), sec)
+    terms = pick(terms, sec)
     terms = lax.dynamic_slice_in_dim(terms, (row * cols + col) * share, share, 1)
 
     def by_layer(zero, one):

time: 541 us -> 495 us (0.915)
  waiting for transfers between devices: 184 us -> 117 us
  local copies, waits for them, and re-layouts: 53.1 us -> 65.3 us
  Pallas kernels: 162 us -> 168 us
    ppermute x53 -> x46, waiting for transfers between devices: 80.3 us -> 26.8 us  [swap(): lax.ppermute(block, axis, [(i, i ^ bit) for i in range(lax.axis_size(axis...]
    ppermute x32, waiting for transfers between devices: 103 us -> 90.5 us  [along_row(): return lax.ppermute(block, 'row', pairs)]
    unnamed x260 -> x266, local copies, waits for them, and re-layouts: 49.9 us -> 60.6 us
    pallas_call x2, Pallas kernels: 7.5 us -> 15.8 us  [assemble(): pl.pallas_call(assemble_kernel, grid_spec=pltpu.PrefetchScalarGridSpec(nu...]
    convert_element_type x7 -> x8, other arithmetic: 3.34 us -> 9.91 us  [the longest x4 3.64 us: send_sums(): add(far, passed).astype(BF16)]
    ppermute x53 -> x46, starting transfers between devices: 54.7 us -> 57.2 us  [swap(): lax.ppermute(block, axis, [(i, i ^ bit) for i in range(lax.axis_size(axis...]
  transfers between devices with their start and end apart: 85 -> 78, of which waited for: 28 -> 21; matrix products, arithmetic and copies ran while one was open for 5% -> 6% of each run, Pallas kernels for 27% -> 33%
where the time goes in v3:
time: 495 us; the launch traced here: 487 us
  Pallas kernels  168 us (34%)
  waiting for transfers between devices  117 us (24%)
  starting transfers between devices  106 us (21%)
  local copies, waits for them, and re-layouts  65.3 us (13%)
  other arithmetic  28.4 us (6%)
    ppermute x32, waiting for transfers between devices, along_row(): return lax.ppermute(block, 'row', pairs)  90.5 us
    pallas_call x32, Pallas kernels, chunk_call(): pl.pallas_call(kernel, grid_spec=pltpu.PrefetchScalarGridSpec(num_scalar_...  82 us
    unnamed x266, local copies, waits for them, and re-layouts  60.6 us
    ppermute x46, starting transfers between devices, swap(): lax.ppermute(block, axis, [(i, i ^ bit) for i in range(lax.axis_size(axis...  57.2 us
    ppermute x32, starting transfers between devices, along_row(): return lax.ppermute(block, 'row', pairs)  48.5 us
    pallas_call x4, Pallas kernels, weight_grads(): pl.pallas_call(outer_kernel, grid=(6,), in_specs=[left, left, left, pl.Bl...  40 us
    ppermute x46, waiting for transfers between devices, swap(): lax.ppermute(block, axis, [(i, i ^ bit) for i in range(lax.axis_size(axis...  26.8 us
    pallas_call x2, Pallas kernels, attend_back(): pl.pallas_call(attend_back_kernel, grid=(pairs,), in_specs=[pl.BlockSpec(...  21.5 us
  transfers between devices with their start and end apart: 78, of which 21 were waited for; matrix products, arithmetic and copies ran while one was open for 6% of the time, Pallas kernels for 33%

profile of v3, /device:TPU:1, one launch (start us, length us, event | category | flops | bytes accessed | tf_op | source)
XLA Modules:
  0.0 487.1 jit_solution(2901721852165461757)
XLA Ops:
  24.1 12.8 %collective-permute-done.7 = f32[2,4,1024]{2,1,0:T(4,128)S(1)} collective-permute-done((f32[2,4,1024]{2,1,0:T(4,128)S(1)}, f32[2,4,1024]{2,1,0:T(4,128)S(1)}, u32[]{:S(2)}, u32[]{:S(2)}) %collective-permute-start.7) | collective-permute-done | bytes 32800 | tf_op jit(solution)/shard_map/ppermute | solution.py:521
  41.8 21.1 %collective-permute-done.15.refs_0_ = bf16[256,1024]{1,0:T(8,128)(2,1)S(1)} collective-permute-done((bf16[256,1024]{1,0:T(8,128)(2,1)S(1)}, bf16[256,1024]{1,0:T(8,128)(2,1)S(1)}, u32[]{:S(2)}, u32[]{:S(2)}) %collective-permute-start.15) | collective-permute-done | bytes 524320 | tf_op jit(solution)/shard_map/ppermute | solution.py:552
  65.2 7.8 %collective-permute-done.13.refs_3_ = bf16[64,3072]{1,0:T(8,128)(2,1)S(1)} collective-permute-done((bf16[64,3072]{1,0:T(8,128)(2,1)S(1)}, bf16[64,3072]{1,0:T(8,128)(2,1)S(1)}, u32[]{:S(2)}, u32[]{:S(2)}) %collective-permute-start.13) | collective-permute-done | bytes 393248 | tf_op jit(solution)/shard_map/ppermute | solution.py:521
  79.3 8.1 %assemble.2.refs_2_.refs_3_.refs_4_.refs_5_.refs_1_.refs_6_ = bf16[1024,3072]{1,0:T(8,128)(2,1)} custom-call(s32[2]{0:T(128)} %pad_add_fusion.place, bf16[128,3072]{1,0:T(8,128)(2,1)} %copy-done.99, bf16[128,3072]{1,0:T(8,128)(2,1)} %copy-done.102, bf16[128,3072]{1,0:T(8,128)(2,1)} %copy-done.103, bf16[64,3072]{1,0:T(8,128)(2,1)} %copy-done.114, ...), custom_call_target="tpu_custom_call" | custom-call | tf_op jit(solution)/shard_map/assemble/pallas_call | solution.py:475
  97.0 3.6 project.8
  100.5 3.6 project.9
  104.1 3.6 project.10
  107.7 3.6 project.11
  132.3 4.1 collective-permute-start.27
  136.5 3.6 collective-permute-start.32
  143.5 15.3 %collective-permute-done.27 = bf16[256,1024]{1,0:T(8,128)(2,1)S(1)} collective-permute-done((bf16[256,1024]{1,0:T(8,128)(2,1)S(1)}, bf16[256,1024]{1,0:T(8,128)(2,1)S(1)}, u32[]{:S(2)}, u32[]{:S(2)}) %collective-permute-start.27) | collective-permute-done | bytes 524320 | tf_op jit(solution)/shard_map/ppermute | solution.py:552
  166.0 7.7 %assemble.3.refs_2_.refs_3_.refs_1_.refs_4_.refs_5_.refs_6_ = bf16[1024,3072]{1,0:T(8,128)(2,1)} custom-call(s32[2]{0:T(128)} %pad_add_fusion.place, bf16[128,3072]{1,0:T(8,128)(2,1)} %get-tuple-element.383.refs_0_, bf16[128,3072]{1,0:T(8,128)(2,1)} %collective-permute-done.21.refs_1_, bf16[128,3072]{1,0:T(8,128)(2,1)} %collective-permute-done.22.refs_2_, ...), custom_call_target="tpu_custom_call" | custom-call | tf_op jit(solution)/shard_map/assemble/pallas_call | solution.py:475
  176.5 3.6 project.12
  182.6 6.7 %collective-permute-done.36.refs_0_ = bf16[256,1024]{1,0:T(8,128)(2,1)S(1)} collective-permute-done((bf16[256,1024]{1,0:T(8,128)(2,1)S(1)}, bf16[256,1024]{1,0:T(8,128)(2,1)S(1)}, u32[]{:S(2)}, u32[]{:S(2)}) %collective-permute-start.36) | collective-permute-done | bytes 524320 | tf_op jit(solution)/shard_map/ppermute | solution.py:552
  191.4 3.6 project.13
  196.5 3.6 project.14
  204.7 3.6 project.15
  208.5 3.9 attend.12
  215.5 3.9 attend.14
  225.3 5.7 %collective-permute-start.42 = (bf16[256,1024]{1,0:T(8,128)(2,1)}, bf16[256,1024]{1,0:T(8,128)(2,1)}, u32[]{:S(2)}, u32[]{:S(2)}) collective-permute-start(bf16[256,1024]{1,0:T(8,128)(2,1)} %get-tuple-element.459), channel_id=1, source_target_pairs={{0,4},{12,8},{1,5},{13,9},{2,6},{14,10},{3,7},{15,11},{16,20},{28,... | collective-permute-start | bytes 1572872 | tf_op jit(solution)/shard_map/ppermute | solution.py:552
  246.0 10.8 %attend_back.2.refs_3_.refs_2_.project_grad = bf16[3,1024,256]{2,1,0:T(8,128)(2,1)S(1)} custom-call(s32[1,1024]{1,0:T(1,128)S(1)} %bitcast.114, bf16[3,1024,256]{2,1,0:T(8,128)(2,1)S(1)} %copy-done.27, bf16[1024,256]{1,0:T(8,128)(2,1)S(1)} %get-tuple-element.468.grads, f32[2,2,1024]{2,1,0:T(2,128)S(1)} %reshape.189.logsum, ...), custom_call_target="tpu_custom_call" | custom-call | tf_op jit(solution)/shard_map/attend_back/pallas_call | solution.py:326
  275.9 9.9 %weight_grads.5.kept = bf16[4,128,3072]{2,1,0:T(8,128)(2,1)} custom-call(bf16[1024,1024]{1,0:T(8,128)(2,1)} %copy-done.32, bf16[1024,1024]{1,0:T(8,128)(2,1)} %copy-done.33, bf16[1024,1024]{1,0:T(8,128)(2,1)} %copy-done.38, bf16[3,1024,256]{2,1,0:T(8,128)(2,1)} %copy-done.31, bf16[1024,256]{1,0:T(8,128)(2,1)} %copy-done.49, bf16[1024,1024]{1,0:T(8,128)(2,1)} %copy-done.13, ...), custom_call_target="tpu_custom_call" | custom-call | tf_op jit(solution)/shard_map/weight_grads/pallas_call | solution.py:413
  285.8 10.0 %weight_grads.4 = bf16[4,128,3072]{2,1,0:T(8,128)(2,1)} custom-call(bf16[1024,1024]{1,0:T(8,128)(2,1)} %copy-done.32, bf16[1024,1024]{1,0:T(8,128)(2,1)} %copy-done.33, bf16[1024,1024]{1,0:T(8,128)(2,1)} %copy-done.38, bf16[3,1024,256]{2,1,0:T(8,128)(2,1)} %copy-done.31, bf16[1024,256]{1,0:T(8,128)(2,1)} %copy-done.49, bf16[1024,1024]{1,0:T(8,128)(2,1)} %copy-done.13, ...), custom_call_target="tpu_custom_call" | custom-call | tf_op jit(solution)/shard_map/weight_grads/pallas_call | solution.py:413
  310.9 18.5 %collective-permute-done.48.refs_0_ = bf16[256,1024]{1,0:T(8,128)(2,1)S(1)} collective-permute-done((bf16[256,1024]{1,0:T(8,128)(2,1)S(1)}, bf16[256,1024]{1,0:T(8,128)(2,1)S(1)}, u32[]{:S(2)}, u32[]{:S(2)}) %collective-permute-start.48) | collective-permute-done | bytes 524320 | tf_op jit(solution)/shard_map/ppermute | solution.py:552
  365.4 10.8 %attend_back.3.refs_3_.refs_2_.project_grad = bf16[3,1024,256]{2,1,0:T(8,128)(2,1)S(1)} custom-call(s32[1,1024]{1,0:T(1,128)S(1)} %bitcast.115, bf16[3,1024,256]{2,1,0:T(8,128)(2,1)S(1)} %copy-done.29, bf16[1024,256]{1,0:T(8,128)(2,1)S(1)} %get-tuple-element.529.grads, f32[2,2,1024]{2,1,0:T(2,128)S(1)} %reshape.190.logsum, ...), custom_call_target="tpu_custom_call" | custom-call | tf_op jit(solution)/shard_map/attend_back/pallas_call | solution.py:326
  388.8 4.2 collective-permute-start.57
  394.5 10.2 %weight_grads.6 = bf16[4,128,3072]{2,1,0:T(8,128)(2,1)} custom-call(bf16[1024,1024]{1,0:T(8,128)(2,1)} %copy-done.34, bf16[1024,1024]{1,0:T(8,128)(2,1)} %copy-done.35, bf16[1024,1024]{1,0:T(8,128)(2,1)} %copy-done.41, bf16[3,1024,256]{2,1,0:T(8,128)(2,1)} %copy-done.30, bf16[1024,256]{1,0:T(8,128)(2,1)} %copy-done.48, bf16[1024,1024]{1,0:T(8,128)(2,1)} %copy-done.18, ...), custom_call_target="tpu_custom_call" | custom-call | tf_op jit(solution)/shard_map/weight_grads/pallas_call | solution.py:413
  407.6 3.5 collective-permute-start.61
  413.1 9.9 %weight_grads.7.kept = bf16[4,128,3072]{2,1,0:T(8,128)(2,1)} custom-call(bf16[1024,1024]{1,0:T(8,128)(2,1)} %copy-done.34, bf16[1024,1024]{1,0:T(8,128)(2,1)} %copy-done.35, bf16[1024,1024]{1,0:T(8,128)(2,1)} %copy-done.41, bf16[3,1024,256]{2,1,0:T(8,128)(2,1)} %copy-done.30, bf16[1024,256]{1,0:T(8,128)(2,1)} %copy-done.48, bf16[1024,1024]{1,0:T(8,128)(2,1)} %copy-done.18, ...), custom_call_target="tpu_custom_call" | custom-call | tf_op jit(solution)/shard_map/weight_grads/pallas_call | solution.py:413
  425.0 4.0 fold.3
  444.2 23.0 %collective-permute-done.66 = bf16[256,1024]{1,0:T(8,128)(2,1)S(1)} collective-permute-done((bf16[256,1024]{1,0:T(8,128)(2,1)S(1)}, bf16[256,1024]{1,0:T(8,128)(2,1)S(1)}, u32[]{:S(2)}, u32[]{:S(2)}) %collective-permute-start.66) | collective-permute-done | bytes 524320 | tf_op jit(solution)/shard_map/ppermute | solution.py:552
  472.2 6.0 %collective-permute-start.74 = (bf16[256,1024]{1,0:T(8,128)(2,1)S(1)}, bf16[256,1024]{1,0:T(8,128)(2,1)S(1)}, u32[]{:S(2)}, u32[]{:S(2)}) collective-permute-start(bf16[256,1024]{1,0:T(8,128)(2,1)S(1)} %get-tuple-element.618), channel_id=1, source_target_pairs={{0,16},{16,0},{1,17},{17,1},{2,18},{18,2},{3,19},{19,3},{4,20},{20... | collective-permute-start | bytes 1572872 | tf_op jit(solution)/shard_map/ppermute | solution.py:521
  (505 shorter events, 234.2 us)
Async XLA Ops:
  36.9 26.0 %collective-permute-start.15 = (bf16[256,1024]{1,0:T(8,128)(2,1)S(1)}, bf16[256,1024]{1,0:T(8,128)(2,1)S(1)}, u32[]{:S(2)}, u32[]{:S(2)}) collective-permute-start(bf16[256,1024]{1,0:T(8,128)(2,1)S(1)} %get-tuple-element.326.refs_0_), channel_id=1, source_target_pairs={{0,8},{8,0},{4,12},{12,4},{1,9},{9,1},{5,13},{13,5},{2,10},{10,2},... | collective-permute-start | bytes 1572872 | tf_op jit(solution)/shard_map/ppermute | solution.py:552
  38.2 25.0 %collective-permute-start.16 = (bf16[256,1024]{1,0:T(8,128)(2,1)S(1)}, bf16[256,1024]{1,0:T(8,128)(2,1)S(1)}, u32[]{:S(2)}, u32[]{:S(2)}) collective-permute-start(bf16[256,1024]{1,0:T(8,128)(2,1)S(1)} %get-tuple-element.326.refs_0_), channel_id=1, source_target_pairs={{0,4},{4,0},{8,12},{12,8},{1,5},{5,1},{9,13},{13,9},{2,6},{6,2},{1... | collective-permute-start | bytes 1572872 | tf_op jit(solution)/shard_map/ppermute | solution.py:552
  38.6 35.1 %collective-permute-start.10 = (bf16[128,3072]{1,0:T(8,128)(2,1)S(1)}, bf16[128,3072]{1,0:T(8,128)(2,1)S(1)}, u32[]{:S(2)}, u32[]{:S(2)}) collective-permute-start(bf16[128,3072]{1,0:T(8,128)(2,1)S(1)} %get-tuple-element.305.refs_0_), channel_id=1, source_target_pairs={{0,16},{16,0},{1,17},{17,1},{2,18},{18,2},{3,19},{19,3},{4,20},{20... | collective-permute-start | bytes 2359304 | tf_op jit(solution)/shard_map/ppermute | solution.py:521
  41.2 32.6 %collective-permute-start.11 = (bf16[128,3072]{1,0:T(8,128)(2,1)S(1)}, bf16[128,3072]{1,0:T(8,128)(2,1)S(1)}, u32[]{:S(2)}, u32[]{:S(2)}) collective-permute-start(bf16[128,3072]{1,0:T(8,128)(2,1)S(1)} %collective-permute-done.8.refs_1_), channel_id=1, source_target_pairs={{0,16},{16,0},{1,17},{17,1},{2,18},{18,2},{3,19},{19,3},{4,20},{20... | collective-permute-start | bytes 2359304 | tf_op jit(solution)/shard_map/ppermute | solution.py:521
  41.3 32.5 %collective-permute-start.12 = (bf16[128,3072]{1,0:T(8,128)(2,1)S(1)}, bf16[128,3072]{1,0:T(8,128)(2,1)S(1)}, u32[]{:S(2)}, u32[]{:S(2)}) collective-permute-start(bf16[128,3072]{1,0:T(8,128)(2,1)S(1)} %collective-permute-done.9.refs_2_), channel_id=1, source_target_pairs={{0,16},{16,0},{1,17},{17,1},{2,18},{18,2},{3,19},{19,3},{4,20},{20... | collective-permute-start | bytes 2359304 | tf_op jit(solution)/shard_map/ppermute | solution.py:521
  89.1 26.9 %collective-permute-start.21 = (bf16[128,3072]{1,0:T(8,128)(2,1)}, bf16[128,3072]{1,0:T(8,128)(2,1)}, u32[]{:S(2)}, u32[]{:S(2)}) collective-permute-start(bf16[128,3072]{1,0:T(8,128)(2,1)} %get-tuple-element.383.refs_0_), channel_id=1, source_target_pairs={{0,1},{1,0},{2,3},{3,2},{4,5},{5,4},{6,7},{7,6},{8,9},{9,8},{10,11... | collective-permute-start | bytes 2359304 | tf_op jit(solution)/shard_map/ppermute | solution.py:521
  90.3 25.7 %collective-permute-start.22 = (bf16[128,3072]{1,0:T(8,128)(2,1)}, bf16[128,3072]{1,0:T(8,128)(2,1)}, u32[]{:S(2)}, u32[]{:S(2)}) collective-permute-start(bf16[128,3072]{1,0:T(8,128)(2,1)} %get-tuple-element.383.refs_0_), channel_id=1, source_target_pairs={{0,2},{1,3},{2,0},{3,1},{4,6},{5,7},{6,4},{7,5},{8,10},{9,11},{10,... | collective-permute-start | bytes 2359304 | tf_op jit(solution)/shard_map/ppermute | solution.py:521
  91.5 24.4 %collective-permute-start.23 = (bf16[256,1024]{1,0:T(8,128)(2,1)}, bf16[256,1024]{1,0:T(8,128)(2,1)S(1)}, u32[]{:S(2)}, u32[]{:S(2)}) collective-permute-start(bf16[256,1024]{1,0:T(8,128)(2,1)} %dynamic-slice_bitcast_fusion.refs_0_), channel_id=1, source_target_pairs={{0,8},{8,0},{4,12},{12,4},{1,9},{9,1},{5,13},{13,5},{2,10},{10,2},... | collective-permute-start | bytes 1572872 | tf_op jit(solution)/shard_map/ppermute | solution.py:552
  93.3 22.6 %collective-permute-start.24 = (bf16[256,1024]{1,0:T(8,128)(2,1)}, bf16[256,1024]{1,0:T(8,128)(2,1)S(1)}, u32[]{:S(2)}, u32[]{:S(2)}) collective-permute-start(bf16[256,1024]{1,0:T(8,128)(2,1)} %dynamic-slice_bitcast_fusion.refs_0_), channel_id=1, source_target_pairs={{0,4},{4,0},{8,12},{12,8},{1,5},{5,1},{9,13},{13,9},{2,6},{6,2},{1... | collective-permute-start | bytes 1572872 | tf_op jit(solution)/shard_map/ppermute | solution.py:552
  132.3 26.5 %collective-permute-start.27 = (bf16[256,1024]{1,0:T(8,128)(2,1)S(1)}, bf16[256,1024]{1,0:T(8,128)(2,1)S(1)}, u32[]{:S(2)}, u32[]{:S(2)}) collective-permute-start(bf16[256,1024]{1,0:T(8,128)(2,1)S(1)} %add_convert_fusion.3), channel_id=1, source_target_pairs={{0,8},{8,0},{4,12},{12,4},{1,9},{9,1},{5,13},{13,5},{2,10},{10,2},... | collective-permute-start | bytes 1572872 | tf_op jit(solution)/shard_map/ppermute | solution.py:552
  136.5 24.2 %collective-permute-start.28 = (bf16[256,1024]{1,0:T(8,128)(2,1)S(1)}, bf16[256,1024]{1,0:T(8,128)(2,1)S(1)}, u32[]{:S(2)}, u32[]{:S(2)}) collective-permute-start(bf16[256,1024]{1,0:T(8,128)(2,1)S(1)} %get-tuple-element.375), channel_id=1, source_target_pairs={{0,4},{4,0},{8,12},{12,8},{1,5},{5,1},{9,13},{13,9},{2,6},{6,2},{1... | collective-permute-start | bytes 1572872 | tf_op jit(solution)/shard_map/ppermute | solution.py:552
  136.5 24.3 %collective-permute-start.32 = (bf16[128,3072]{1,0:T(8,128)(2,1)}, bf16[128,3072]{1,0:T(8,128)(2,1)S(1)}, u32[]{:S(2)}, u32[]{:S(2)}) collective-permute-start(bf16[128,3072]{1,0:T(8,128)(2,1)} %collective-permute-done.21.refs_1_), channel_id=1, source_target_pairs={{0,16},{16,0},{1,17},{17,1},{2,18},{18,2},{3,19},{19,3},{4,20},{20... | collective-permute-start | bytes 2359304 | tf_op jit(solution)/shard_map/ppermute | solution.py:521
  163.9 25.5 %collective-permute-start.36 = (bf16[256,1024]{1,0:T(8,128)(2,1)S(1)}, bf16[256,1024]{1,0:T(8,128)(2,1)S(1)}, u32[]{:S(2)}, u32[]{:S(2)}) collective-permute-start(bf16[256,1024]{1,0:T(8,128)(2,1)S(1)} %get-tuple-element.623.refs_0_), channel_id=1, source_target_pairs={{0,8},{8,0},{4,12},{12,4},{1,9},{9,1},{5,13},{13,5},{2,10},{10,2},... | collective-permute-start | bytes 1572872 | tf_op jit(solution)/shard_map/ppermute | solution.py:552
  164.8 24.6 %collective-permute-start.37 = (bf16[256,1024]{1,0:T(8,128)(2,1)S(1)}, bf16[256,1024]{1,0:T(8,128)(2,1)S(1)}, u32[]{:S(2)}, u32[]{:S(2)}) collective-permute-start(bf16[256,1024]{1,0:T(8,128)(2,1)S(1)} %get-tuple-element.623.refs_0_), channel_id=1, source_target_pairs={{0,4},{4,0},{8,12},{12,8},{1,5},{5,1},{9,13},{13,9},{2,6},{6,2},{1... | collective-permute-start | bytes 1572872 | tf_op jit(solution)/shard_map/ppermute | solution.py:552
  165.3 37.2 %collective-permute-start.39 = (bf16[256,1024]{1,0:T(8,128)(2,1)S(1)}, bf16[256,1024]{1,0:T(8,128)(2,1)S(1)}, u32[]{:S(2)}, u32[]{:S(2)}) collective-permute-start(bf16[256,1024]{1,0:T(8,128)(2,1)S(1)} %get-tuple-element.623.refs_0_), channel_id=1, source_target_pairs={{4,8},{8,4},{5,9},{9,5},{6,10},{10,6},{7,11},{11,7},{20,24},{24,20... | collective-permute-start | bytes 1572872 | tf_op jit(solution)/shard_map/ppermute | solution.py:552
  190.7 32.9 %collective-permute-start.41 = (bf16[256,1024]{1,0:T(8,128)(2,1)}, bf16[256,1024]{1,0:T(8,128)(2,1)S(1)}, u32[]{:S(2)}, u32[]{:S(2)}) collective-permute-start(bf16[256,1024]{1,0:T(8,128)(2,1)} %dynamic-slice_bitcast_fusion.refs_0_), channel_id=1, source_target_pairs={{4,8},{8,4},{5,9},{9,5},{6,10},{10,6},{7,11},{11,7},{20,24},{24,20... | collective-permute-start | bytes 1572872 | tf_op jit(solution)/shard_map/ppermute | solution.py:552
  225.3 31.5 %collective-permute-start.42 = (bf16[256,1024]{1,0:T(8,128)(2,1)}, bf16[256,1024]{1,0:T(8,128)(2,1)}, u32[]{:S(2)}, u32[]{:S(2)}) collective-permute-start(bf16[256,1024]{1,0:T(8,128)(2,1)} %get-tuple-element.459), channel_id=1, source_target_pairs={{0,4},{12,8},{1,5},{13,9},{2,6},{14,10},{3,7},{15,11},{16,20},{28,... | collective-permute-start | bytes 1572872 | tf_op jit(solution)/shard_map/ppermute | solution.py:552
  231.0 25.8 %collective-permute-start.43 = (bf16[256,1024]{1,0:T(8,128)(2,1)}, bf16[256,1024]{1,0:T(8,128)(2,1)}, u32[]{:S(2)}, u32[]{:S(2)}) collective-permute-start(bf16[256,1024]{1,0:T(8,128)(2,1)} %get-tuple-element.459), channel_id=1, source_target_pairs={{4,8},{8,4},{5,9},{9,5},{6,10},{10,6},{7,11},{11,7},{20,24},{24,20... | collective-permute-start | bytes 1572872 | tf_op jit(solution)/shard_map/ppermute | solution.py:552
  272.4 26.3 %collective-permute-start.46 = (bf16[256,1024]{1,0:T(8,128)(2,1)S(1)}, bf16[256,1024]{1,0:T(8,128)(2,1)S(1)}, u32[]{:S(2)}, u32[]{:S(2)}) collective-permute-start(bf16[256,1024]{1,0:T(8,128)(2,1)S(1)} %add_convert_fusion.2), channel_id=1, source_target_pairs={{0,8},{8,0},{4,12},{12,4},{1,9},{9,1},{5,13},{13,5},{2,10},{10,2},... | collective-permute-start | bytes 1572872 | tf_op jit(solution)/shard_map/ppermute | solution.py:552
  275.5 23.2 %collective-permute-start.47 = (bf16[256,1024]{1,0:T(8,128)(2,1)}, bf16[256,1024]{1,0:T(8,128)(2,1)S(1)}, u32[]{:S(2)}, u32[]{:S(2)}) collective-permute-start(bf16[256,1024]{1,0:T(8,128)(2,1)} %get-tuple-element.486), channel_id=1, source_target_pairs={{0,4},{4,0},{8,12},{12,8},{1,5},{5,1},{9,13},{13,9},{2,6},{6,2},{1... | collective-permute-start | bytes 1572872 | tf_op jit(solution)/shard_map/ppermute | solution.py:552
  298.7 31.4 %collective-permute-start.50 = (bf16[4,128,3072]{2,1,0:T(8,128)(2,1)}, bf16[4,128,3072]{2,1,0:T(8,128)(2,1)S(1)}, u32[]{:S(2)}, u32[]{:S(2)}) collective-permute-start(bf16[4,128,3072]{2,1,0:T(8,128)(2,1)} %weight_grads.4), channel_id=1, source_target_pairs={{0,16},{16,0},{1,17},{17,1},{2,18},{18,2},{3,19},{19,3},{4,20},{20... | collective-permute-start | bytes 9437192 | tf_op jit(solution)/shard_map/ppermute | solution.py:521
  303.4 26.0 %collective-permute-start.48 = (bf16[256,1024]{1,0:T(8,128)(2,1)S(1)}, bf16[256,1024]{1,0:T(8,128)(2,1)S(1)}, u32[]{:S(2)}, u32[]{:S(2)}) collective-permute-start(bf16[256,1024]{1,0:T(8,128)(2,1)S(1)} %fusion.17.refs_0_), channel_id=1, source_target_pairs={{0,8},{8,0},{4,12},{12,4},{1,9},{9,1},{5,13},{13,5},{2,10},{10,2},... | collective-permute-start | bytes 1572872 | tf_op jit(solution)/shard_map/ppermute | solution.py:552
  305.9 24.2 %collective-permute-start.49 = (bf16[256,1024]{1,0:T(8,128)(2,1)S(1)}, bf16[256,1024]{1,0:T(8,128)(2,1)S(1)}, u32[]{:S(2)}, u32[]{:S(2)}) collective-permute-start(bf16[256,1024]{1,0:T(8,128)(2,1)S(1)} %fusion.17.refs_0_), channel_id=1, source_target_pairs={{0,4},{4,0},{8,12},{12,8},{1,5},{5,1},{9,13},{13,9},{2,6},{6,2},{1... | collective-permute-start | bytes 1572872 | tf_op jit(solution)/shard_map/ppermute | solution.py:552
  305.9 39.2 %collective-permute-start.52 = (bf16[256,1024]{1,0:T(8,128)(2,1)S(1)}, bf16[256,1024]{1,0:T(8,128)(2,1)S(1)}, u32[]{:S(2)}, u32[]{:S(2)}) collective-permute-start(bf16[256,1024]{1,0:T(8,128)(2,1)S(1)} %fusion.17.refs_0_), channel_id=1, source_target_pairs={{4,8},{8,4},{5,9},{9,5},{6,10},{10,6},{7,11},{11,7},{20,24},{24,20... | collective-permute-start | bytes 1572872 | tf_op jit(solution)/shard_map/ppermute | solution.py:552
  345.1 35.5 %collective-permute-start.53 = (bf16[2,64,3072]{2,1,0:T(8,128)(2,1)}, bf16[2,64,3072]{2,1,0:T(8,128)(2,1)}, u32[]{:S(2)}, u32[]{:S(2)}) collective-permute-start(bf16[2,64,3072]{2,1,0:T(8,128)(2,1)} %get-tuple-element.519), channel_id=1, source_target_pairs={{0,1},{1,0},{2,3},{3,2},{4,5},{5,4},{6,7},{7,6},{8,9},{9,8},{10,11... | collective-permute-start | bytes 2359304 | tf_op jit(solution)/shard_map/ppermute | solution.py:521
  346.4 34.2 %collective-permute-start.54 = (bf16[2,64,3072]{2,1,0:T(8,128)(2,1)}, bf16[2,64,3072]{2,1,0:T(8,128)(2,1)}, u32[]{:S(2)}, u32[]{:S(2)}) collective-permute-start(bf16[2,64,3072]{2,1,0:T(8,128)(2,1)} %get-tuple-element.520), channel_id=1, source_target_pairs={{0,2},{1,3},{2,0},{3,1},{4,6},{5,7},{6,4},{7,5},{8,10},{9,11},{10,... | collective-permute-start | bytes 2359304 | tf_op jit(solution)/shard_map/ppermute | solution.py:521
  349.6 31.0 %collective-permute-start.55 = (bf16[256,1024]{1,0:T(8,128)(2,1)}, bf16[256,1024]{1,0:T(8,128)(2,1)}, u32[]{:S(2)}, u32[]{:S(2)}) collective-permute-start(bf16[256,1024]{1,0:T(8,128)(2,1)} %add_convert_fusion.1), channel_id=1, source_target_pairs={{0,8},{8,0},{4,12},{12,4},{1,9},{9,1},{5,13},{13,5},{2,10},{10,2},... | collective-permute-start | bytes 1572872 | tf_op jit(solution)/shard_map/ppermute | solution.py:552
  351.8 28.8 %collective-permute-start.56 = (bf16[256,1024]{1,0:T(8,128)(2,1)}, bf16[256,1024]{1,0:T(8,128)(2,1)}, u32[]{:S(2)}, u32[]{:S(2)}) collective-permute-start(bf16[256,1024]{1,0:T(8,128)(2,1)} %get-tuple-element.523), channel_id=1, source_target_pairs={{0,4},{4,0},{8,12},{12,8},{1,5},{5,1},{9,13},{13,9},{2,6},{6,2},{1... | collective-permute-start | bytes 1572872 | tf_op jit(solution)/shard_map/ppermute | solution.py:552
  434.4 32.8 %collective-permute-start.64 = (bf16[2,64,3072]{2,1,0:T(8,128)(2,1)S(1)}, bf16[2,64,3072]{2,1,0:T(8,128)(2,1)S(1)}, u32[]{:S(2)}, u32[]{:S(2)}) collective-permute-start(bf16[2,64,3072]{2,1,0:T(8,128)(2,1)S(1)} %get-tuple-element.565), channel_id=1, source_target_pairs={{0,1},{1,0},{2,3},{3,2},{4,5},{5,4},{6,7},{7,6},{8,9},{9,8},{10,11... | collective-permute-start | bytes 2359304 | tf_op jit(solution)/shard_map/ppermute | solution.py:521
  435.0 32.2 %collective-permute-start.65 = (bf16[2,64,3072]{2,1,0:T(8,128)(2,1)S(1)}, bf16[2,64,3072]{2,1,0:T(8,128)(2,1)S(1)}, u32[]{:S(2)}, u32[]{:S(2)}) collective-permute-start(bf16[2,64,3072]{2,1,0:T(8,128)(2,1)S(1)} %get-tuple-element.566), channel_id=1, source_target_pairs={{0,2},{1,3},{2,0},{3,1},{4,6},{5,7},{6,4},{7,5},{8,10},{9,11},{10,... | collective-permute-start | bytes 2359304 | tf_op jit(solution)/shard_map/ppermute | solution.py:521
  440.8 26.4 %collective-permute-start.66 = (bf16[256,1024]{1,0:T(8,128)(2,1)S(1)}, bf16[256,1024]{1,0:T(8,128)(2,1)S(1)}, u32[]{:S(2)}, u32[]{:S(2)}) collective-permute-start(bf16[256,1024]{1,0:T(8,128)(2,1)S(1)} %add_convert_fusion), channel_id=1, source_target_pairs={{0,8},{8,0},{4,12},{12,4},{1,9},{9,1},{5,13},{13,5},{2,10},{10,2},... | collective-permute-start | bytes 1572872 | tf_op jit(solution)/shard_map/ppermute | solution.py:552
  442.2 25.0 %collective-permute-start.67 = (bf16[256,1024]{1,0:T(8,128)(2,1)S(1)}, bf16[256,1024]{1,0:T(8,128)(2,1)S(1)}, u32[]{:S(2)}, u32[]{:S(2)}) collective-permute-start(bf16[256,1024]{1,0:T(8,128)(2,1)S(1)} %copy-done.96), channel_id=1, source_target_pairs={{0,4},{4,0},{8,12},{12,8},{1,5},{5,1},{9,13},{13,9},{2,6},{6,2},{1... | collective-permute-start | bytes 1572872 | tf_op jit(solution)/shard_map/ppermute | solution.py:552
  (177 other events, 1666.1 us)

commit v4 on v3

--- a/solution.py
+++ b/solution.py
@@ -79,11 +79,15 @@
     return (jnp.where(rotated, jnp.cos(angles), 1.0), jnp.where(rotated, jnp.sin(angles), 0.0))
 
 
-def params(mib=24):
+def params(mib=18):
     return pltpu.CompilerParams(vmem_limit_bytes=mib << 20)
 
 
-def chunk_call(body, name, index, outs, inputs, kept=(), place=None):
+def cost(us):
+    return pl.CostEstimate(flops=int(us * 1.1e+09), bytes_accessed=int(us * 3.2e+06), transcendentals=0)
+
+
+def chunk_call(body, name, us, index, outs, inputs, kept=(), place=None):
     given = len(inputs)
     number = index.reshape(1).astype(jnp.int32)
     if place is not None:
@@ -105,6 +109,7 @@
         out_shape=[jax.ShapeDtypeStruct(shape, dtype) for shape, dtype, _, _ in outs],
         input_output_aliases={1 + given + i: i for i in range(len(kept))},
         compiler_params=params(),
+        cost_estimate=cost(us),
         name=name,
     )(number, *[array for array, _, _ in inputs], *kept)
 
@@ -161,6 +166,7 @@
     return chunk_call(
         partial(project_body, len(chunk)),
         "project",
+        3.5,
         index,
         [
             ((tokens, model), BF16, (TOKENS, model), ROWS),
@@ -229,6 +235,7 @@
     return chunk_call(
         attend_body,
         "attend",
+        3,
         index,
         [
             ((tokens, width), BF16, (TOKENS, width), ROWS),
@@ -261,6 +268,7 @@
     return chunk_call(
         partial(through_branch_body, len(chunk)),
         "through_branch",
+        1.5,
         index,
         [
             ((tokens, hidden), BF16, (TOKENS, hidden), ROWS),
@@ -338,6 +346,7 @@
         out_shape=jax.ShapeDtypeStruct((3, tokens, width), BF16),
         scratch_shapes=[pltpu.VMEM((tokens, 128), F32), pltpu.VMEM((tokens, 128), F32)],
         compiler_params=params(),
+        cost_estimate=cost(11),
         name="attend_back",
     )(starts, qkv, context_grad, logsum.reshape(pairs, heads, tokens), *tables)
 
@@ -364,6 +373,7 @@
     return chunk_call(
         partial(through_inputs_body, len(chunk)),
         "through_inputs",
+        1.5,
         index,
         [
             ((TOKENS, model), BF16, (TOKENS, model), HERE),
@@ -424,7 +434,8 @@
         ],
         out_specs=pl.BlockSpec((4, model // 8, 2 * width), lambda j: (0, 0, j)),
         out_shape=jax.ShapeDtypeStruct((4, model // 8, 12 * width), BF16),
-        compiler_params=params(58),
+        compiler_params=params(18),
+        cost_estimate=cost(9),
         name="weight_grads",
     )(attn_in, feed_in, upstream, project_grad, context, pre_grad, active)
 
@@ -454,6 +465,7 @@
         out_specs=[block(2, rows // 2), block(2, rows // 2), block(4, rows // 2)],
         out_shape=[shape(2), shape(2), shape(4)],
         compiler_params=params(),
+        cost_estimate=cost(4),
         name="fold",
     )(kept, came)
 
@@ -481,7 +493,8 @@
             out_specs=pl.BlockSpec((8 * rows, step), lambda j, place: (0, j)),
         ),
         out_shape=jax.ShapeDtypeStruct((8 * rows, width), BF16),
-        compiler_params=params(58),
+        compiler_params=params(18),
+        cost_estimate=cost(6),
         name="assemble",
     )(place, *pieces)
 
@@ -512,7 +525,8 @@
             out_specs=[pl.BlockSpec(shape, lambda i, place: (0, 0)) for shape in shapes],
         ),
         out_shape=[jax.ShapeDtypeStruct(shape, F32) for shape in shapes],
-        compiler_params=params(32),
+        compiler_params=params(18),
+        cost_estimate=cost(2),
         name="unpack",
     )(sec.reshape(1).astype(jnp.int32), upper, lower, came)
 
@@ -640,6 +654,7 @@
         return result.astype(BF16)
 
 
+    far_x0, near_x0 = send_own(x_own)
     vectors = jnp.stack([attn_gain[0], attn_shift[0], mlp_gain[0], mlp_shift[0]])
     norms = lax.dynamic_update_slice(
         jnp.zeros((2, 4, model), F32), vectors[None], (sec, 0, (row * cols + col) * share)
@@ -664,49 +679,53 @@
     norms, half0, half1 = join(norms, half0, half1)
 
     norms = sum_over(norms, "col")
+    norms, half0 = join(norms, half0)
+
     side0, ahead0 = send_sides(half0)
-    far_x0, near_x0 = send_own(x_own)
     starts = jnp.sum((docs[None, :] < docs[:, None]).astype(jnp.int32), axis=1)
     tables = rope_tables(docs, starts)
     starts = starts[None]
-    norms, half0, side0, ahead0, starts, tables = join(
-        norms, half0, side0, ahead0, starts, tables
-    )
+    half0, side0, ahead0, starts, tables, far_x0, near_x0 = join(
+        half0, side0, ahead0, starts, tables, far_x0, near_x0
+    )
+    passed_x0, middle_x0 = pass_on(x_own, far_x0)
+    chunks_x0 = [(x_own,), (near_x0,), (far_x0,), (middle_x0, passed_x0)]
 
     across0 = send_corner(side0, ahead0)
     mine = [half0, side0, ahead0]
     theirs = [swap(piece, "section", 1) for piece in mine]
-    mine, theirs, across0, far_x0, near_x0 = join(mine, theirs, across0, far_x0, near_x0)
-
-    passed_x0, middle_x0 = pass_on(x_own, far_x0)
+    mine, theirs, across0 = join(mine, theirs, across0)
+
     theirs = theirs + [swap(piece, "section", 1) for piece in across0]
-    packs = [assemble(place, mine + across0 + theirs), None]
-    chunks_x0 = [(x_own,), (near_x0,), (far_x0,), (middle_x0, passed_x0)]
-    packs, given, half1, chunks_x0 = join(packs, given, half1, chunks_x0)
+    mine, theirs, half1, given = join(mine + across0, theirs, half1, given)
 
     side1, ahead1 = send_sides(half1)
+    packs = [assemble(place, mine + theirs), None]
+    entered0 = ()
+    for number in range(3):
+        entered0 = enter(entered0, chunks_x0[number], number, 0)
+    chunks_x0, entered0, packs, given = join(chunks_x0, entered0, packs, given)
+
     far_g1, near_g1 = send_own(given)
-    entered0 = ()
-    for number in range(4):
-        entered0 = enter(entered0, chunks_x0[number], number, 0)
+    entered0 = enter(entered0, chunks_x0[3], 3, 0)
     kept, last = leave((), entered0, 3, 0)
-    half1, side1, ahead1, far_g1, near_g1, entered0, kept, last = join(
-        half1, side1, ahead1, far_g1, near_g1, entered0, kept, last
-    )
+    side1, ahead1, entered0, kept, last = join(side1, ahead1, entered0, kept, last)
 
     passed_y0, middle_y0 = send_last(last)
+    across1 = send_corner(side1, ahead1)
     kept, far = leave(kept, entered0, 2, 0)
     kept, near = leave(kept, entered0, 1, 0)
     (context0, logsum0), share_of = leave(kept, entered0, 0, 0)
-    passed_y0, middle_y0, far, near, share_of, context0, half1, side1, ahead1 = join(
-        passed_y0, middle_y0, far, near, share_of, context0, half1, side1, ahead1
+    passed_y0, middle_y0, across1, far, near, share_of, context0, half1, side1, ahead1 = join(
+        passed_y0, middle_y0, across1, far, near, share_of, context0, half1, side1, ahead1
     )
 
     far_y0, near_y0 = send_sums(far, passed_y0, near)
-    across1 = send_corner(side1, ahead1)
     mine = [half1, side1, ahead1] + across1
     theirs = [swap(piece, "section", 1) for piece in mine]
-    far_y0, near_y0, mine, theirs, far_g1 = join(far_y0, near_y0, mine, theirs, far_g1)
+    far_y0, near_y0, mine, theirs, far_g1, near_g1 = join(
+        far_y0, near_y0, mine, theirs, far_g1, near_g1
+    )
     total = add(share_of, near_y0) + add(middle_y0, far_y0)
     y0_own = (x_own.astype(F32) + total).astype(BF16)
 
@@ -721,19 +740,19 @@
     branch1 = back_branch(branch1, (near_g1,), 1, entered1[5], 1)
     entered1 = enter(entered1, (far_x1,), 2, 1)
     branch1 = back_branch(branch1, (far_g1,), 2, entered1[5], 1)
-    passed_x1, middle_x1, entered1, branch1, far_g1 = join(
-        passed_x1, middle_x1, entered1, branch1, far_g1
+    passed_x1, middle_x1, entered1, branch1, given, far_g1 = join(
+        passed_x1, middle_x1, entered1, branch1, given, far_g1
     )
 
     chunks_x1 = [(y0_own,), (near_x1,), (far_x1,), (middle_x1, passed_x1)]
+    passed_g1, middle_g1 = pass_on(given, far_g1)
     entered1 = enter(entered1, chunks_x1[3], 3, 1)
-    passed_g1, middle_g1 = pass_on(given, far_g1)
     kept, last_b1 = leave((), entered1, 3, 1)
     kept, far_b1 = leave(kept, entered1, 2, 1)
     kept, near_b1 = leave(kept, entered1, 1, 1)
     (context1, logsum1), share_b1 = leave(kept, entered1, 0, 1)
-    passed_g1, middle_g1, last_b1, far_b1, near_b1, share_b1, context1, entered1 = join(
-        passed_g1, middle_g1, last_b1, far_b1, near_b1, share_b1, context1, entered1
+    passed_g1, middle_g1, last_b1, far_b1, near_b1, share_b1, context1, logsum1, entered1 = join(
+        passed_g1, middle_g1, last_b1, far_b1, near_b1, share_b1, context1, logsum1, entered1
     )
 
     passed_y1, middle_y1 = send_last(last_b1)
@@ -742,50 +761,51 @@
     )
     saved1 = (entered1[0], entered1[1], entered1[4], context1)
     project_grad1 = attend_back(starts, entered1[2], context_grad1, logsum1, tables)
-    passed_y1, middle_y1, pre_grad1, project_grad1 = join(
-        passed_y1, middle_y1, pre_grad1, project_grad1
-    )
-
     last, terms1 = back_inputs(chunks_x1, 3, 1, project_grad1, pre_grad1)
-    last, terms1, project_grad1 = join(last, terms1, project_grad1)
+    last, terms1, project_grad1, pre_grad1, passed_y1, middle_y1 = join(
+        last, terms1, project_grad1, pre_grad1, passed_y1, middle_y1
+    )
 
     passed_n1, middle_n1 = send_last(last)
     others = [back_inputs(chunks_x1, number, 1, project_grad1, pre_grad1) for number in (2, 1, 0)]
     (far, near, share_of), terms = zip(*others)
     terms1 = sum(terms, start=terms1)
-    passed_n1, middle_n1, far, near, share_of, terms1, project_grad1 = join(
-        passed_n1, middle_n1, far, near, share_of, terms1, project_grad1
+    leaving1 = weight_grads(1, saved1, grads1, pre_grad1, project_grad1)
+    passed_n1, middle_n1, far, near, share_of, terms1, leaving1, project_grad1 = join(
+        passed_n1, middle_n1, far, near, share_of, terms1, leaving1, project_grad1
     )
 
     far_n1, near_n1 = send_sums(far, passed_n1, near)
-    leaving1 = weight_grads(1, saved1, grads1, pre_grad1, project_grad1)
+    came1 = swap(leaving1, "section", 1)
     kept1 = weight_grads(0, saved1, grads1, pre_grad1, project_grad1)
-    far_n1, near_n1, leaving1, kept1 = join(far_n1, near_n1, leaving1, kept1)
+    far_n1, near_n1, came1, kept1 = join(far_n1, near_n1, came1, kept1)
     total = add(share_of, near_n1) + add(middle_n1, far_n1)
     dx1_own = input_grad(total, y0_own, given)
 
     slope0 = entered0[5]
     far_g0, near_g0 = send_own(dx1_own)
-    came1 = swap(leaving1, "section", 1)
     branch0 = back_branch((), (dx1_own,), 0, slope0, 0)
-    far_g0, near_g0, came1, branch0 = join(far_g0, near_g0, came1, branch0)
+    side1, ahead1, rest1 = fold(kept1, came1)
+    far_g0, near_g0, branch0, side1, ahead1, rest1 = join(
+        far_g0, near_g0, branch0, side1, ahead1, rest1
+    )
 
     passed_g0, middle_g0 = pass_on(dx1_own, far_g0)
-    side1, ahead1, rest1 = fold(kept1, came1)
+    first1, second1 = (swap(side1, "col", 1), swap(ahead1, "col", 2))
     branch0 = back_branch(branch0, (near_g0,), 1, slope0, 0)
     branch0 = back_branch(branch0, (far_g0,), 2, slope0, 0)
-    passed_g0, middle_g0, branch0, side1, ahead1, rest1, far_b1, near_b1 = join(
-        passed_g0, middle_g0, branch0, side1, ahead1, rest1, far_b1, near_b1
-    )
-
-    first1, second1 = (swap(side1, "col", 1), swap(ahead1, "col", 2))
-    far_y1, near_y1 = send_sums(far_b1, passed_y1, near_b1)
+    far_b1 = add(far_b1, passed_y1).astype(BF16)
+    passed_g0, middle_g0, branch0, far_b1, near_b1 = join(
+        passed_g0, middle_g0, branch0, far_b1, near_b1
+    )
+
+    near_y1 = along_row(near_b1, ONE_OVER)
     pre_grad0, context_grad0, grads0 = back_branch(branch0, (middle_g0, passed_g0), 3, slope0, 0)
     saved0 = (entered0[0], entered0[1], entered0[4], context0)
     project_grad0 = attend_back(starts, entered0[2], context_grad0, logsum0, tables)
     last, terms0 = back_inputs(chunks_x0, 3, 0, project_grad0, pre_grad0)
-    first1, second1, far_y1, near_y1, last, terms0, project_grad0 = join(
-        first1, second1, far_y1, near_y1, last, terms0, project_grad0
+    last, terms0, project_grad0, near_y1, first1, second1 = join(
+        last, terms0, project_grad0, near_y1, first1, second1
     )
 
     passed_n0, middle_n0 = send_last(last)
@@ -793,38 +813,40 @@
         swap(add(rest1[1], first1[1]).astype(BF16), "col", 2),
         swap(add(rest1[3], second1[1]).astype(BF16), "col", 1),
     )
+    leaving0 = weight_grads(1, saved0, grads0, pre_grad0, project_grad0)
+    others = [back_inputs(chunks_x0, number, 0, project_grad0, pre_grad0) for number in (2, 1, 0)]
+    (far, near, share_of), terms = zip(*others)
+    terms = jnp.stack([sum(terms, start=terms0), terms1])
+    passed_n0, middle_n0, far, near, share_of, terms, leaving0, project_grad0, passed1 = join(
+        passed_n0, middle_n0, far, near, share_of, terms, leaving0, project_grad0, passed1
+    )
+
+    far_n0, near_n0 = send_sums(far, passed_n0, near)
+    came0 = swap(leaving0, "section", 1)
+    terms = sum_over(terms, "section")
+    kept0 = weight_grads(0, saved0, grads0, pre_grad0, project_grad0)
+    came0, kept0, terms = join(came0, kept0, terms)
+
+    side0, ahead0, rest0 = fold(kept0, came0)
+    terms = sum_over(terms, "col")
+    side0, ahead0, rest0, terms, far_b1 = join(side0, ahead0, rest0, terms, far_b1)
+
+    first0, second0 = (swap(side0, "col", 1), swap(ahead0, "col", 2))
+    far_y1 = along_row(far_b1, TWO_OVER)
+    first0, second0, far_n0, near_n0, terms = join(first0, second0, far_n0, near_n0, terms)
+
+    passed0 = (
+        swap(add(rest0[1], first0[1]).astype(BF16), "col", 2),
+        swap(add(rest0[3], second0[1]).astype(BF16), "col", 1),
+    )
+    terms = sum_over(terms, "row")
+    total = add(share_b1, near_y1) + add(middle_y1, far_y1)
+    y1_own = (y0_own.astype(F32) + total).astype(BF16)
+    total = add(share_of, near_n0) + add(middle_n0, far_n0)
+    dx0_own = input_grad(total, x_own, dx1_own)
     sums1 = (
         add(add(rest1[0], first1[0]), passed1[0]),
         add(add(rest1[2], second1[0]), passed1[1]),
-    )
-    others = [back_inputs(chunks_x0, number, 0, project_grad0, pre_grad0) for number in (2, 1, 0)]
-    (far, near, share_of), terms = zip(*others)
-    terms0 = sum(terms, start=terms0)
-    leaving0 = weight_grads(1, saved0, grads0, pre_grad0, project_grad0)
-    passed_n0, middle_n0, far, near, share_of, terms0, leaving0, project_grad0, sums1 = join(
-        passed_n0, middle_n0, far, near, share_of, terms0, leaving0, project_grad0, sums1
-    )
-
-    far_n0, near_n0 = send_sums(far, passed_n0, near)
-    came0 = swap(leaving0, "section", 1)
-    kept0 = weight_grads(0, saved0, grads0, pre_grad0, project_grad0)
-    came0, kept0 = join(came0, kept0)
-
-    side0, ahead0, rest0 = fold(kept0, came0)
-    total = add(share_b1, near_y1) + add(middle_y1, far_y1)
-    y1_own = (y0_own.astype(F32) + total).astype(BF16)
-    terms = sum_over(jnp.stack([terms0, terms1]), "section")
-    side0, ahead0, rest0, terms, y1_own = join(side0, ahead0, rest0, terms, y1_own)
-
-    first0, second0 = (swap(side0, "col", 1), swap(ahead0, "col", 2))
-    terms = sum_over(sum_over(terms, "col"), "row")
-    first0, second0, far_n0, near_n0, terms = join(first0, second0, far_n0, near_n0, terms)
-
-    total = add(share_of, near_n0) + add(middle_n0, far_n0)
-    dx0_own = input_grad(total, x_own, dx1_own)
-    passed0 = (
-        swap(add(rest0[1], first0[1]).astype(BF16), "col", 2),
-        swap(add(rest0[3], second0[1]).astype(BF16), "col", 1),
     )
     sums0 = (
         add(add(rest0[0], first0[0]), passed0[0]),

time: 495 us -> 470 us (0.949)
  waiting for transfers between devices: 117 us -> 162 us
  Pallas kernels: 168 us -> 141 us
  local copies, waits for them, and re-layouts: 65.3 us -> 40.6 us
  starting transfers between devices: 106 us -> 93.7 us
    ppermute x32, waiting for transfers between devices: 90.5 us -> 141 us  [along_row(): return lax.ppermute(block, 'row', pairs)]
    unnamed x266 -> x242, local copies, waits for them, and re-layouts: 60.6 us -> 34.7 us
    pallas_call x4, Pallas kernels: 40 us -> 22.8 us  [weight_grads(): pl.pallas_call(outer_kernel, grid=(6,), in_specs=[left, left, left, pl.Bl...]
    pallas_call x2, Pallas kernels: 15.8 us -> 7.68 us  [assemble(): pl.pallas_call(assemble_kernel, grid_spec=pltpu.PrefetchScalarGridSpec(nu...]
    ppermute x32, starting transfers between devices: 48.5 us -> 42.1 us  [along_row(): return lax.ppermute(block, 'row', pairs)]
    ppermute x46, waiting for transfers between devices: 26.8 us -> 20.7 us  [swap(): lax.ppermute(block, axis, [(i, i ^ bit) for i in range(lax.axis_size(axis...]
    ppermute x46, starting transfers between devices: 57.2 us -> 51.6 us  [swap(): lax.ppermute(block, axis, [(i, i ^ bit) for i in range(lax.axis_size(axis...]
  transfers between devices with their start and end apart: 78 -> 78, of which waited for: 21 -> 22; matrix products, arithmetic and copies ran while one was open for 6% -> 6% of each run, Pallas kernels for 33% -> 30%
where the time goes in v4:
time: 470 us; the launch traced here: 464 us
  waiting for transfers between devices  162 us (34%)
  Pallas kernels  141 us (30%)
  starting transfers between devices  93.7 us (20%)
  local copies, waits for them, and re-layouts  40.6 us (9%)
  other arithmetic  23.6 us (5%)
    ppermute x32, waiting for transfers between devices, along_row(): return lax.ppermute(block, 'row', pairs)  141 us
    pallas_call x32, Pallas kernels, chunk_call(): pl.pallas_call(kernel, grid_spec=pltpu.PrefetchScalarGridSpec(num_scalar_...  81.2 us
    ppermute x46, starting transfers between devices, swap(): lax.ppermute(block, axis, [(i, i ^ bit) for i in range(lax.axis_size(axis...  51.6 us
    ppermute x32, starting transfers between devices, along_row(): return lax.ppermute(block, 'row', pairs)  42.1 us
    unnamed x242, local copies, waits for them, and re-layouts  34.7 us
    pallas_call x4, Pallas kernels, weight_grads(): pl.pallas_call(outer_kernel, grid=(6,), in_specs=[left, left, left, pl.Bl...  22.8 us
    pallas_call x2, Pallas kernels, attend_back(): pl.pallas_call(attend_back_kernel, grid=(pairs,), in_specs=[pl.BlockSpec(...  21.5 us
    ppermute x46, waiting for transfers between devices, swap(): lax.ppermute(block, axis, [(i, i ^ bit) for i in range(lax.axis_size(axis...  20.7 us
  transfers between devices with their start and end apart: 78, of which 22 were waited for; matrix products, arithmetic and copies ran while one was open for 6% of the time, Pallas kernels for 30%

profile of v4, /device:TPU:1, one launch (start us, length us, event | category | flops | bytes accessed | tf_op | source)
XLA Modules:
  0.0 463.8 jit_solution(2049070911883420685)
XLA Ops:
  28.2 11.4 %collective-permute-done.10.refs_0_ = bf16[256,1024]{1,0:T(8,128)(2,1)S(1)} collective-permute-done((bf16[256,1024]{1,0:T(8,128)(2,1)S(1)}, bf16[256,1024]{1,0:T(8,128)(2,1)S(1)}, u32[]{:S(2)}, u32[]{:S(2)}) %collective-permute-start.10) | collective-permute-done | bytes 524320 | tf_op jit(solution)/shard_map/ppermute | solution.py:566
  51.4 6.7 %collective-permute-done.15.refs_3_ = bf16[64,3072]{1,0:T(8,128)(2,1)} collective-permute-done((bf16[64,3072]{1,0:T(8,128)(2,1)}, bf16[64,3072]{1,0:T(8,128)(2,1)}, u32[]{:S(2)}, u32[]{:S(2)}) %collective-permute-start.15) | collective-permute-done | bytes 393248 | tf_op jit(solution)/shard_map/ppermute | solution.py:535
  65.7 5.4 %assemble.2.refs_2_.refs_3_.refs_4_.refs_5_.refs_1_.refs_6_ = bf16[1024,3072]{1,0:T(8,128)(2,1)S(1)} custom-call(s32[2]{0:T(128)S(1)} %pad_add_fusion.place, bf16[128,3072]{1,0:T(8,128)(2,1)} %get-tuple-element.338.refs_0_, bf16[128,3072]{1,0:T(8,128)(2,1)} %collective-permute-done.8.refs_1_, bf16[128,3072]{1,0:T(8,128)(2,1)} %collective-permute-done.9.refs_2_, ...), custom_call_target="tpu_custom_call" | custom-call | flops 6600000000 | bytes 19200000 | tf_op jit(solution)/shard_map/assemble/pallas_call | solution.py:487
  71.0 3.6 project.8
  74.6 4.6 project.9
  79.3 3.6 project.10
  82.9 3.6 project.11
  86.6 3.6 attend.8
  108.8 16.7 %collective-permute-done.23 = bf16[256,1024]{1,0:T(8,128)(2,1)S(1)} collective-permute-done((bf16[256,1024]{1,0:T(8,128)(2,1)S(1)}, bf16[256,1024]{1,0:T(8,128)(2,1)S(1)}, u32[]{:S(2)}, u32[]{:S(2)}) %collective-permute-start.23) | collective-permute-done | bytes 524320 | tf_op jit(solution)/shard_map/ppermute | solution.py:566
  132.1 23.2 %collective-permute-done.27 = bf16[256,1024]{1,0:T(8,128)(2,1)S(1)} collective-permute-done((bf16[256,1024]{1,0:T(8,128)(2,1)S(1)}, bf16[256,1024]{1,0:T(8,128)(2,1)S(1)}, u32[]{:S(2)}, u32[]{:S(2)}) %collective-permute-start.27) | collective-permute-done | bytes 524320 | tf_op jit(solution)/shard_map/ppermute | solution.py:566
  161.1 3.6 project.12
  166.3 15.3 %collective-permute-done.36.refs_0_ = bf16[256,1024]{1,0:T(8,128)(2,1)S(1)} collective-permute-done((bf16[256,1024]{1,0:T(8,128)(2,1)S(1)}, bf16[256,1024]{1,0:T(8,128)(2,1)S(1)}, u32[]{:S(2)}, u32[]{:S(2)}) %collective-permute-start.36) | collective-permute-done | bytes 524320 | tf_op jit(solution)/shard_map/ppermute | solution.py:566
  182.9 3.6 project.13
  188.1 3.6 project.14
  196.6 3.6 project.15
  200.3 3.9 attend.12
  218.0 6.0 %collective-permute-start.42 = (bf16[256,1024]{1,0:T(8,128)(2,1)}, bf16[256,1024]{1,0:T(8,128)(2,1)}, u32[]{:S(2)}, u32[]{:S(2)}) collective-permute-start(bf16[256,1024]{1,0:T(8,128)(2,1)} %get-tuple-element.508), channel_id=1, source_target_pairs={{0,4},{12,8},{1,5},{13,9},{2,6},{14,10},{3,7},{15,11},{16,20},{28,... | collective-permute-start | bytes 1572872 | tf_op jit(solution)/shard_map/ppermute | solution.py:566
  237.8 10.8 %attend_back.2.refs_3_.refs_2_.project_grad = bf16[3,1024,256]{2,1,0:T(8,128)(2,1)S(1)} custom-call(s32[1,1024]{1,0:T(1,128)S(1)} %bitcast.118, bf16[3,1024,256]{2,1,0:T(8,128)(2,1)S(1)} %copy-done.18, bf16[1024,256]{1,0:T(8,128)(2,1)S(1)} %get-tuple-element.503.grads, f32[2,2,1024]{2,1,0:T(2,128)S(1)} %reshape.189.logsum, ...), custom_call_target="tpu_custom_call" | custom-call | flops 12099999744 | bytes 35200000 | tf_op jit(solution)/shard_map/attend_back/pallas_call | solution.py:334
  258.3 6.2 %weight_grads.4 = bf16[4,128,3072]{2,1,0:T(8,128)(2,1)} custom-call(bf16[1024,1024]{1,0:T(8,128)(2,1)S(1)} %copy-done.28, bf16[1024,1024]{1,0:T(8,128)(2,1)S(1)} %copy-done.31, bf16[1024,1024]{1,0:T(8,128)(2,1)S(1)} %copy-done.40, bf16[3,1024,256]{2,1,0:T(8,128)(2,1)S(1)} %attend_back.2.refs_3_.refs_2_.project_grad, bf16[1024,256]{1,0:T(8,128)(2,1)S(1)} %copy-done.49, ...), custom_call_target="tpu_custom_call" | custom-call | flops 9900000256 | bytes 28800000 | tf_op jit(solution)/shard_map/weight_grads/pallas_call | solution.py:423
  269.0 4.6 collective-permute-start.48
  285.9 5.5 %weight_grads.5.kept = bf16[4,128,3072]{2,1,0:T(8,128)(2,1)S(1)} custom-call(bf16[1024,1024]{1,0:T(8,128)(2,1)S(1)} %copy-done.29, bf16[1024,1024]{1,0:T(8,128)(2,1)S(1)} %copy-done.32, bf16[1024,1024]{1,0:T(8,128)(2,1)S(1)} %copy-done.41, bf16[3,1024,256]{2,1,0:T(8,128)(2,1)S(1)} %copy-done.26, bf16[1024,256]{1,0:T(8,128)(2,1)S(1)} %copy-done.50, ...), custom_call_target="tpu_custom_call" | custom-call | flops 9900000256 | bytes 28800000 | tf_op jit(solution)/shard_map/weight_grads/pallas_call | solution.py:423
  291.4 10.8 %collective-permute-done.46 = bf16[256,1024]{1,0:T(8,128)(2,1)S(1)} collective-permute-done((bf16[256,1024]{1,0:T(8,128)(2,1)S(1)}, bf16[256,1024]{1,0:T(8,128)(2,1)S(1)}, u32[]{:S(2)}, u32[]{:S(2)}) %collective-permute-start.46) | collective-permute-done | bytes 524320 | tf_op jit(solution)/shard_map/ppermute | solution.py:566
  306.7 4.1 fold.2
  310.8 18.6 %collective-permute-done.49.refs_0_ = bf16[256,1024]{1,0:T(8,128)(2,1)S(1)} collective-permute-done((bf16[256,1024]{1,0:T(8,128)(2,1)S(1)}, bf16[256,1024]{1,0:T(8,128)(2,1)S(1)}, u32[]{:S(2)}, u32[]{:S(2)}) %collective-permute-start.49) | collective-permute-done | bytes 524320 | tf_op jit(solution)/shard_map/ppermute | solution.py:566
  335.8 8.4 %collective-permute-done.51.refs_1_ = bf16[256,1024]{1,0:T(8,128)(2,1)S(1)} collective-permute-done((bf16[256,1024]{1,0:T(8,128)(2,1)S(1)}, bf16[256,1024]{1,0:T(8,128)(2,1)S(1)}, u32[]{:S(2)}, u32[]{:S(2)}) %collective-permute-start.51) | collective-permute-done | bytes 524320 | tf_op jit(solution)/shard_map/ppermute | solution.py:566
  345.7 10.8 %attend_back.3.refs_3_.refs_2_.project_grad = bf16[3,1024,256]{2,1,0:T(8,128)(2,1)S(1)} custom-call(s32[1,1024]{1,0:T(1,128)S(1)} %bitcast.119, bf16[3,1024,256]{2,1,0:T(8,128)(2,1)S(1)} %copy-done.20, bf16[1024,256]{1,0:T(8,128)(2,1)S(1)} %get-tuple-element.561.grads, f32[2,2,1024]{2,1,0:T(2,128)S(1)} %reshape.190.logsum, ...), custom_call_target="tpu_custom_call" | custom-call | flops 12099999744 | bytes 35200000 | tf_op jit(solution)/shard_map/attend_back/pallas_call | solution.py:334
  358.1 3.5 collective-permute-start.56
  366.0 5.5 %weight_grads.6 = bf16[4,128,3072]{2,1,0:T(8,128)(2,1)S(1)} custom-call(bf16[1024,1024]{1,0:T(8,128)(2,1)S(1)} %copy-done.34, bf16[1024,1024]{1,0:T(8,128)(2,1)S(1)} %copy-done.36, bf16[1024,1024]{1,0:T(8,128)(2,1)S(1)} %get-tuple-element.586.upstream, bf16[3,1024,256]{2,1,0:T(8,128)(2,1)S(1)} %attend_back.3.refs_3_.refs_2_.project_grad, ...), custom_call_target="tpu_custom_call" | custom-call | flops 9900000256 | bytes 28800000 | tf_op jit(solution)/shard_map/weight_grads/pallas_call | solution.py:423
  377.9 5.5 %weight_grads.7.kept = bf16[4,128,3072]{2,1,0:T(8,128)(2,1)S(1)} custom-call(bf16[1024,1024]{1,0:T(8,128)(2,1)S(1)} %copy-done.34, bf16[1024,1024]{1,0:T(8,128)(2,1)S(1)} %copy-done.36, bf16[1024,1024]{1,0:T(8,128)(2,1)S(1)} %get-tuple-element.586.upstream, bf16[3,1024,256]{2,1,0:T(8,128)(2,1)S(1)} %attend_back.3.refs_3_.refs_2_.project_grad, ...), custom_call_target="tpu_custom_call" | custom-call | flops 9900000256 | bytes 28800000 | tf_op jit(solution)/shard_map/weight_grads/pallas_call | solution.py:423
  397.8 30.1 %collective-permute-done.65 = bf16[256,1024]{1,0:T(8,128)(2,1)} collective-permute-done((bf16[256,1024]{1,0:T(8,128)(2,1)}, bf16[256,1024]{1,0:T(8,128)(2,1)}, u32[]{:S(2)}, u32[]{:S(2)}) %collective-permute-start.65) | collective-permute-done | bytes 524320 | tf_op jit(solution)/shard_map/ppermute | solution.py:566
  433.3 5.8 %collective-permute-done.69 = bf16[256,1024]{1,0:T(8,128)(2,1)S(1)} collective-permute-done((bf16[256,1024]{1,0:T(8,128)(2,1)S(1)}, bf16[256,1024]{1,0:T(8,128)(2,1)S(1)}, u32[]{:S(2)}, u32[]{:S(2)}) %collective-permute-start.69) | collective-permute-done | bytes 524320 | tf_op jit(solution)/shard_map/ppermute | solution.py:566
  451.2 3.7 collective-permute-done.72
  (478 shorter events, 204.9 us)
Async XLA Ops:
  13.9 25.8 %collective-permute-start.10 = (bf16[256,1024]{1,0:T(8,128)(2,1)S(1)}, bf16[256,1024]{1,0:T(8,128)(2,1)S(1)}, u32[]{:S(2)}, u32[]{:S(2)}) collective-permute-start(bf16[256,1024]{1,0:T(8,128)(2,1)S(1)} %get-tuple-element.577.refs_0_), channel_id=1, source_target_pairs={{0,8},{8,0},{4,12},{12,4},{1,9},{9,1},{5,13},{13,5},{2,10},{10,2},... | collective-permute-start | bytes 1572872 | tf_op jit(solution)/shard_map/ppermute | solution.py:566
  15.6 24.0 %collective-permute-start.11 = (bf16[256,1024]{1,0:T(8,128)(2,1)S(1)}, bf16[256,1024]{1,0:T(8,128)(2,1)}, u32[]{:S(2)}, u32[]{:S(2)}) collective-permute-start(bf16[256,1024]{1,0:T(8,128)(2,1)S(1)} %get-tuple-element.577.refs_0_), channel_id=1, source_target_pairs={{0,4},{4,0},{8,12},{12,8},{1,5},{5,1},{9,13},{13,9},{2,6},{6,2},{1... | collective-permute-start | bytes 1572872 | tf_op jit(solution)/shard_map/ppermute | solution.py:566
  58.0 24.8 %collective-permute-start.21 = (bf16[256,1024]{1,0:T(8,128)(2,1)S(1)}, bf16[256,1024]{1,0:T(8,128)(2,1)S(1)}, u32[]{:S(2)}, u32[]{:S(2)}) collective-permute-start(bf16[256,1024]{1,0:T(8,128)(2,1)S(1)} %get-tuple-element.577.refs_0_), channel_id=1, source_target_pairs={{4,8},{8,4},{5,9},{9,5},{6,10},{10,6},{7,11},{11,7},{20,24},{24,20... | collective-permute-start | bytes 1572872 | tf_op jit(solution)/shard_map/ppermute | solution.py:566
  64.1 26.2 %collective-permute-start.19 = (bf16[128,3072]{1,0:T(8,128)(2,1)}, bf16[128,3072]{1,0:T(8,128)(2,1)S(1)}, u32[]{:S(2)}, u32[]{:S(2)}) collective-permute-start(bf16[128,3072]{1,0:T(8,128)(2,1)} %get-tuple-element.417.refs_0_), channel_id=1, source_target_pairs={{0,1},{1,0},{2,3},{3,2},{4,5},{5,4},{6,7},{7,6},{8,9},{9,8},{10,11... | collective-permute-start | bytes 2359304 | tf_op jit(solution)/shard_map/ppermute | solution.py:535
  65.2 25.1 %collective-permute-start.20 = (bf16[128,3072]{1,0:T(8,128)(2,1)}, bf16[128,3072]{1,0:T(8,128)(2,1)S(1)}, u32[]{:S(2)}, u32[]{:S(2)}) collective-permute-start(bf16[128,3072]{1,0:T(8,128)(2,1)} %get-tuple-element.417.refs_0_), channel_id=1, source_target_pairs={{0,2},{1,3},{2,0},{3,1},{4,6},{5,7},{6,4},{7,5},{8,10},{9,11},{10,... | collective-permute-start | bytes 2359304 | tf_op jit(solution)/shard_map/ppermute | solution.py:535
  91.4 37.0 %collective-permute-start.34 = (bf16[256,1024]{1,0:T(8,128)(2,1)S(1)}, bf16[256,1024]{1,0:T(8,128)(2,1)S(1)}, u32[]{:S(2)}, u32[]{:S(2)}) collective-permute-start(bf16[256,1024]{1,0:T(8,128)(2,1)S(1)} %dynamic-slice_bitcast_fusion.refs_0_), channel_id=1, source_target_pairs={{0,8},{8,0},{4,12},{12,4},{1,9},{9,1},{5,13},{13,5},{2,10},{10,2},... | collective-permute-start | bytes 1572872 | tf_op jit(solution)/shard_map/ppermute | solution.py:566
  93.3 35.2 %collective-permute-start.35 = (bf16[256,1024]{1,0:T(8,128)(2,1)S(1)}, bf16[256,1024]{1,0:T(8,128)(2,1)S(1)}, u32[]{:S(2)}, u32[]{:S(2)}) collective-permute-start(bf16[256,1024]{1,0:T(8,128)(2,1)S(1)} %dynamic-slice_bitcast_fusion.refs_0_), channel_id=1, source_target_pairs={{0,4},{4,0},{8,12},{12,8},{1,5},{5,1},{9,13},{13,9},{2,6},{6,2},{1... | collective-permute-start | bytes 1572872 | tf_op jit(solution)/shard_map/ppermute | solution.py:566
  93.3 32.2 %collective-permute-start.23 = (bf16[256,1024]{1,0:T(8,128)(2,1)S(1)}, bf16[256,1024]{1,0:T(8,128)(2,1)S(1)}, u32[]{:S(2)}, u32[]{:S(2)}) collective-permute-start(bf16[256,1024]{1,0:T(8,128)(2,1)S(1)} %get-tuple-element.388), channel_id=1, source_target_pairs={{0,4},{12,8},{1,5},{13,9},{2,6},{14,10},{3,7},{15,11},{16,20},{28,... | collective-permute-start | bytes 1572872 | tf_op jit(solution)/shard_map/ppermute | solution.py:566
  96.7 28.8 %collective-permute-start.24 = (bf16[256,1024]{1,0:T(8,128)(2,1)S(1)}, bf16[256,1024]{1,0:T(8,128)(2,1)S(1)}, u32[]{:S(2)}, u32[]{:S(2)}) collective-permute-start(bf16[256,1024]{1,0:T(8,128)(2,1)S(1)} %get-tuple-element.388), channel_id=1, source_target_pairs={{4,8},{8,4},{5,9},{9,5},{6,10},{10,6},{7,11},{11,7},{20,24},{24,20... | collective-permute-start | bytes 1572872 | tf_op jit(solution)/shard_map/ppermute | solution.py:566
  127.9 27.4 %collective-permute-start.29 = (bf16[128,3072]{1,0:T(8,128)(2,1)S(1)}, bf16[128,3072]{1,0:T(8,128)(2,1)S(1)}, u32[]{:S(2)}, u32[]{:S(2)}) collective-permute-start(bf16[128,3072]{1,0:T(8,128)(2,1)S(1)} %copy-done.75), channel_id=1, source_target_pairs={{0,16},{16,0},{1,17},{17,1},{2,18},{18,2},{3,19},{19,3},{4,20},{20... | collective-permute-start | bytes 2359304 | tf_op jit(solution)/shard_map/ppermute | solution.py:535
  128.4 26.9 %collective-permute-start.30 = (bf16[128,3072]{1,0:T(8,128)(2,1)S(1)}, bf16[128,3072]{1,0:T(8,128)(2,1)S(1)}, u32[]{:S(2)}, u32[]{:S(2)}) collective-permute-start(bf16[128,3072]{1,0:T(8,128)(2,1)S(1)} %collective-permute-done.19.refs_1_), channel_id=1, source_target_pairs={{0,16},{16,0},{1,17},{17,1},{2,18},{18,2},{3,19},{19,3},{4,20},{20... | collective-permute-start | bytes 2359304 | tf_op jit(solution)/shard_map/ppermute | solution.py:535
  128.5 26.8 %collective-permute-start.31 = (bf16[128,3072]{1,0:T(8,128)(2,1)S(1)}, bf16[128,3072]{1,0:T(8,128)(2,1)S(1)}, u32[]{:S(2)}, u32[]{:S(2)}) collective-permute-start(bf16[128,3072]{1,0:T(8,128)(2,1)S(1)} %collective-permute-done.20.refs_2_), channel_id=1, source_target_pairs={{0,16},{16,0},{1,17},{17,1},{2,18},{18,2},{3,19},{19,3},{4,20},{20... | collective-permute-start | bytes 2359304 | tf_op jit(solution)/shard_map/ppermute | solution.py:535
  129.3 26.1 %collective-permute-start.27 = (bf16[256,1024]{1,0:T(8,128)(2,1)S(1)}, bf16[256,1024]{1,0:T(8,128)(2,1)S(1)}, u32[]{:S(2)}, u32[]{:S(2)}) collective-permute-start(bf16[256,1024]{1,0:T(8,128)(2,1)S(1)} %add_convert_fusion.3), channel_id=1, source_target_pairs={{0,8},{8,0},{4,12},{12,4},{1,9},{9,1},{5,13},{13,5},{2,10},{10,2},... | collective-permute-start | bytes 1572872 | tf_op jit(solution)/shard_map/ppermute | solution.py:566
  156.6 25.0 %collective-permute-start.36 = (bf16[256,1024]{1,0:T(8,128)(2,1)S(1)}, bf16[256,1024]{1,0:T(8,128)(2,1)S(1)}, u32[]{:S(2)}, u32[]{:S(2)}) collective-permute-start(bf16[256,1024]{1,0:T(8,128)(2,1)S(1)} %get-tuple-element.663.refs_0_), channel_id=1, source_target_pairs={{0,8},{8,0},{4,12},{12,4},{1,9},{9,1},{5,13},{13,5},{2,10},{10,2},... | collective-permute-start | bytes 1572872 | tf_op jit(solution)/shard_map/ppermute | solution.py:566
  158.0 23.6 %collective-permute-start.37 = (bf16[256,1024]{1,0:T(8,128)(2,1)S(1)}, bf16[256,1024]{1,0:T(8,128)(2,1)S(1)}, u32[]{:S(2)}, u32[]{:S(2)}) collective-permute-start(bf16[256,1024]{1,0:T(8,128)(2,1)S(1)} %get-tuple-element.663.refs_0_), channel_id=1, source_target_pairs={{0,4},{4,0},{8,12},{12,8},{1,5},{5,1},{9,13},{13,9},{2,6},{6,2},{1... | collective-permute-start | bytes 1572872 | tf_op jit(solution)/shard_map/ppermute | solution.py:566
  158.1 35.1 %collective-permute-start.39 = (bf16[256,1024]{1,0:T(8,128)(2,1)S(1)}, bf16[256,1024]{1,0:T(8,128)(2,1)S(1)}, u32[]{:S(2)}, u32[]{:S(2)}) collective-permute-start(bf16[256,1024]{1,0:T(8,128)(2,1)S(1)} %get-tuple-element.663.refs_0_), channel_id=1, source_target_pairs={{4,8},{8,4},{5,9},{9,5},{6,10},{10,6},{7,11},{11,7},{20,24},{24,20... | collective-permute-start | bytes 1572872 | tf_op jit(solution)/shard_map/ppermute | solution.py:566
  218.0 34.3 %collective-permute-start.42 = (bf16[256,1024]{1,0:T(8,128)(2,1)}, bf16[256,1024]{1,0:T(8,128)(2,1)}, u32[]{:S(2)}, u32[]{:S(2)}) collective-permute-start(bf16[256,1024]{1,0:T(8,128)(2,1)} %get-tuple-element.508), channel_id=1, source_target_pairs={{0,4},{12,8},{1,5},{13,9},{2,6},{14,10},{3,7},{15,11},{16,20},{28,... | collective-permute-start | bytes 1572872 | tf_op jit(solution)/shard_map/ppermute | solution.py:566
  224.0 28.3 %collective-permute-start.43 = (bf16[256,1024]{1,0:T(8,128)(2,1)}, bf16[256,1024]{1,0:T(8,128)(2,1)}, u32[]{:S(2)}, u32[]{:S(2)}) collective-permute-start(bf16[256,1024]{1,0:T(8,128)(2,1)} %get-tuple-element.508), channel_id=1, source_target_pairs={{4,8},{8,4},{5,9},{9,5},{6,10},{10,6},{7,11},{11,7},{20,24},{24,20... | collective-permute-start | bytes 1572872 | tf_op jit(solution)/shard_map/ppermute | solution.py:566
  269.0 33.2 %collective-permute-start.48 = (bf16[4,128,3072]{2,1,0:T(8,128)(2,1)}, bf16[4,128,3072]{2,1,0:T(8,128)(2,1)}, u32[]{:S(2)}, u32[]{:S(2)}) collective-permute-start(bf16[4,128,3072]{2,1,0:T(8,128)(2,1)} %weight_grads.4), channel_id=1, source_target_pairs={{0,16},{16,0},{1,17},{17,1},{2,18},{18,2},{3,19},{19,3},{4,20},{20... | collective-permute-start | bytes 9437192 | tf_op jit(solution)/shard_map/ppermute | solution.py:535
  276.7 25.5 %collective-permute-start.46 = (bf16[256,1024]{1,0:T(8,128)(2,1)S(1)}, bf16[256,1024]{1,0:T(8,128)(2,1)S(1)}, u32[]{:S(2)}, u32[]{:S(2)}) collective-permute-start(bf16[256,1024]{1,0:T(8,128)(2,1)S(1)} %add_convert_fusion.2), channel_id=1, source_target_pairs={{0,8},{8,0},{4,12},{12,4},{1,9},{9,1},{5,13},{13,5},{2,10},{10,2},... | collective-permute-start | bytes 1572872 | tf_op jit(solution)/shard_map/ppermute | solution.py:566
  278.6 23.6 %collective-permute-start.47 = (bf16[256,1024]{1,0:T(8,128)(2,1)}, bf16[256,1024]{1,0:T(8,128)(2,1)S(1)}, u32[]{:S(2)}, u32[]{:S(2)}) collective-permute-start(bf16[256,1024]{1,0:T(8,128)(2,1)} %copy-done.90), channel_id=1, source_target_pairs={{0,4},{4,0},{8,12},{12,8},{1,5},{5,1},{9,13},{13,9},{2,6},{6,2},{1... | collective-permute-start | bytes 1572872 | tf_op jit(solution)/shard_map/ppermute | solution.py:566
  303.4 26.0 %collective-permute-start.49 = (bf16[256,1024]{1,0:T(8,128)(2,1)S(1)}, bf16[256,1024]{1,0:T(8,128)(2,1)S(1)}, u32[]{:S(2)}, u32[]{:S(2)}) collective-permute-start(bf16[256,1024]{1,0:T(8,128)(2,1)S(1)} %fusion.17.refs_0_), channel_id=1, source_target_pairs={{0,8},{8,0},{4,12},{12,4},{1,9},{9,1},{5,13},{13,5},{2,10},{10,2},... | collective-permute-start | bytes 1572872 | tf_op jit(solution)/shard_map/ppermute | solution.py:566
  303.6 25.8 %collective-permute-start.50 = (bf16[256,1024]{1,0:T(8,128)(2,1)S(1)}, bf16[256,1024]{1,0:T(8,128)(2,1)S(1)}, u32[]{:S(2)}, u32[]{:S(2)}) collective-permute-start(bf16[256,1024]{1,0:T(8,128)(2,1)S(1)} %fusion.17.refs_0_), channel_id=1, source_target_pairs={{0,4},{4,0},{8,12},{12,8},{1,5},{5,1},{9,13},{13,9},{2,6},{6,2},{1... | collective-permute-start | bytes 1572872 | tf_op jit(solution)/shard_map/ppermute | solution.py:566
  304.3 31.5 %collective-permute-start.52 = (bf16[256,1024]{1,0:T(8,128)(2,1)S(1)}, bf16[256,1024]{1,0:T(8,128)(2,1)S(1)}, u32[]{:S(2)}, u32[]{:S(2)}) collective-permute-start(bf16[256,1024]{1,0:T(8,128)(2,1)S(1)} %fusion.17.refs_0_), channel_id=1, source_target_pairs={{4,8},{8,4},{5,9},{9,5},{6,10},{10,6},{7,11},{11,7},{20,24},{24,20... | collective-permute-start | bytes 1572872 | tf_op jit(solution)/shard_map/ppermute | solution.py:566
  332.8 25.3 %collective-permute-start.54 = (bf16[2,64,3072]{2,1,0:T(8,128)(2,1)S(1)}, bf16[2,64,3072]{2,1,0:T(8,128)(2,1)S(1)}, u32[]{:S(2)}, u32[]{:S(2)}) collective-permute-start(bf16[2,64,3072]{2,1,0:T(8,128)(2,1)S(1)} %get-tuple-element.567), channel_id=1, source_target_pairs={{0,1},{1,0},{2,3},{3,2},{4,5},{5,4},{6,7},{7,6},{8,9},{9,8},{10,11... | collective-permute-start | bytes 2359304 | tf_op jit(solution)/shard_map/ppermute | solution.py:535
  332.8 25.3 %collective-permute-start.55 = (bf16[2,64,3072]{2,1,0:T(8,128)(2,1)S(1)}, bf16[2,64,3072]{2,1,0:T(8,128)(2,1)S(1)}, u32[]{:S(2)}, u32[]{:S(2)}) collective-permute-start(bf16[2,64,3072]{2,1,0:T(8,128)(2,1)S(1)} %get-tuple-element.568), channel_id=1, source_target_pairs={{0,2},{1,3},{2,0},{3,1},{4,6},{5,7},{6,4},{7,5},{8,10},{9,11},{10,... | collective-permute-start | bytes 2359304 | tf_op jit(solution)/shard_map/ppermute | solution.py:535
  391.8 36.1 %collective-permute-start.65 = (bf16[256,1024]{1,0:T(8,128)(2,1)}, bf16[256,1024]{1,0:T(8,128)(2,1)}, u32[]{:S(2)}, u32[]{:S(2)}) collective-permute-start(bf16[256,1024]{1,0:T(8,128)(2,1)} %add_convert_fusion.1), channel_id=1, source_target_pairs={{0,8},{8,0},{4,12},{12,4},{1,9},{9,1},{5,13},{13,5},{2,10},{10,2},... | collective-permute-start | bytes 1572872 | tf_op jit(solution)/shard_map/ppermute | solution.py:566
  393.5 45.5 %collective-permute-start.67 = (bf16[2,64,3072]{2,1,0:T(8,128)(2,1)}, bf16[2,64,3072]{2,1,0:T(8,128)(2,1)S(1)}, u32[]{:S(2)}, u32[]{:S(2)}) collective-permute-start(bf16[2,64,3072]{2,1,0:T(8,128)(2,1)} %copy-done.86), channel_id=1, source_target_pairs={{0,1},{1,0},{2,3},{3,2},{4,5},{5,4},{6,7},{7,6},{8,9},{9,8},{10,11... | collective-permute-start | bytes 2359304 | tf_op jit(solution)/shard_map/ppermute | solution.py:535
  394.0 45.1 %collective-permute-start.68 = (bf16[2,64,3072]{2,1,0:T(8,128)(2,1)}, bf16[2,64,3072]{2,1,0:T(8,128)(2,1)S(1)}, u32[]{:S(2)}, u32[]{:S(2)}) collective-permute-start(bf16[2,64,3072]{2,1,0:T(8,128)(2,1)} %copy-done.85), channel_id=1, source_target_pairs={{0,2},{1,3},{2,0},{3,1},{4,6},{5,7},{6,4},{7,5},{8,10},{9,11},{10,... | collective-permute-start | bytes 2359304 | tf_op jit(solution)/shard_map/ppermute | solution.py:535
  396.7 42.3 %collective-permute-start.69 = (bf16[256,1024]{1,0:T(8,128)(2,1)S(1)}, bf16[256,1024]{1,0:T(8,128)(2,1)S(1)}, u32[]{:S(2)}, u32[]{:S(2)}) collective-permute-start(bf16[256,1024]{1,0:T(8,128)(2,1)S(1)} %add_convert_fusion), channel_id=1, source_target_pairs={{0,8},{8,0},{4,12},{12,4},{1,9},{9,1},{5,13},{13,5},{2,10},{10,2},... | collective-permute-start | bytes 1572872 | tf_op jit(solution)/shard_map/ppermute | solution.py:566
  397.4 41.7 %collective-permute-start.70 = (bf16[256,1024]{1,0:T(8,128)(2,1)}, bf16[256,1024]{1,0:T(8,128)(2,1)S(1)}, u32[]{:S(2)}, u32[]{:S(2)}) collective-permute-start(bf16[256,1024]{1,0:T(8,128)(2,1)} %copy-done.89), channel_id=1, source_target_pairs={{0,4},{4,0},{8,12},{12,8},{1,5},{5,1},{9,13},{13,9},{2,6},{6,2},{1... | collective-permute-start | bytes 1572872 | tf_op jit(solution)/shard_map/ppermute | solution.py:566
  429.8 28.2 %collective-permute-start.66 = (bf16[256,1024]{1,0:T(8,128)(2,1)S(1)}, bf16[256,1024]{1,0:T(8,128)(2,1)S(1)}, u32[]{:S(2)}, u32[]{:S(2)}) collective-permute-start(bf16[256,1024]{1,0:T(8,128)(2,1)S(1)} %get-tuple-element.660), channel_id=1, source_target_pairs={{0,16},{16,0},{1,17},{17,1},{2,18},{18,2},{3,19},{19,3},{4,20},{20... | collective-permute-start | bytes 1572872 | tf_op jit(solution)/shard_map/ppermute | solution.py:535
  (165 other events, 1940.6 us)

commit v5 on v4

--- a/solution.py
+++ b/solution.py
@@ -373,7 +373,7 @@
     return chunk_call(
         partial(through_inputs_body, len(chunk)),
         "through_inputs",
-        1.5,
+        0.3,
         index,
         [
             ((TOKENS, model), BF16, (TOKENS, model), HERE),
@@ -435,7 +435,7 @@
         out_specs=pl.BlockSpec((4, model // 8, 2 * width), lambda j: (0, 0, j)),
         out_shape=jax.ShapeDtypeStruct((4, model // 8, 12 * width), BF16),
         compiler_params=params(18),
-        cost_estimate=cost(9),
+        cost_estimate=cost(0.3),
         name="weight_grads",
     )(attn_in, feed_in, upstream, project_grad, context, pre_grad, active)
 
@@ -465,7 +465,7 @@
         out_specs=[block(2, rows // 2), block(2, rows // 2), block(4, rows // 2)],
         out_shape=[shape(2), shape(2), shape(4)],
         compiler_params=params(),
-        cost_estimate=cost(4),
+        cost_estimate=cost(0.3),
         name="fold",
     )(kept, came)
 
@@ -644,6 +644,13 @@
             chunks[number], row ^ number, norms[layer], project_grad, pre_grad, packs[layer]
         )
 
+    choose = lambda here, there: jnp.where(first, here, there)
+
+    def by_layer(zero, one):
+        away = swap(choose(one, zero), "section", 1)
+        here = choose(zero, one)
+        return jnp.stack([choose(here, away), choose(away, here)])
+
     def input_grad(total, own, own_grads):
         normed, scale = normalize(own)
         result = own_grads.astype(F32) + scale * (
@@ -694,38 +701,36 @@
     across0 = send_corner(side0, ahead0)
     mine = [half0, side0, ahead0]
     theirs = [swap(piece, "section", 1) for piece in mine]
-    mine, theirs, across0 = join(mine, theirs, across0)
+    mine, theirs, across0, chunks_x0, given = join(mine, theirs, across0, chunks_x0, given)
 
     theirs = theirs + [swap(piece, "section", 1) for piece in across0]
     mine, theirs, half1, given = join(mine + across0, theirs, half1, given)
 
+    far_g1, near_g1 = send_own(given)
     side1, ahead1 = send_sides(half1)
     packs = [assemble(place, mine + theirs), None]
     entered0 = ()
-    for number in range(3):
+    for number in range(4):
         entered0 = enter(entered0, chunks_x0[number], number, 0)
-    chunks_x0, entered0, packs, given = join(chunks_x0, entered0, packs, given)
-
-    far_g1, near_g1 = send_own(given)
-    entered0 = enter(entered0, chunks_x0[3], 3, 0)
     kept, last = leave((), entered0, 3, 0)
-    side1, ahead1, entered0, kept, last = join(side1, ahead1, entered0, kept, last)
+    far_g1, near_g1, side1, ahead1, entered0, kept, last, packs = join(
+        far_g1, near_g1, side1, ahead1, entered0, kept, last, packs
+    )
 
     passed_y0, middle_y0 = send_last(last)
-    across1 = send_corner(side1, ahead1)
     kept, far = leave(kept, entered0, 2, 0)
     kept, near = leave(kept, entered0, 1, 0)
     (context0, logsum0), share_of = leave(kept, entered0, 0, 0)
-    passed_y0, middle_y0, across1, far, near, share_of, context0, half1, side1, ahead1 = join(
-        passed_y0, middle_y0, across1, far, near, share_of, context0, half1, side1, ahead1
+    passed_g1, middle_g1 = pass_on(given, far_g1)
+    passed_y0, middle_y0, far, near, half1, side1, ahead1, passed_g1, middle_g1 = join(
+        passed_y0, middle_y0, far, near, half1, side1, ahead1, passed_g1, middle_g1
     )
 
     far_y0, near_y0 = send_sums(far, passed_y0, near)
+    across1 = send_corner(side1, ahead1)
     mine = [half1, side1, ahead1] + across1
     theirs = [swap(piece, "section", 1) for piece in mine]
-    far_y0, near_y0, mine, theirs, far_g1, near_g1 = join(
-        far_y0, near_y0, mine, theirs, far_g1, near_g1
-    )
+    far_y0, near_y0, mine, theirs = join(far_y0, near_y0, mine, theirs)
     total = add(share_of, near_y0) + add(middle_y0, far_y0)
     y0_own = (x_own.astype(F32) + total).astype(BF16)
 
@@ -733,49 +738,42 @@
     packs[1] = assemble(place, mine + theirs)
     entered1 = enter((), (y0_own,), 0, 1)
     branch1 = back_branch((), (given,), 0, entered1[5], 1)
-    far_x1, near_x1, entered1, branch1 = join(far_x1, near_x1, entered1, branch1)
+    far_x1, near_x1, y0_own, entered1, branch1 = join(far_x1, near_x1, y0_own, entered1, branch1)
 
     passed_x1, middle_x1 = pass_on(y0_own, far_x1)
     entered1 = enter(entered1, (near_x1,), 1, 1)
     branch1 = back_branch(branch1, (near_g1,), 1, entered1[5], 1)
     entered1 = enter(entered1, (far_x1,), 2, 1)
     branch1 = back_branch(branch1, (far_g1,), 2, entered1[5], 1)
-    passed_x1, middle_x1, entered1, branch1, given, far_g1 = join(
-        passed_x1, middle_x1, entered1, branch1, given, far_g1
-    )
+    passed_x1, middle_x1, entered1, branch1 = join(passed_x1, middle_x1, entered1, branch1)
 
     chunks_x1 = [(y0_own,), (near_x1,), (far_x1,), (middle_x1, passed_x1)]
-    passed_g1, middle_g1 = pass_on(given, far_g1)
     entered1 = enter(entered1, chunks_x1[3], 3, 1)
+    pre_grad1, context_grad1, grads1 = back_branch(
+        branch1, (middle_g1, passed_g1), 3, entered1[5], 1
+    )
+    context_grad1, entered1 = join(context_grad1, entered1)
     kept, last_b1 = leave((), entered1, 3, 1)
     kept, far_b1 = leave(kept, entered1, 2, 1)
     kept, near_b1 = leave(kept, entered1, 1, 1)
     (context1, logsum1), share_b1 = leave(kept, entered1, 0, 1)
-    passed_g1, middle_g1, last_b1, far_b1, near_b1, share_b1, context1, logsum1, entered1 = join(
-        passed_g1, middle_g1, last_b1, far_b1, near_b1, share_b1, context1, logsum1, entered1
-    )
-
-    passed_y1, middle_y1 = send_last(last_b1)
-    pre_grad1, context_grad1, grads1 = back_branch(
-        branch1, (middle_g1, passed_g1), 3, entered1[5], 1
-    )
+
     saved1 = (entered1[0], entered1[1], entered1[4], context1)
     project_grad1 = attend_back(starts, entered1[2], context_grad1, logsum1, tables)
     last, terms1 = back_inputs(chunks_x1, 3, 1, project_grad1, pre_grad1)
-    last, terms1, project_grad1, pre_grad1, passed_y1, middle_y1 = join(
-        last, terms1, project_grad1, pre_grad1, passed_y1, middle_y1
-    )
+    last, project_grad1 = join(last, project_grad1)
 
     passed_n1, middle_n1 = send_last(last)
     others = [back_inputs(chunks_x1, number, 1, project_grad1, pre_grad1) for number in (2, 1, 0)]
     (far, near, share_of), terms = zip(*others)
     terms1 = sum(terms, start=terms1)
+    far = add(far, passed_n1).astype(BF16)
     leaving1 = weight_grads(1, saved1, grads1, pre_grad1, project_grad1)
-    passed_n1, middle_n1, far, near, share_of, terms1, leaving1, project_grad1 = join(
-        passed_n1, middle_n1, far, near, share_of, terms1, leaving1, project_grad1
-    )
-
-    far_n1, near_n1 = send_sums(far, passed_n1, near)
+    far, middle_n1, near, leaving1, project_grad1 = join(
+        far, middle_n1, near, leaving1, project_grad1
+    )
+
+    far_n1, near_n1 = (along_row(far, TWO_OVER), along_row(near, ONE_OVER))
     came1 = swap(leaving1, "section", 1)
     kept1 = weight_grads(0, saved1, grads1, pre_grad1, project_grad1)
     far_n1, near_n1, came1, kept1 = join(far_n1, near_n1, came1, kept1)
@@ -784,76 +782,73 @@
 
     slope0 = entered0[5]
     far_g0, near_g0 = send_own(dx1_own)
+    side1, ahead1, rest1 = fold(kept1, came1)
+    first1, second1 = (swap(side1, "col", 1), swap(ahead1, "col", 2))
     branch0 = back_branch((), (dx1_own,), 0, slope0, 0)
-    side1, ahead1, rest1 = fold(kept1, came1)
-    far_g0, near_g0, branch0, side1, ahead1, rest1 = join(
-        far_g0, near_g0, branch0, side1, ahead1, rest1
-    )
-
+    far_g0, near_g0, dx1_own, last_b1 = join(far_g0, near_g0, dx1_own, last_b1)
+
+    passed_y1 = along_row(last_b1, INWARD)
     passed_g0, middle_g0 = pass_on(dx1_own, far_g0)
-    first1, second1 = (swap(side1, "col", 1), swap(ahead1, "col", 2))
     branch0 = back_branch(branch0, (near_g0,), 1, slope0, 0)
     branch0 = back_branch(branch0, (far_g0,), 2, slope0, 0)
-    far_b1 = add(far_b1, passed_y1).astype(BF16)
-    passed_g0, middle_g0, branch0, far_b1, near_b1 = join(
-        passed_g0, middle_g0, branch0, far_b1, near_b1
-    )
-
-    near_y1 = along_row(near_b1, ONE_OVER)
+    passed_g0, middle_g0, first1, second1, last_b1, near_b1, far_b1, passed_y1 = join(
+        passed_g0, middle_g0, first1, second1, last_b1, near_b1, far_b1, passed_y1
+    )
+
+    passed1 = (
+        swap(add(rest1[1], first1[1]).astype(BF16), "col", 2),
+        swap(add(rest1[3], second1[1]).astype(BF16), "col", 1),
+    )
+    far_y1, near_y1 = send_sums(far_b1, passed_y1, near_b1)
     pre_grad0, context_grad0, grads0 = back_branch(branch0, (middle_g0, passed_g0), 3, slope0, 0)
     saved0 = (entered0[0], entered0[1], entered0[4], context0)
     project_grad0 = attend_back(starts, entered0[2], context_grad0, logsum0, tables)
     last, terms0 = back_inputs(chunks_x0, 3, 0, project_grad0, pre_grad0)
-    last, terms0, project_grad0, near_y1, first1, second1 = join(
-        last, terms0, project_grad0, near_y1, first1, second1
+    last, project_grad0, passed1, far_y1, near_y1, last_b1 = join(
+        last, project_grad0, passed1, far_y1, near_y1, last_b1
     )
 
     passed_n0, middle_n0 = send_last(last)
-    passed1 = (
-        swap(add(rest1[1], first1[1]).astype(BF16), "col", 2),
-        swap(add(rest1[3], second1[1]).astype(BF16), "col", 1),
-    )
     leaving0 = weight_grads(1, saved0, grads0, pre_grad0, project_grad0)
     others = [back_inputs(chunks_x0, number, 0, project_grad0, pre_grad0) for number in (2, 1, 0)]
     (far, near, share_of), terms = zip(*others)
-    terms = jnp.stack([sum(terms, start=terms0), terms1])
-    passed_n0, middle_n0, far, near, share_of, terms, leaving0, project_grad0, passed1 = join(
-        passed_n0, middle_n0, far, near, share_of, terms, leaving0, project_grad0, passed1
+    terms = sum_over(sum_over(jnp.stack([sum(terms, start=terms0), terms1]), "section"), "col")
+    passed_n0, middle_n0, far, near, terms, leaving0, project_grad0 = join(
+        passed_n0, middle_n0, far, near, terms, leaving0, project_grad0
     )
 
     far_n0, near_n0 = send_sums(far, passed_n0, near)
     came0 = swap(leaving0, "section", 1)
-    terms = sum_over(terms, "section")
     kept0 = weight_grads(0, saved0, grads0, pre_grad0, project_grad0)
-    came0, kept0, terms = join(came0, kept0, terms)
-
     side0, ahead0, rest0 = fold(kept0, came0)
-    terms = sum_over(terms, "col")
-    side0, ahead0, rest0, terms, far_b1 = join(side0, ahead0, rest0, terms, far_b1)
+    sums1 = (
+        add(add(rest1[0], first1[0]), passed1[0]),
+        add(add(rest1[2], second1[0]), passed1[1]),
+    )
+    far_n0, near_n0, side0, ahead0, terms, sums1, last_b1 = join(
+        far_n0, near_n0, side0, ahead0, terms, sums1, last_b1
+    )
 
     first0, second0 = (swap(side0, "col", 1), swap(ahead0, "col", 2))
-    far_y1 = along_row(far_b1, TWO_OVER)
-    first0, second0, far_n0, near_n0, terms = join(first0, second0, far_n0, near_n0, terms)
+    middle_y1 = along_row(last_b1, MIDDLE)
+    total = add(share_of, near_n0) + add(middle_n0, far_n0)
+    dx0_own = input_grad(total, x_own, dx1_own)
+    terms, dx0_own = join(terms, dx0_own)
+    terms = sum_over(terms, "row")
+    first0, second0, dx0_own, middle_y1, terms = join(first0, second0, dx0_own, middle_y1, terms)
 
     passed0 = (
         swap(add(rest0[1], first0[1]).astype(BF16), "col", 2),
         swap(add(rest0[3], second0[1]).astype(BF16), "col", 1),
     )
-    terms = sum_over(terms, "row")
     total = add(share_b1, near_y1) + add(middle_y1, far_y1)
     y1_own = (y0_own.astype(F32) + total).astype(BF16)
-    total = add(share_of, near_n0) + add(middle_n0, far_n0)
-    dx0_own = input_grad(total, x_own, dx1_own)
-    sums1 = (
-        add(add(rest1[0], first1[0]), passed1[0]),
-        add(add(rest1[2], second1[0]), passed1[1]),
-    )
+    outputs = by_layer(y0_own, y1_own)
     sums0 = (
         add(add(rest0[0], first0[0]), passed0[0]),
         add(add(rest0[2], second0[0]), passed0[1]),
     )
 
-    choose = lambda here, there: jnp.where(first, here, there)
     leaving = jnp.concatenate([choose(b, a) for a, b in zip(sums0, sums1)]).astype(BF16)
     upper, lower = [choose(a, b) for a, b in zip(sums0, sums1)]
     qkv_grad, out_grad, up_grad, down_grad = unpack(
@@ -862,13 +857,8 @@
     terms = pick(terms, sec)
     terms = lax.dynamic_slice_in_dim(terms, (row * cols + col) * share, share, 1)
 
-    def by_layer(zero, one):
-        away = swap(choose(one, zero), "section", 1)
-        here = choose(zero, one)
-        return jnp.stack([choose(here, away), choose(away, here)])
-
     return (
-        by_layer(y0_own, y1_own)[None, :, None],
+        outputs[None, :, None],
         by_layer(dx0_own, dx1_own)[None, :, None],
         qkv_grad.reshape(1, block, 3, width),
         out_grad[None],

time: 470 us -> 444 us (0.945)
  waiting for transfers between devices: 162 us -> 124 us
  starting transfers between devices: 93.7 us -> 115 us
  local copies, waits for them, and re-layouts: 40.6 us -> 21.8 us
  Pallas kernels: 141 us -> 146 us
    ppermute x32, waiting for transfers between devices: 141 us -> 106 us  [along_row(): return lax.ppermute(block, 'row', pairs)]
    unnamed x242 -> x174, local copies, waits for them, and re-layouts: 34.7 us -> 16.5 us
    ppermute x46, starting transfers between devices: 51.6 us -> 69 us  [swap(): lax.ppermute(block, axis, [(i, i ^ bit) for i in range(lax.axis_size(axis...]
    pallas_call x32, Pallas kernels: 81.2 us -> 86.2 us  [chunk_call(): pl.pallas_call(kernel, grid_spec=pltpu.PrefetchScalarGridSpec(num_scalar_...]
  transfers between devices with their start and end apart: 78 -> 78, of which waited for: 22 -> 23; matrix products, arithmetic and copies ran while one was open for 6% -> 7% of each run, Pallas kernels for 30% -> 24%
where the time goes in v5:
time: 444 us; the launch traced here: 438 us
  Pallas kernels  146 us (33%)
  waiting for transfers between devices  124 us (28%)
  starting transfers between devices  115 us (26%)
  other arithmetic  28.2 us (6%)
  local copies, waits for them, and re-layouts  21.8 us (5%)
    ppermute x32, waiting for transfers between devices, along_row(): return lax.ppermute(block, 'row', pairs)  106 us
    pallas_call x32, Pallas kernels, chunk_call(): pl.pallas_call(kernel, grid_spec=pltpu.PrefetchScalarGridSpec(num_scalar_...  86.2 us
    ppermute x46, starting transfers between devices, swap(): lax.ppermute(block, axis, [(i, i ^ bit) for i in range(lax.axis_size(axis...  69 us
    ppermute x32, starting transfers between devices, along_row(): return lax.ppermute(block, 'row', pairs)  45.8 us
    pallas_call x4, Pallas kernels, weight_grads(): pl.pallas_call(outer_kernel, grid=(6,), in_specs=[left, left, left, pl.Bl...  22.6 us
    pallas_call x2, Pallas kernels, attend_back(): pl.pallas_call(attend_back_kernel, grid=(pairs,), in_specs=[pl.BlockSpec(...  22.2 us
    ppermute x46, waiting for transfers between devices, swap(): lax.ppermute(block, axis, [(i, i ^ bit) for i in range(lax.axis_size(axis...  18.5 us
    unnamed x174, local copies, waits for them, and re-layouts  16.5 us
  transfers between devices with their start and end apart: 78, of which 23 were waited for; matrix products, arithmetic and copies ran while one was open for 7% of the time, Pallas kernels for 24%

profile of v5, /device:TPU:1, one launch (start us, length us, event | category | flops | bytes accessed | tf_op | source)
XLA Modules:
  0.0 437.7 jit_solution(1139338444092173990)
XLA Ops:
  28.1 11.6 %collective-permute-done.10.refs_0_ = bf16[256,1024]{1,0:T(8,128)(2,1)} collective-permute-done((bf16[256,1024]{1,0:T(8,128)(2,1)S(1)}, bf16[256,1024]{1,0:T(8,128)(2,1)}, u32[]{:S(2)}, u32[]{:S(2)}) %collective-permute-start.10) | collective-permute-done | bytes 524320 | tf_op jit(solution)/shard_map/ppermute | solution.py:566
  43.6 3.7 collective-permute-start.13
  53.0 7.1 %collective-permute-done.16.refs_4_ = bf16[64,3072]{1,0:T(8,128)(2,1)} collective-permute-done((bf16[64,3072]{1,0:T(8,128)(2,1)}, bf16[64,3072]{1,0:T(8,128)(2,1)}, u32[]{:S(2)}, u32[]{:S(2)}) %collective-permute-start.16) | collective-permute-done | bytes 393248 | tf_op jit(solution)/shard_map/ppermute | solution.py:535
  60.0 4.9 %collective-permute-done.18.refs_1_ = bf16[256,1024]{1,0:T(8,128)(2,1)} collective-permute-done((bf16[256,1024]{1,0:T(8,128)(2,1)}, bf16[256,1024]{1,0:T(8,128)(2,1)}, u32[]{:S(2)}, u32[]{:S(2)}) %collective-permute-start.18) | collective-permute-done | bytes 524320 | tf_op jit(solution)/shard_map/ppermute | solution.py:566
  73.4 5.5 %assemble.2.refs_2_.refs_3_.refs_4_.refs_5_.refs_1_.refs_6_ = bf16[1024,3072]{1,0:T(8,128)(2,1)S(1)} custom-call(s32[2]{0:T(128)S(1)} %pad_add_fusion.place, bf16[128,3072]{1,0:T(8,128)(2,1)} %get-tuple-element.317.refs_0_, bf16[128,3072]{1,0:T(8,128)(2,1)} %collective-permute-done.8.refs_1_, bf16[128,3072]{1,0:T(8,128)(2,1)} %collective-permute-done.9.refs_2_, ...), custom_call_target="tpu_custom_call" | custom-call | flops 6600000000 | bytes 19200000 | tf_op jit(solution)/shard_map/assemble/pallas_call | solution.py:487
  82.6 3.6 project.9
  86.3 4.6 %project.10 = (bf16[1024,1024]{1,0:T(8,128)(2,1)S(1)}, bf16[1024,1024]{1,0:T(8,128)(2,1)S(1)}, bf16[3,1024,256]{2,1,0:T(8,128)(2,1)S(1)}, bf16[256,1024]{1,0:T(8...) custom-call(s32[3]{0:T(128)S(1)} %get-tuple-element.637.number, ...), custom_call_target="tpu_custom_call", output_to_operand_aliasing={{0}: (7, {}), {1}: (8, {}), {2}: (9, {}), {3}: (10, {}), {4... | custom-call | flops 3849999872 | bytes 11200000 | tf_op jit(solution)/shard_map/project/pallas_call | solution.py:100
  90.9 4.6 %project.11 = (bf16[1024,1024]{1,0:T(8,128)(2,1)S(1)}, bf16[1024,1024]{1,0:T(8,128)(2,1)S(1)}, bf16[3,1024,256]{2,1,0:T(8,128)(2,1)S(1)}, bf16[256,1024]{1,0:T(8...) custom-call(s32[3]{0:T(128)S(1)} %get-tuple-element.636.number, ...), custom_call_target="tpu_custom_call", output_to_operand_aliasing={{0}: (8, {}), {1}: (9, {}), {2}: (10, {}), {3}: (11, {}), {... | custom-call | flops 3849999872 | bytes 11200000 | tf_op jit(solution)/shard_map/project/pallas_call | solution.py:100
  98.9 5.4 %collective-permute-start.25 = (bf16[256,1024]{1,0:T(8,128)(2,1)S(1)}, bf16[256,1024]{1,0:T(8,128)(2,1)S(1)}, u32[]{:S(2)}, u32[]{:S(2)}) collective-permute-start(bf16[256,1024]{1,0:T(8,128)(2,1)S(1)} %get-tuple-element.370), channel_id=1, source_target_pairs={{0,4},{12,8},{1,5},{13,9},{2,6},{14,10},{3,7},{15,11},{16,20},{28,... | collective-permute-start | bytes 1572872 | tf_op jit(solution)/shard_map/ppermute | solution.py:566
  113.7 4.6 %collective-permute-done.27.refs_1_ = bf16[256,1024]{1,0:T(8,128)(2,1)S(1)} collective-permute-done((bf16[256,1024]{1,0:T(8,128)(2,1)S(1)}, bf16[256,1024]{1,0:T(8,128)(2,1)S(1)}, u32[]{:S(2)}, u32[]{:S(2)}) %collective-permute-start.27) | collective-permute-done | bytes 524320 | tf_op jit(solution)/shard_map/ppermute | solution.py:566
  120.9 4.1 collective-permute-start.34
  126.0 3.9 collective-permute-start.33
  130.2 14.4 %collective-permute-done.29 = bf16[256,1024]{1,0:T(8,128)(2,1)S(1)} collective-permute-done((bf16[256,1024]{1,0:T(8,128)(2,1)S(1)}, bf16[256,1024]{1,0:T(8,128)(2,1)S(1)}, u32[]{:S(2)}, u32[]{:S(2)}) %collective-permute-start.29) | collective-permute-done | bytes 524320 | tf_op jit(solution)/shard_map/ppermute | solution.py:566
  153.6 3.6 project.12
  158.7 16.2 %collective-permute-done.38.refs_0_ = bf16[256,1024]{1,0:T(8,128)(2,1)S(1)} collective-permute-done((bf16[256,1024]{1,0:T(8,128)(2,1)S(1)}, bf16[256,1024]{1,0:T(8,128)(2,1)S(1)}, u32[]{:S(2)}, u32[]{:S(2)}) %collective-permute-start.38) | collective-permute-done | bytes 524320 | tf_op jit(solution)/shard_map/ppermute | solution.py:566
  177.2 3.6 project.13
  182.3 3.6 project.14
  195.5 4.3 attend.12
  215.1 11.0 %attend_back.2.refs_3_.refs_2_.project_grad = bf16[3,1024,256]{2,1,0:T(8,128)(2,1)S(1)} custom-call(s32[1,1024]{1,0:T(1,128)S(1)} %bitcast.109, bf16[3,1024,256]{2,1,0:T(8,128)(2,1)S(1)} %copy-done.13, bf16[1024,256]{1,0:T(8,128)(2,1)S(1)} %copy-done.37, f32[2,2,1024]{2,1,0:T(2,128)S(1)} %reshape.189.logsum, f32[1024,128]{1,0:T(8,128)S(1)} %copy-done.28, ...), custom_call_target="tpu_custom_call" | custom-call | flops 12099999744 | bytes 35200000 | tf_op jit(solution)/shard_map/attend_back/pallas_call | solution.py:334
  227.7 5.2 %collective-permute-start.42 = (bf16[256,1024]{1,0:T(8,128)(2,1)S(1)}, bf16[256,1024]{1,0:T(8,128)(2,1)S(1)}, u32[]{:S(2)}, u32[]{:S(2)}) collective-permute-start(bf16[256,1024]{1,0:T(8,128)(2,1)S(1)} %get-tuple-element.472), channel_id=1, source_target_pairs={{0,4},{12,8},{1,5},{13,9},{2,6},{14,10},{3,7},{15,11},{16,20},{28,... | collective-permute-start | bytes 1572872 | tf_op jit(solution)/shard_map/ppermute | solution.py:566
  237.9 5.8 %weight_grads.4 = bf16[4,128,3072]{2,1,0:T(8,128)(2,1)S(1)} custom-call(bf16[1024,1024]{1,0:T(8,128)(2,1)S(1)} %copy-done.17, bf16[1024,1024]{1,0:T(8,128)(2,1)S(1)} %copy-done.19, bf16[1024,1024]{1,0:T(8,128)(2,1)S(1)} %copy-done.25, bf16[3,1024,256]{2,1,0:T(8,128)(2,1)S(1)} %attend_back.2.refs_3_.refs_2_.project_grad, bf16[1024,256]{1,0:T(8,128)(2,1)S(1)} %copy-done.33, ...), custom_call_target="tpu_custom_call" | custom-call | flops 330000000 | bytes 960000 | tf_op jit(solution)/shard_map/weight_grads/pallas_call | solution.py:423
  251.0 5.6 %weight_grads.5.kept = bf16[4,128,3072]{2,1,0:T(8,128)(2,1)S(1)} custom-call(bf16[1024,1024]{1,0:T(8,128)(2,1)S(1)} %copy-done.17, bf16[1024,1024]{1,0:T(8,128)(2,1)S(1)} %copy-done.19, bf16[1024,1024]{1,0:T(8,128)(2,1)S(1)} %copy-done.25, bf16[3,1024,256]{2,1,0:T(8,128)(2,1)S(1)} %attend_back.2.refs_3_.refs_2_.project_grad, ...), custom_call_target="tpu_custom_call" | custom-call | flops 330000000 | bytes 960000 | tf_op jit(solution)/shard_map/weight_grads/pallas_call | solution.py:423
  256.5 16.2 %collective-permute-done.44 = bf16[256,1024]{1,0:T(8,128)(2,1)S(1)} collective-permute-done((bf16[256,1024]{1,0:T(8,128)(2,1)S(1)}, bf16[256,1024]{1,0:T(8,128)(2,1)S(1)}, u32[]{:S(2)}, u32[]{:S(2)}) %collective-permute-start.44) | collective-permute-done | bytes 524320 | tf_op jit(solution)/shard_map/ppermute | solution.py:566
  282.5 17.6 %collective-permute-done.47.refs_0_ = bf16[256,1024]{1,0:T(8,128)(2,1)} collective-permute-done((bf16[256,1024]{1,0:T(8,128)(2,1)}, bf16[256,1024]{1,0:T(8,128)(2,1)}, u32[]{:S(2)}, u32[]{:S(2)}) %collective-permute-start.47) | collective-permute-done | bytes 524320 | tf_op jit(solution)/shard_map/ppermute | solution.py:566
  302.1 5.9 %collective-permute-start.53 = (bf16[256,1024]{1,0:T(8,128)(2,1)}, bf16[256,1024]{1,0:T(8,128)(2,1)S(1)}, u32[]{:S(2)}, u32[]{:S(2)}) collective-permute-start(bf16[256,1024]{1,0:T(8,128)(2,1)} %get-tuple-element.555), channel_id=1, source_target_pairs={{0,4},{12,8},{1,5},{13,9},{2,6},{14,10},{3,7},{15,11},{16,20},{28,... | collective-permute-start | bytes 1572872 | tf_op jit(solution)/shard_map/ppermute | solution.py:566
  326.3 11.2 %attend_back.3.refs_3_.refs_2_.project_grad = bf16[3,1024,256]{2,1,0:T(8,128)(2,1)S(1)} custom-call(s32[1,1024]{1,0:T(1,128)S(1)} %bitcast.110, bf16[3,1024,256]{2,1,0:T(8,128)(2,1)S(1)} %copy-done.15, bf16[1024,256]{1,0:T(8,128)(2,1)S(1)} %get-tuple-element.508.grads, f32[2,2,1024]{2,1,0:T(2,128)S(1)} %reshape.190.logsum, f32[1024,128]{1,0:T(8,128)S(1)} %copy-done.29, ...), custom_call_target="tpu_custom_call" | custom-call | flops 12099999744 | bytes 35200000 | tf_op jit(solution)/shard_map/attend_back/pallas_call | solution.py:334
  351.7 5.3 %collective-permute-start.60 = (f32[2,4,1024]{2,1,0:T(4,128)S(1)}, f32[2,4,1024]{2,1,0:T(4,128)S(1)}, u32[]{:S(2)}, u32[]{:S(2)}) collective-permute-start(f32[2,4,1024]{2,1,0:T(4,128)S(1)} %pad_maximum_fusion.2), channel_id=1, source_target_pairs={{0,16},{16,0},{1,17},{17,1},{2,18},{18,2},{3,19},{19,3},{4,20},{20... | collective-permute-start | bytes 98312 | tf_op jit(solution)/shard_map/ppermute | solution.py:535
  360.6 5.8 %weight_grads.6 = bf16[4,128,3072]{2,1,0:T(8,128)(2,1)S(1)} custom-call(bf16[1024,1024]{1,0:T(8,128)(2,1)S(1)} %copy-done.21, bf16[1024,1024]{1,0:T(8,128)(2,1)S(1)} %copy-done.23, bf16[1024,1024]{1,0:T(8,128)(2,1)S(1)} %get-tuple-element.534.upstream, bf16[3,1024,256]{2,1,0:T(8,128)(2,1)S(1)} %attend_back.3.refs_3_.refs_2_.project_grad, ...), custom_call_target="tpu_custom_call" | custom-call | flops 330000000 | bytes 960000 | tf_op jit(solution)/shard_map/weight_grads/pallas_call | solution.py:423
  372.3 5.6 %weight_grads.7.kept = bf16[4,128,3072]{2,1,0:T(8,128)(2,1)S(1)} custom-call(bf16[1024,1024]{1,0:T(8,128)(2,1)S(1)} %copy-done.21, bf16[1024,1024]{1,0:T(8,128)(2,1)S(1)} %copy-done.23, bf16[1024,1024]{1,0:T(8,128)(2,1)S(1)} %get-tuple-element.534.upstream, bf16[3,1024,256]{2,1,0:T(8,128)(2,1)S(1)} %attend_back.3.refs_3_.refs_2_.project_grad, ...), custom_call_target="tpu_custom_call" | custom-call | flops 330000000 | bytes 960000 | tf_op jit(solution)/shard_map/weight_grads/pallas_call | solution.py:423
  380.4 13.2 %collective-permute-done.64 = bf16[256,1024]{1,0:T(8,128)(2,1)S(1)} collective-permute-done((bf16[256,1024]{1,0:T(8,128)(2,1)S(1)}, bf16[256,1024]{1,0:T(8,128)(2,1)S(1)}, u32[]{:S(2)}, u32[]{:S(2)}) %collective-permute-start.64) | collective-permute-done | bytes 524320 | tf_op jit(solution)/shard_map/ppermute | solution.py:566
  403.5 8.7 %collective-permute-start.70 = (f32[2,4,1024]{2,1,0:T(4,128)S(1)}, f32[2,4,1024]{2,1,0:T(4,128)S(1)}, u32[]{:S(2)}, u32[]{:S(2)}) collective-permute-start(f32[2,4,1024]{2,1,0:T(4,128)S(1)} %add_add_fusion.3), channel_id=1, source_target_pairs={{0,4},{4,0},{8,12},{12,8},{1,5},{5,1},{9,13},{13,9},{2,6},{6,2},{1... | collective-permute-start | bytes 98312 | tf_op jit(solution)/shard_map/ppermute | solution.py:535
  417.5 4.8 %collective-permute-start.74 = (bf16[256,1024]{1,0:T(8,128)(2,1)S(1)}, bf16[256,1024]{1,0:T(8,128)(2,1)S(1)}, u32[]{:S(2)}, u32[]{:S(2)}) collective-permute-start(bf16[256,1024]{1,0:T(8,128)(2,1)S(1)} %broadcast_select_fusion.2), channel_id=1, source_target_pairs={{0,16},{16,0},{1,17},{17,1},{2,18},{18,2},{3,19},{19,3},{4,20},{20... | collective-permute-start | bytes 1572872 | tf_op jit(solution)/shard_map/ppermute | solution.py:535
  (413 shorter events, 203.9 us)
Async XLA Ops:
  13.9 25.9 %collective-permute-start.10 = (bf16[256,1024]{1,0:T(8,128)(2,1)S(1)}, bf16[256,1024]{1,0:T(8,128)(2,1)}, u32[]{:S(2)}, u32[]{:S(2)}) collective-permute-start(bf16[256,1024]{1,0:T(8,128)(2,1)S(1)} %get-tuple-element.331.refs_0_), channel_id=1, source_target_pairs={{0,8},{8,0},{4,12},{12,4},{1,9},{9,1},{5,13},{13,5},{2,10},{10,2},... | collective-permute-start | bytes 1572872 | tf_op jit(solution)/shard_map/ppermute | solution.py:566
  15.6 24.1 %collective-permute-start.11 = (bf16[256,1024]{1,0:T(8,128)(2,1)S(1)}, bf16[256,1024]{1,0:T(8,128)(2,1)S(1)}, u32[]{:S(2)}, u32[]{:S(2)}) collective-permute-start(bf16[256,1024]{1,0:T(8,128)(2,1)S(1)} %get-tuple-element.331.refs_0_), channel_id=1, source_target_pairs={{0,4},{4,0},{8,12},{12,8},{1,5},{5,1},{9,13},{13,9},{2,6},{6,2},{1... | collective-permute-start | bytes 1572872 | tf_op jit(solution)/shard_map/ppermute | solution.py:566
  22.0 25.7 %collective-permute-start.17 = (bf16[256,1024]{1,0:T(8,128)(2,1)S(1)}, bf16[256,1024]{1,0:T(8,128)(2,1)S(1)}, u32[]{:S(2)}, u32[]{:S(2)}) collective-permute-start(bf16[256,1024]{1,0:T(8,128)(2,1)S(1)} %get-tuple-element.331.refs_0_), channel_id=1, source_target_pairs={{4,8},{8,4},{5,9},{9,5},{6,10},{10,6},{7,11},{11,7},{20,24},{24,20... | collective-permute-start | bytes 1572872 | tf_op jit(solution)/shard_map/ppermute | solution.py:566
  43.6 21.4 %collective-permute-start.13 = (bf16[128,3072]{1,0:T(8,128)(2,1)}, bf16[128,3072]{1,0:T(8,128)(2,1)}, u32[]{:S(2)}, u32[]{:S(2)}) collective-permute-start(bf16[128,3072]{1,0:T(8,128)(2,1)} %collective-permute-done.8.refs_1_), channel_id=1, source_target_pairs={{0,16},{16,0},{1,17},{17,1},{2,18},{18,2},{3,19},{19,3},{4,20},{20... | collective-permute-start | bytes 2359304 | tf_op jit(solution)/shard_map/ppermute | solution.py:535
  68.6 30.3 %collective-permute-start.23 = (bf16[128,3072]{1,0:T(8,128)(2,1)}, bf16[128,3072]{1,0:T(8,128)(2,1)S(1)}, u32[]{:S(2)}, u32[]{:S(2)}) collective-permute-start(bf16[128,3072]{1,0:T(8,128)(2,1)} %get-tuple-element.385.refs_0_), channel_id=1, source_target_pairs={{0,1},{1,0},{2,3},{3,2},{4,5},{5,4},{6,7},{7,6},{8,9},{9,8},{10,11... | collective-permute-start | bytes 2359304 | tf_op jit(solution)/shard_map/ppermute | solution.py:535
  69.9 29.0 %collective-permute-start.24 = (bf16[128,3072]{1,0:T(8,128)(2,1)}, bf16[128,3072]{1,0:T(8,128)(2,1)S(1)}, u32[]{:S(2)}, u32[]{:S(2)}) collective-permute-start(bf16[128,3072]{1,0:T(8,128)(2,1)} %get-tuple-element.385.refs_0_), channel_id=1, source_target_pairs={{0,2},{1,3},{2,0},{3,1},{4,6},{5,7},{6,4},{7,5},{8,10},{9,11},{10,... | collective-permute-start | bytes 2359304 | tf_op jit(solution)/shard_map/ppermute | solution.py:535
  71.1 27.7 %collective-permute-start.21 = (bf16[256,1024]{1,0:T(8,128)(2,1)S(1)}, bf16[256,1024]{1,0:T(8,128)(2,1)S(1)}, u32[]{:S(2)}, u32[]{:S(2)}) collective-permute-start(bf16[256,1024]{1,0:T(8,128)(2,1)S(1)} %dynamic-slice_bitcast_fusion.refs_0_), channel_id=1, source_target_pairs={{0,8},{8,0},{4,12},{12,4},{1,9},{9,1},{5,13},{13,5},{2,10},{10,2},... | collective-permute-start | bytes 1572872 | tf_op jit(solution)/shard_map/ppermute | solution.py:566
  72.5 26.3 %collective-permute-start.22 = (bf16[256,1024]{1,0:T(8,128)(2,1)S(1)}, bf16[256,1024]{1,0:T(8,128)(2,1)S(1)}, u32[]{:S(2)}, u32[]{:S(2)}) collective-permute-start(bf16[256,1024]{1,0:T(8,128)(2,1)S(1)} %dynamic-slice_bitcast_fusion.refs_0_), channel_id=1, source_target_pairs={{0,4},{4,0},{8,12},{12,8},{1,5},{5,1},{9,13},{13,9},{2,6},{6,2},{1... | collective-permute-start | bytes 1572872 | tf_op jit(solution)/shard_map/ppermute | solution.py:566
  72.7 39.8 %collective-permute-start.28 = (bf16[256,1024]{1,0:T(8,128)(2,1)S(1)}, bf16[256,1024]{1,0:T(8,128)(2,1)S(1)}, u32[]{:S(2)}, u32[]{:S(2)}) collective-permute-start(bf16[256,1024]{1,0:T(8,128)(2,1)S(1)} %dynamic-slice_bitcast_fusion.refs_0_), channel_id=1, source_target_pairs={{4,8},{8,4},{5,9},{9,5},{6,10},{10,6},{7,11},{11,7},{20,24},{24,20... | collective-permute-start | bytes 1572872 | tf_op jit(solution)/shard_map/ppermute | solution.py:566
  119.1 25.6 %collective-permute-start.29 = (bf16[256,1024]{1,0:T(8,128)(2,1)S(1)}, bf16[256,1024]{1,0:T(8,128)(2,1)S(1)}, u32[]{:S(2)}, u32[]{:S(2)}) collective-permute-start(bf16[256,1024]{1,0:T(8,128)(2,1)S(1)} %add_convert_fusion.3), channel_id=1, source_target_pairs={{0,8},{8,0},{4,12},{12,4},{1,9},{9,1},{5,13},{13,5},{2,10},{10,2},... | collective-permute-start | bytes 1572872 | tf_op jit(solution)/shard_map/ppermute | solution.py:566
  119.3 25.9 %collective-permute-start.30 = (bf16[256,1024]{1,0:T(8,128)(2,1)S(1)}, bf16[256,1024]{1,0:T(8,128)(2,1)S(1)}, u32[]{:S(2)}, u32[]{:S(2)}) collective-permute-start(bf16[256,1024]{1,0:T(8,128)(2,1)S(1)} %get-tuple-element.378), channel_id=1, source_target_pairs={{0,4},{4,0},{8,12},{12,8},{1,5},{5,1},{9,13},{13,9},{2,6},{6,2},{1... | collective-permute-start | bytes 1572872 | tf_op jit(solution)/shard_map/ppermute | solution.py:566
  120.9 27.4 %collective-permute-start.34 = (bf16[128,3072]{1,0:T(8,128)(2,1)S(1)}, bf16[128,3072]{1,0:T(8,128)(2,1)S(1)}, u32[]{:S(2)}, u32[]{:S(2)}) collective-permute-start(bf16[128,3072]{1,0:T(8,128)(2,1)S(1)} %collective-permute-done.23.refs_1_), channel_id=1, source_target_pairs={{0,16},{16,0},{1,17},{17,1},{2,18},{18,2},{3,19},{19,3},{4,20},{20... | collective-permute-start | bytes 2359304 | tf_op jit(solution)/shard_map/ppermute | solution.py:535
  126.0 22.3 %collective-permute-start.33 = (bf16[128,3072]{1,0:T(8,128)(2,1)S(1)}, bf16[128,3072]{1,0:T(8,128)(2,1)S(1)}, u32[]{:S(2)}, u32[]{:S(2)}) collective-permute-start(bf16[128,3072]{1,0:T(8,128)(2,1)S(1)} %copy-done.59), channel_id=1, source_target_pairs={{0,16},{16,0},{1,17},{17,1},{2,18},{18,2},{3,19},{19,3},{4,20},{20... | collective-permute-start | bytes 2359304 | tf_op jit(solution)/shard_map/ppermute | solution.py:535
  129.9 18.4 %collective-permute-start.35 = (bf16[128,3072]{1,0:T(8,128)(2,1)S(1)}, bf16[128,3072]{1,0:T(8,128)(2,1)S(1)}, u32[]{:S(2)}, u32[]{:S(2)}) collective-permute-start(bf16[128,3072]{1,0:T(8,128)(2,1)S(1)} %collective-permute-done.24.refs_2_), channel_id=1, source_target_pairs={{0,16},{16,0},{1,17},{17,1},{2,18},{18,2},{3,19},{19,3},{4,20},{20... | collective-permute-start | bytes 2359304 | tf_op jit(solution)/shard_map/ppermute | solution.py:535
  149.5 25.5 %collective-permute-start.38 = (bf16[256,1024]{1,0:T(8,128)(2,1)S(1)}, bf16[256,1024]{1,0:T(8,128)(2,1)S(1)}, u32[]{:S(2)}, u32[]{:S(2)}) collective-permute-start(bf16[256,1024]{1,0:T(8,128)(2,1)S(1)} %get-tuple-element.404.refs_0_), channel_id=1, source_target_pairs={{0,8},{8,0},{4,12},{12,4},{1,9},{9,1},{5,13},{13,5},{2,10},{10,2},... | collective-permute-start | bytes 1572872 | tf_op jit(solution)/shard_map/ppermute | solution.py:566
  149.8 25.2 %collective-permute-start.39 = (bf16[256,1024]{1,0:T(8,128)(2,1)S(1)}, bf16[256,1024]{1,0:T(8,128)(2,1)S(1)}, u32[]{:S(2)}, u32[]{:S(2)}) collective-permute-start(bf16[256,1024]{1,0:T(8,128)(2,1)S(1)} %get-tuple-element.404.refs_0_), channel_id=1, source_target_pairs={{0,4},{4,0},{8,12},{12,8},{1,5},{5,1},{9,13},{13,9},{2,6},{6,2},{1... | collective-permute-start | bytes 1572872 | tf_op jit(solution)/shard_map/ppermute | solution.py:566
  243.9 28.8 %collective-permute-start.46 = (bf16[4,128,3072]{2,1,0:T(8,128)(2,1)S(1)}, bf16[4,128,3072]{2,1,0:T(8,128)(2,1)S(1)}, u32[]{:S(2)}, u32[]{:S(2)}) collective-permute-start(bf16[4,128,3072]{2,1,0:T(8,128)(2,1)S(1)} %weight_grads.4), channel_id=1, source_target_pairs={{0,16},{16,0},{1,17},{17,1},{2,18},{18,2},{3,19},{19,3},{4,20},{20... | collective-permute-start | bytes 9437192 | tf_op jit(solution)/shard_map/ppermute | solution.py:535
  246.1 26.6 %collective-permute-start.44 = (bf16[256,1024]{1,0:T(8,128)(2,1)S(1)}, bf16[256,1024]{1,0:T(8,128)(2,1)S(1)}, u32[]{:S(2)}, u32[]{:S(2)}) collective-permute-start(bf16[256,1024]{1,0:T(8,128)(2,1)S(1)} %add_convert_fusion.2), channel_id=1, source_target_pairs={{0,8},{8,0},{4,12},{12,4},{1,9},{9,1},{5,13},{13,5},{2,10},{10,2},... | collective-permute-start | bytes 1572872 | tf_op jit(solution)/shard_map/ppermute | solution.py:566
  249.2 23.5 %collective-permute-start.45 = (bf16[256,1024]{1,0:T(8,128)(2,1)S(1)}, bf16[256,1024]{1,0:T(8,128)(2,1)S(1)}, u32[]{:S(2)}, u32[]{:S(2)}) collective-permute-start(bf16[256,1024]{1,0:T(8,128)(2,1)S(1)} %get-tuple-element.479), channel_id=1, source_target_pairs={{0,4},{4,0},{8,12},{12,8},{1,5},{5,1},{9,13},{13,9},{2,6},{6,2},{1... | collective-permute-start | bytes 1572872 | tf_op jit(solution)/shard_map/ppermute | solution.py:566
  274.8 25.4 %collective-permute-start.47 = (bf16[256,1024]{1,0:T(8,128)(2,1)}, bf16[256,1024]{1,0:T(8,128)(2,1)}, u32[]{:S(2)}, u32[]{:S(2)}) collective-permute-start(bf16[256,1024]{1,0:T(8,128)(2,1)} %fusion.17.refs_0_), channel_id=1, source_target_pairs={{0,8},{8,0},{4,12},{12,4},{1,9},{9,1},{5,13},{13,5},{2,10},{10,2},... | collective-permute-start | bytes 1572872 | tf_op jit(solution)/shard_map/ppermute | solution.py:566
  276.4 23.7 %collective-permute-start.48 = (bf16[256,1024]{1,0:T(8,128)(2,1)}, bf16[256,1024]{1,0:T(8,128)(2,1)}, u32[]{:S(2)}, u32[]{:S(2)}) collective-permute-start(bf16[256,1024]{1,0:T(8,128)(2,1)} %fusion.17.refs_0_), channel_id=1, source_target_pairs={{0,4},{4,0},{8,12},{12,8},{1,5},{5,1},{9,13},{13,9},{2,6},{6,2},{1... | collective-permute-start | bytes 1572872 | tf_op jit(solution)/shard_map/ppermute | solution.py:566
  280.4 38.0 %collective-permute-start.51 = (bf16[2,64,3072]{2,1,0:T(8,128)(2,1)}, bf16[2,64,3072]{2,1,0:T(8,128)(2,1)}, u32[]{:S(2)}, u32[]{:S(2)}) collective-permute-start(bf16[2,64,3072]{2,1,0:T(8,128)(2,1)} %get-tuple-element.490), channel_id=1, source_target_pairs={{0,1},{1,0},{2,3},{3,2},{4,5},{5,4},{6,7},{7,6},{8,9},{9,8},{10,11... | collective-permute-start | bytes 2359304 | tf_op jit(solution)/shard_map/ppermute | solution.py:535
  281.3 37.1 %collective-permute-start.52 = (bf16[2,64,3072]{2,1,0:T(8,128)(2,1)}, bf16[2,64,3072]{2,1,0:T(8,128)(2,1)}, u32[]{:S(2)}, u32[]{:S(2)}) collective-permute-start(bf16[2,64,3072]{2,1,0:T(8,128)(2,1)} %get-tuple-element.491), channel_id=1, source_target_pairs={{0,2},{1,3},{2,0},{3,1},{4,6},{5,7},{6,4},{7,5},{8,10},{9,11},{10,... | collective-permute-start | bytes 2359304 | tf_op jit(solution)/shard_map/ppermute | solution.py:535
  300.1 18.3 %collective-permute-start.49 = (bf16[256,1024]{1,0:T(8,128)(2,1)}, bf16[256,1024]{1,0:T(8,128)(2,1)S(1)}, u32[]{:S(2)}, u32[]{:S(2)}) collective-permute-start(bf16[256,1024]{1,0:T(8,128)(2,1)} %collective-permute-done.47.refs_0_), channel_id=1, source_target_pairs={{4,0},{8,12},{5,1},{9,13},{6,2},{10,14},{7,3},{11,15},{20,16},{24,... | collective-permute-start | bytes 1572872 | tf_op jit(solution)/shard_map/ppermute | solution.py:566
  318.7 25.2 %collective-permute-start.56 = (bf16[256,1024]{1,0:T(8,128)(2,1)S(1)}, bf16[256,1024]{1,0:T(8,128)(2,1)S(1)}, u32[]{:S(2)}, u32[]{:S(2)}) collective-permute-start(bf16[256,1024]{1,0:T(8,128)(2,1)S(1)} %add_convert_fusion.1), channel_id=1, source_target_pairs={{0,8},{8,0},{4,12},{12,4},{1,9},{9,1},{5,13},{13,5},{2,10},{10,2},... | collective-permute-start | bytes 1572872 | tf_op jit(solution)/shard_map/ppermute | solution.py:566
  321.7 18.5 %collective-permute-start.54 = (bf16[64,3072]{1,0:T(8,128)(2,1)S(1)}, bf16[64,3072]{1,0:T(8,128)(2,1)S(1)}, u32[]{:S(2)}, u32[]{:S(2)}) collective-permute-start(bf16[64,3072]{1,0:T(8,128)(2,1)S(1)} %get-tuple-element.621), channel_id=1, source_target_pairs={{0,2},{1,3},{2,0},{3,1},{4,6},{5,7},{6,4},{7,5},{8,10},{9,11},{10,... | collective-permute-start | bytes 1179656 | tf_op jit(solution)/shard_map/ppermute | solution.py:535
  324.3 19.6 %collective-permute-start.57 = (bf16[256,1024]{1,0:T(8,128)(2,1)S(1)}, bf16[256,1024]{1,0:T(8,128)(2,1)S(1)}, u32[]{:S(2)}, u32[]{:S(2)}) collective-permute-start(bf16[256,1024]{1,0:T(8,128)(2,1)S(1)} %copy-done.65), channel_id=1, source_target_pairs={{0,4},{4,0},{8,12},{12,8},{1,5},{5,1},{9,13},{13,9},{2,6},{6,2},{1... | collective-permute-start | bytes 1572872 | tf_op jit(solution)/shard_map/ppermute | solution.py:566
  367.9 25.8 %collective-permute-start.64 = (bf16[256,1024]{1,0:T(8,128)(2,1)S(1)}, bf16[256,1024]{1,0:T(8,128)(2,1)S(1)}, u32[]{:S(2)}, u32[]{:S(2)}) collective-permute-start(bf16[256,1024]{1,0:T(8,128)(2,1)S(1)} %add_convert_fusion), channel_id=1, source_target_pairs={{0,8},{8,0},{4,12},{12,4},{1,9},{9,1},{5,13},{13,5},{2,10},{10,2},... | collective-permute-start | bytes 1572872 | tf_op jit(solution)/shard_map/ppermute | solution.py:566
  369.7 24.0 %collective-permute-start.65 = (bf16[256,1024]{1,0:T(8,128)(2,1)S(1)}, bf16[256,1024]{1,0:T(8,128)(2,1)S(1)}, u32[]{:S(2)}, u32[]{:S(2)}) collective-permute-start(bf16[256,1024]{1,0:T(8,128)(2,1)S(1)} %get-tuple-element.538), channel_id=1, source_target_pairs={{0,4},{4,0},{8,12},{12,8},{1,5},{5,1},{9,13},{13,9},{2,6},{6,2},{1... | collective-permute-start | bytes 1572872 | tf_op jit(solution)/shard_map/ppermute | solution.py:566
  394.2 19.7 %collective-permute-start.67 = (bf16[2,64,3072]{2,1,0:T(8,128)(2,1)}, bf16[2,64,3072]{2,1,0:T(8,128)(2,1)}, u32[]{:S(2)}, u32[]{:S(2)}) collective-permute-start(bf16[2,64,3072]{2,1,0:T(8,128)(2,1)} %get-tuple-element.547), channel_id=1, source_target_pairs={{0,1},{1,0},{2,3},{3,2},{4,5},{5,4},{6,7},{7,6},{8,9},{9,8},{10,11... | collective-permute-start | bytes 2359304 | tf_op jit(solution)/shard_map/ppermute | solution.py:535
  394.7 19.2 %collective-permute-start.68 = (bf16[2,64,3072]{2,1,0:T(8,128)(2,1)S(1)}, bf16[2,64,3072]{2,1,0:T(8,128)(2,1)}, u32[]{:S(2)}, u32[]{:S(2)}) collective-permute-start(bf16[2,64,3072]{2,1,0:T(8,128)(2,1)S(1)} %get-tuple-element.548), channel_id=1, source_target_pairs={{0,2},{1,3},{2,0},{3,1},{4,6},{5,7},{6,4},{7,5},{8,10},{9,11},{10,... | collective-permute-start | bytes 2359304 | tf_op jit(solution)/shard_map/ppermute | solution.py:535
  394.9 19.0 %collective-permute-start.69 = (bf16[256,1024]{1,0:T(8,128)(2,1)}, bf16[256,1024]{1,0:T(8,128)(2,1)}, u32[]{:S(2)}, u32[]{:S(2)}) collective-permute-start(bf16[256,1024]{1,0:T(8,128)(2,1)} %get-tuple-element.555), channel_id=1, source_target_pairs={{4,8},{8,4},{5,9},{9,5},{6,10},{10,6},{7,11},{11,7},{20,24},{24,20... | collective-permute-start | bytes 1572872 | tf_op jit(solution)/shard_map/ppermute | solution.py:566
  (131 other events, 1475.1 us)

commit v6 on v5

--- a/solution.py
+++ b/solution.py
@@ -722,8 +722,8 @@
     kept, near = leave(kept, entered0, 1, 0)
     (context0, logsum0), share_of = leave(kept, entered0, 0, 0)
     passed_g1, middle_g1 = pass_on(given, far_g1)
-    passed_y0, middle_y0, far, near, half1, side1, ahead1, passed_g1, middle_g1 = join(
-        passed_y0, middle_y0, far, near, half1, side1, ahead1, passed_g1, middle_g1
+    passed_y0, middle_y0, far, near, share_of, half1, side1, ahead1, passed_g1, middle_g1 = join(
+        passed_y0, middle_y0, far, near, share_of, half1, side1, ahead1, passed_g1, middle_g1
     )
 
     far_y0, near_y0 = send_sums(far, passed_y0, near)
@@ -785,7 +785,9 @@
     side1, ahead1, rest1 = fold(kept1, came1)
     first1, second1 = (swap(side1, "col", 1), swap(ahead1, "col", 2))
     branch0 = back_branch((), (dx1_own,), 0, slope0, 0)
-    far_g0, near_g0, dx1_own, last_b1 = join(far_g0, near_g0, dx1_own, last_b1)
+    far_g0, near_g0, dx1_own, last_b1, branch0 = join(
+        far_g0, near_g0, dx1_own, last_b1, branch0
+    )
 
     passed_y1 = along_row(last_b1, INWARD)
     passed_g0, middle_g0 = pass_on(dx1_own, far_g0)
@@ -799,13 +801,13 @@
         swap(add(rest1[1], first1[1]).astype(BF16), "col", 2),
         swap(add(rest1[3], second1[1]).astype(BF16), "col", 1),
     )
-    far_y1, near_y1 = send_sums(far_b1, passed_y1, near_b1)
+    far_y1 = along_row(add(far_b1, passed_y1).astype(BF16), TWO_OVER)
     pre_grad0, context_grad0, grads0 = back_branch(branch0, (middle_g0, passed_g0), 3, slope0, 0)
     saved0 = (entered0[0], entered0[1], entered0[4], context0)
     project_grad0 = attend_back(starts, entered0[2], context_grad0, logsum0, tables)
     last, terms0 = back_inputs(chunks_x0, 3, 0, project_grad0, pre_grad0)
-    last, project_grad0, passed1, far_y1, near_y1, last_b1 = join(
-        last, project_grad0, passed1, far_y1, near_y1, last_b1
+    last, project_grad0, passed1, far_y1, near_b1, last_b1 = join(
+        last, project_grad0, passed1, far_y1, near_b1, last_b1
     )
 
     passed_n0, middle_n0 = send_last(last)
@@ -825,17 +827,20 @@
         add(add(rest1[0], first1[0]), passed1[0]),
         add(add(rest1[2], second1[0]), passed1[1]),
     )
-    far_n0, near_n0, side0, ahead0, terms, sums1, last_b1 = join(
-        far_n0, near_n0, side0, ahead0, terms, sums1, last_b1
+    far_n0, near_n0, side0, ahead0, terms, sums1, last_b1, near_b1 = join(
+        far_n0, near_n0, side0, ahead0, terms, sums1, last_b1, near_b1
     )
 
     first0, second0 = (swap(side0, "col", 1), swap(ahead0, "col", 2))
-    middle_y1 = along_row(last_b1, MIDDLE)
+    middle_y1, near_y1 = (along_row(last_b1, MIDDLE), along_row(near_b1, ONE_OVER))
     total = add(share_of, near_n0) + add(middle_n0, far_n0)
     dx0_own = input_grad(total, x_own, dx1_own)
     terms, dx0_own = join(terms, dx0_own)
     terms = sum_over(terms, "row")
-    first0, second0, dx0_own, middle_y1, terms = join(first0, second0, dx0_own, middle_y1, terms)
+    grads_out = by_layer(dx0_own, dx1_own)
+    first0, second0, grads_out, middle_y1, near_y1, terms = join(
+        first0, second0, grads_out, middle_y1, near_y1, terms
+    )
 
     passed0 = (
         swap(add(rest0[1], first0[1]).astype(BF16), "col", 2),
@@ -859,7 +864,7 @@
 
     return (
         outputs[None, :, None],
-        by_layer(dx0_own, dx1_own)[None, :, None],
+        grads_out[None, :, None],
         qkv_grad.reshape(1, block, 3, width),
         out_grad[None],
         up_grad[None],

time: 444 us -> 440 us (level)
  starting transfers between devices: 115 us -> 106 us
  waiting for transfers between devices: 124 us -> 132 us
    ppermute x46, starting transfers between devices: 69 us -> 59.8 us  [swap(): lax.ppermute(block, axis, [(i, i ^ bit) for i in range(lax.axis_size(axis...]
    ppermute x46, waiting for transfers between devices: 18.5 us -> 24.1 us  [swap(): lax.ppermute(block, axis, [(i, i ^ bit) for i in range(lax.axis_size(axis...]
    unnamed x174 -> x172, local copies, waits for them, and re-layouts: 16.5 us -> 16.5 us
  transfers between devices with their start and end apart: 78 -> 78, of which waited for: 23 -> 30; matrix products, arithmetic and copies ran while one was open for 7% -> 6% of each run, Pallas kernels for 24% -> 25%
where the time goes in v6:
time: 440 us; the launch traced here: 434 us
  Pallas kernels  145 us (33%)
  waiting for transfers between devices  132 us (30%)
  starting transfers between devices  106 us (24%)
  other arithmetic  26.4 us (6%)
  local copies, waits for them, and re-layouts  21.8 us (5%)
    ppermute x32, waiting for transfers between devices, along_row(): return lax.ppermute(block, 'row', pairs)  108 us
    pallas_call x32, Pallas kernels, chunk_call(): pl.pallas_call(kernel, grid_spec=pltpu.PrefetchScalarGridSpec(num_scalar_...  85.4 us
    ppermute x46, starting transfers between devices, swap(): lax.ppermute(block, axis, [(i, i ^ bit) for i in range(lax.axis_size(axis...  59.8 us
    ppermute x32, starting transfers between devices, along_row(): return lax.ppermute(block, 'row', pairs)  46.1 us
    ppermute x46, waiting for transfers between devices, swap(): lax.ppermute(block, axis, [(i, i ^ bit) for i in range(lax.axis_size(axis...  24.1 us
    pallas_call x4, Pallas kernels, weight_grads(): pl.pallas_call(outer_kernel, grid=(6,), in_specs=[left, left, left, pl.Bl...  22.6 us
    pallas_call x2, Pallas kernels, attend_back(): pl.pallas_call(attend_back_kernel, grid=(pairs,), in_specs=[pl.BlockSpec(...  22.2 us
    unnamed x172, local copies, waits for them, and re-layouts  16.5 us
  transfers between devices with their start and end apart: 78, of which 30 were waited for; matrix products, arithmetic and copies ran while one was open for 6% of the time, Pallas kernels for 25%

profile of v6, /device:TPU:1, one launch (start us, length us, event | category | flops | bytes accessed | tf_op | source)
XLA Modules:
  0.0 433.6 jit_solution(16320920546376901554)
XLA Ops:
  28.1 11.6 %collective-permute-done.10.refs_0_ = bf16[256,1024]{1,0:T(8,128)(2,1)} collective-permute-done((bf16[256,1024]{1,0:T(8,128)(2,1)S(1)}, bf16[256,1024]{1,0:T(8,128)(2,1)}, u32[]{:S(2)}, u32[]{:S(2)}) %collective-permute-start.10) | collective-permute-done | bytes 524320 | tf_op jit(solution)/shard_map/ppermute | solution.py:566
  43.5 3.7 collective-permute-start.13
  53.0 7.1 %collective-permute-done.16.refs_4_ = bf16[64,3072]{1,0:T(8,128)(2,1)} collective-permute-done((bf16[64,3072]{1,0:T(8,128)(2,1)}, bf16[64,3072]{1,0:T(8,128)(2,1)}, u32[]{:S(2)}, u32[]{:S(2)}) %collective-permute-start.16) | collective-permute-done | bytes 393248 | tf_op jit(solution)/shard_map/ppermute | solution.py:535
  60.1 4.9 %collective-permute-done.18.refs_1_ = bf16[256,1024]{1,0:T(8,128)(2,1)} collective-permute-done((bf16[256,1024]{1,0:T(8,128)(2,1)}, bf16[256,1024]{1,0:T(8,128)(2,1)}, u32[]{:S(2)}, u32[]{:S(2)}) %collective-permute-start.18) | collective-permute-done | bytes 524320 | tf_op jit(solution)/shard_map/ppermute | solution.py:566
  73.4 5.5 %assemble.2.refs_2_.refs_3_.refs_4_.refs_5_.refs_1_.refs_6_ = bf16[1024,3072]{1,0:T(8,128)(2,1)S(1)} custom-call(s32[2]{0:T(128)S(1)} %pad_add_fusion.place, bf16[128,3072]{1,0:T(8,128)(2,1)} %get-tuple-element.322.refs_0_, bf16[128,3072]{1,0:T(8,128)(2,1)} %collective-permute-done.8.refs_1_, bf16[128,3072]{1,0:T(8,128)(2,1)} %collective-permute-done.9.refs_2_, ...), custom_call_target="tpu_custom_call" | custom-call | flops 6600000000 | bytes 19200000 | tf_op jit(solution)/shard_map/assemble/pallas_call | solution.py:487
  79.0 3.6 project.8
  82.6 3.6 project.9
  86.3 4.6 %project.10 = (bf16[1024,1024]{1,0:T(8,128)(2,1)S(1)}, bf16[1024,1024]{1,0:T(8,128)(2,1)S(1)}, bf16[3,1024,256]{2,1,0:T(8,128)(2,1)S(1)}, bf16[256,1024]{1,0:T(8...) custom-call(s32[3]{0:T(128)S(1)} %get-tuple-element.649.number, ...), custom_call_target="tpu_custom_call", output_to_operand_aliasing={{0}: (7, {}), {1}: (8, {}), {2}: (9, {}), {3}: (10, {}), {4... | custom-call | flops 3849999872 | bytes 11200000 | tf_op jit(solution)/shard_map/project/pallas_call | solution.py:100
  90.9 4.6 %project.11 = (bf16[1024,1024]{1,0:T(8,128)(2,1)S(1)}, bf16[1024,1024]{1,0:T(8,128)(2,1)S(1)}, bf16[3,1024,256]{2,1,0:T(8,128)(2,1)S(1)}, bf16[256,1024]{1,0:T(8...) custom-call(s32[3]{0:T(128)S(1)} %get-tuple-element.648.number, ...), custom_call_target="tpu_custom_call", output_to_operand_aliasing={{0}: (8, {}), {1}: (9, {}), {2}: (10, {}), {3}: (11, {}), {... | custom-call | flops 3849999872 | bytes 11200000 | tf_op jit(solution)/shard_map/project/pallas_call | solution.py:100
  98.9 5.5 %collective-permute-start.25 = (bf16[256,1024]{1,0:T(8,128)(2,1)S(1)}, bf16[256,1024]{1,0:T(8,128)(2,1)S(1)}, u32[]{:S(2)}, u32[]{:S(2)}) collective-permute-start(bf16[256,1024]{1,0:T(8,128)(2,1)S(1)} %get-tuple-element.365), channel_id=1, source_target_pairs={{0,4},{12,8},{1,5},{13,9},{2,6},{14,10},{3,7},{15,11},{16,20},{28,... | collective-permute-start | bytes 1572872 | tf_op jit(solution)/shard_map/ppermute | solution.py:566
  120.9 4.1 collective-permute-start.34
  126.0 3.9 collective-permute-start.33
  130.2 14.4 %collective-permute-done.29 = bf16[256,1024]{1,0:T(8,128)(2,1)S(1)} collective-permute-done((bf16[256,1024]{1,0:T(8,128)(2,1)S(1)}, bf16[256,1024]{1,0:T(8,128)(2,1)S(1)}, u32[]{:S(2)}, u32[]{:S(2)}) %collective-permute-start.29) | collective-permute-done | bytes 524320 | tf_op jit(solution)/shard_map/ppermute | solution.py:566
  152.2 3.6 project.12
  157.4 16.1 %collective-permute-done.38.refs_0_ = bf16[256,1024]{1,0:T(8,128)(2,1)S(1)} collective-permute-done((bf16[256,1024]{1,0:T(8,128)(2,1)S(1)}, bf16[256,1024]{1,0:T(8,128)(2,1)S(1)}, u32[]{:S(2)}, u32[]{:S(2)}) %collective-permute-start.38) | collective-permute-done | bytes 524320 | tf_op jit(solution)/shard_map/ppermute | solution.py:566
  175.6 3.6 project.13
  180.8 3.6 project.14
  188.1 3.6 project.15
  212.6 11.0 %attend_back.2.refs_3_.refs_2_.project_grad = bf16[3,1024,256]{2,1,0:T(8,128)(2,1)S(1)} custom-call(s32[1,1024]{1,0:T(1,128)S(1)} %bitcast.108, bf16[3,1024,256]{2,1,0:T(8,128)(2,1)S(1)} %copy-done.13, bf16[1024,256]{1,0:T(8,128)(2,1)S(1)} %copy-done.37, f32[2,2,1024]{2,1,0:T(2,128)S(1)} %reshape.189.logsum, f32[1024,128]{1,0:T(8,128)S(1)} %copy-done.28, ...), custom_call_target="tpu_custom_call" | custom-call | flops 12099999744 | bytes 35200000 | tf_op jit(solution)/shard_map/attend_back/pallas_call | solution.py:334
  225.2 5.2 %collective-permute-start.42 = (bf16[256,1024]{1,0:T(8,128)(2,1)S(1)}, bf16[256,1024]{1,0:T(8,128)(2,1)S(1)}, u32[]{:S(2)}, u32[]{:S(2)}) collective-permute-start(bf16[256,1024]{1,0:T(8,128)(2,1)S(1)} %get-tuple-element.479), channel_id=1, source_target_pairs={{0,4},{12,8},{1,5},{13,9},{2,6},{14,10},{3,7},{15,11},{16,20},{28,... | collective-permute-start | bytes 1572872 | tf_op jit(solution)/shard_map/ppermute | solution.py:566
  235.4 5.8 %weight_grads.4 = bf16[4,128,3072]{2,1,0:T(8,128)(2,1)S(1)} custom-call(bf16[1024,1024]{1,0:T(8,128)(2,1)S(1)} %copy-done.17, bf16[1024,1024]{1,0:T(8,128)(2,1)S(1)} %copy-done.19, bf16[1024,1024]{1,0:T(8,128)(2,1)S(1)} %copy-done.25, bf16[3,1024,256]{2,1,0:T(8,128)(2,1)S(1)} %attend_back.2.refs_3_.refs_2_.project_grad, bf16[1024,256]{1,0:T(8,128)(2,1)S(1)} %copy-done.33, ...), custom_call_target="tpu_custom_call" | custom-call | flops 330000000 | bytes 960000 | tf_op jit(solution)/shard_map/weight_grads/pallas_call | solution.py:423
  248.3 5.6 %weight_grads.5.kept = bf16[4,128,3072]{2,1,0:T(8,128)(2,1)S(1)} custom-call(bf16[1024,1024]{1,0:T(8,128)(2,1)S(1)} %copy-done.17, bf16[1024,1024]{1,0:T(8,128)(2,1)S(1)} %copy-done.19, bf16[1024,1024]{1,0:T(8,128)(2,1)S(1)} %copy-done.25, bf16[3,1024,256]{2,1,0:T(8,128)(2,1)S(1)} %attend_back.2.refs_3_.refs_2_.project_grad, ...), custom_call_target="tpu_custom_call" | custom-call | flops 330000000 | bytes 960000 | tf_op jit(solution)/shard_map/weight_grads/pallas_call | solution.py:423
  253.9 16.2 %collective-permute-done.44 = bf16[256,1024]{1,0:T(8,128)(2,1)S(1)} collective-permute-done((bf16[256,1024]{1,0:T(8,128)(2,1)S(1)}, bf16[256,1024]{1,0:T(8,128)(2,1)S(1)}, u32[]{:S(2)}, u32[]{:S(2)}) %collective-permute-start.44) | collective-permute-done | bytes 524320 | tf_op jit(solution)/shard_map/ppermute | solution.py:566
  285.6 11.9 %collective-permute-done.47.refs_0_ = bf16[256,1024]{1,0:T(8,128)(2,1)} collective-permute-done((bf16[256,1024]{1,0:T(8,128)(2,1)}, bf16[256,1024]{1,0:T(8,128)(2,1)}, u32[]{:S(2)}, u32[]{:S(2)}) %collective-permute-start.47) | collective-permute-done | bytes 524320 | tf_op jit(solution)/shard_map/ppermute | solution.py:566
  299.5 6.0 %collective-permute-start.53 = (bf16[256,1024]{1,0:T(8,128)(2,1)S(1)}, bf16[256,1024]{1,0:T(8,128)(2,1)S(1)}, u32[]{:S(2)}, u32[]{:S(2)}) collective-permute-start(bf16[256,1024]{1,0:T(8,128)(2,1)S(1)} %copy-done.65), channel_id=1, source_target_pairs={{0,4},{12,8},{1,5},{13,9},{2,6},{14,10},{3,7},{15,11},{16,20},{28,... | collective-permute-start | bytes 1572872 | tf_op jit(solution)/shard_map/ppermute | solution.py:566
  323.1 11.2 %attend_back.3.refs_3_.refs_2_.project_grad = bf16[3,1024,256]{2,1,0:T(8,128)(2,1)S(1)} custom-call(s32[1,1024]{1,0:T(1,128)S(1)} %bitcast.109, bf16[3,1024,256]{2,1,0:T(8,128)(2,1)S(1)} %copy-done.15, bf16[1024,256]{1,0:T(8,128)(2,1)S(1)} %get-tuple-element.518.grads, f32[2,2,1024]{2,1,0:T(2,128)S(1)} %reshape.190.logsum, f32[1024,128]{1,0:T(8,128)S(1)} %copy-done.29, ...), custom_call_target="tpu_custom_call" | custom-call | flops 12099999744 | bytes 35200000 | tf_op jit(solution)/shard_map/attend_back/pallas_call | solution.py:334
  353.2 5.7 %weight_grads.6 = bf16[4,128,3072]{2,1,0:T(8,128)(2,1)S(1)} custom-call(bf16[1024,1024]{1,0:T(8,128)(2,1)S(1)} %copy-done.21, bf16[1024,1024]{1,0:T(8,128)(2,1)S(1)} %copy-done.23, bf16[1024,1024]{1,0:T(8,128)(2,1)S(1)} %get-tuple-element.543.upstream, bf16[3,1024,256]{2,1,0:T(8,128)(2,1)S(1)} %attend_back.3.refs_3_.refs_2_.project_grad, ...), custom_call_target="tpu_custom_call" | custom-call | flops 330000000 | bytes 960000 | tf_op jit(solution)/shard_map/weight_grads/pallas_call | solution.py:423
  365.0 5.6 %weight_grads.7.kept = bf16[4,128,3072]{2,1,0:T(8,128)(2,1)S(1)} custom-call(bf16[1024,1024]{1,0:T(8,128)(2,1)S(1)} %copy-done.21, bf16[1024,1024]{1,0:T(8,128)(2,1)S(1)} %copy-done.23, bf16[1024,1024]{1,0:T(8,128)(2,1)S(1)} %get-tuple-element.543.upstream, bf16[3,1024,256]{2,1,0:T(8,128)(2,1)S(1)} %attend_back.3.refs_3_.refs_2_.project_grad, ...), custom_call_target="tpu_custom_call" | custom-call | flops 330000000 | bytes 960000 | tf_op jit(solution)/shard_map/weight_grads/pallas_call | solution.py:423
  373.2 13.0 %collective-permute-done.63 = bf16[256,1024]{1,0:T(8,128)(2,1)S(1)} collective-permute-done((bf16[256,1024]{1,0:T(8,128)(2,1)S(1)}, bf16[256,1024]{1,0:T(8,128)(2,1)S(1)}, u32[]{:S(2)}, u32[]{:S(2)}) %collective-permute-start.63) | collective-permute-done | bytes 524320 | tf_op jit(solution)/shard_map/ppermute | solution.py:566
  404.2 8.3 %collective-permute-done.70 = bf16[256,1024]{1,0:T(8,128)(2,1)S(1)} collective-permute-done((bf16[256,1024]{1,0:T(8,128)(2,1)}, bf16[256,1024]{1,0:T(8,128)(2,1)S(1)}, u32[]{:S(2)}, u32[]{:S(2)}) %collective-permute-start.70) | collective-permute-done | bytes 524320 | tf_op jit(solution)/shard_map/ppermute | solution.py:566
  415.0 3.7 collective-permute-start.74
  423.0 4.5 %collective-permute-start.77 = (bf16[128,3072]{1,0:T(8,128)(2,1)S(1)}, bf16[128,3072]{1,0:T(8,128)(2,1)S(1)}, u32[]{:S(2)}, u32[]{:S(2)}) collective-permute-start(bf16[128,3072]{1,0:T(8,128)(2,1)S(1)} %pad_maximum_fusion.2), channel_id=1, source_target_pairs={{0,16},{16,0},{1,17},{17,1},{2,18},{18,2},{3,19},{19,3},{4,20},{20... | collective-permute-start | bytes 2359304 | tf_op jit(solution)/shard_map/ppermute | solution.py:535
  (411 shorter events, 209.7 us)
Async XLA Ops:
  13.9 25.9 %collective-permute-start.10 = (bf16[256,1024]{1,0:T(8,128)(2,1)S(1)}, bf16[256,1024]{1,0:T(8,128)(2,1)}, u32[]{:S(2)}, u32[]{:S(2)}) collective-permute-start(bf16[256,1024]{1,0:T(8,128)(2,1)S(1)} %get-tuple-element.336.refs_0_), channel_id=1, source_target_pairs={{0,8},{8,0},{4,12},{12,4},{1,9},{9,1},{5,13},{13,5},{2,10},{10,2},... | collective-permute-start | bytes 1572872 | tf_op jit(solution)/shard_map/ppermute | solution.py:566
  15.6 24.1 %collective-permute-start.11 = (bf16[256,1024]{1,0:T(8,128)(2,1)S(1)}, bf16[256,1024]{1,0:T(8,128)(2,1)S(1)}, u32[]{:S(2)}, u32[]{:S(2)}) collective-permute-start(bf16[256,1024]{1,0:T(8,128)(2,1)S(1)} %get-tuple-element.336.refs_0_), channel_id=1, source_target_pairs={{0,4},{4,0},{8,12},{12,8},{1,5},{5,1},{9,13},{13,9},{2,6},{6,2},{1... | collective-permute-start | bytes 1572872 | tf_op jit(solution)/shard_map/ppermute | solution.py:566
  22.0 25.7 %collective-permute-start.17 = (bf16[256,1024]{1,0:T(8,128)(2,1)S(1)}, bf16[256,1024]{1,0:T(8,128)(2,1)S(1)}, u32[]{:S(2)}, u32[]{:S(2)}) collective-permute-start(bf16[256,1024]{1,0:T(8,128)(2,1)S(1)} %get-tuple-element.336.refs_0_), channel_id=1, source_target_pairs={{4,8},{8,4},{5,9},{9,5},{6,10},{10,6},{7,11},{11,7},{20,24},{24,20... | collective-permute-start | bytes 1572872 | tf_op jit(solution)/shard_map/ppermute | solution.py:566
  24.2 17.2 %collective-permute-start.8 = (bf16[128,3072]{1,0:T(8,128)(2,1)}, bf16[128,3072]{1,0:T(8,128)(2,1)}, u32[]{:S(2)}, u32[]{:S(2)}) collective-permute-start(bf16[128,3072]{1,0:T(8,128)(2,1)} %get-tuple-element.322.refs_0_), channel_id=1, source_target_pairs={{0,1},{1,0},{2,3},{3,2},{4,5},{5,4},{6,7},{7,6},{8,9},{9,8},{10,11... | collective-permute-start | bytes 2359304 | tf_op jit(solution)/shard_map/ppermute | solution.py:535
  24.3 17.1 %collective-permute-start.9 = (bf16[128,3072]{1,0:T(8,128)(2,1)}, bf16[128,3072]{1,0:T(8,128)(2,1)}, u32[]{:S(2)}, u32[]{:S(2)}) collective-permute-start(bf16[128,3072]{1,0:T(8,128)(2,1)} %get-tuple-element.322.refs_0_), channel_id=1, source_target_pairs={{0,2},{1,3},{2,0},{3,1},{4,6},{5,7},{6,4},{7,5},{8,10},{9,11},{10,... | collective-permute-start | bytes 2359304 | tf_op jit(solution)/shard_map/ppermute | solution.py:535
  43.5 21.4 %collective-permute-start.13 = (bf16[128,3072]{1,0:T(8,128)(2,1)}, bf16[128,3072]{1,0:T(8,128)(2,1)}, u32[]{:S(2)}, u32[]{:S(2)}) collective-permute-start(bf16[128,3072]{1,0:T(8,128)(2,1)} %collective-permute-done.8.refs_1_), channel_id=1, source_target_pairs={{0,16},{16,0},{1,17},{17,1},{2,18},{18,2},{3,19},{19,3},{4,20},{20... | collective-permute-start | bytes 2359304 | tf_op jit(solution)/shard_map/ppermute | solution.py:535
  47.2 17.7 %collective-permute-start.12 = (bf16[128,3072]{1,0:T(8,128)(2,1)}, bf16[128,3072]{1,0:T(8,128)(2,1)}, u32[]{:S(2)}, u32[]{:S(2)}) collective-permute-start(bf16[128,3072]{1,0:T(8,128)(2,1)} %get-tuple-element.322.refs_0_), channel_id=1, source_target_pairs={{0,16},{16,0},{1,17},{17,1},{2,18},{18,2},{3,19},{19,3},{4,20},{20... | collective-permute-start | bytes 2359304 | tf_op jit(solution)/shard_map/ppermute | solution.py:535
  47.2 17.7 %collective-permute-start.14 = (bf16[128,3072]{1,0:T(8,128)(2,1)}, bf16[128,3072]{1,0:T(8,128)(2,1)}, u32[]{:S(2)}, u32[]{:S(2)}) collective-permute-start(bf16[128,3072]{1,0:T(8,128)(2,1)} %collective-permute-done.9.refs_2_), channel_id=1, source_target_pairs={{0,16},{16,0},{1,17},{17,1},{2,18},{18,2},{3,19},{19,3},{4,20},{20... | collective-permute-start | bytes 2359304 | tf_op jit(solution)/shard_map/ppermute | solution.py:535
  68.6 30.3 %collective-permute-start.23 = (bf16[128,3072]{1,0:T(8,128)(2,1)}, bf16[128,3072]{1,0:T(8,128)(2,1)S(1)}, u32[]{:S(2)}, u32[]{:S(2)}) collective-permute-start(bf16[128,3072]{1,0:T(8,128)(2,1)} %get-tuple-element.392.refs_0_), channel_id=1, source_target_pairs={{0,1},{1,0},{2,3},{3,2},{4,5},{5,4},{6,7},{7,6},{8,9},{9,8},{10,11... | collective-permute-start | bytes 2359304 | tf_op jit(solution)/shard_map/ppermute | solution.py:535
  69.9 29.0 %collective-permute-start.24 = (bf16[128,3072]{1,0:T(8,128)(2,1)}, bf16[128,3072]{1,0:T(8,128)(2,1)S(1)}, u32[]{:S(2)}, u32[]{:S(2)}) collective-permute-start(bf16[128,3072]{1,0:T(8,128)(2,1)} %get-tuple-element.392.refs_0_), channel_id=1, source_target_pairs={{0,2},{1,3},{2,0},{3,1},{4,6},{5,7},{6,4},{7,5},{8,10},{9,11},{10,... | collective-permute-start | bytes 2359304 | tf_op jit(solution)/shard_map/ppermute | solution.py:535
  71.1 27.7 %collective-permute-start.21 = (bf16[256,1024]{1,0:T(8,128)(2,1)S(1)}, bf16[256,1024]{1,0:T(8,128)(2,1)S(1)}, u32[]{:S(2)}, u32[]{:S(2)}) collective-permute-start(bf16[256,1024]{1,0:T(8,128)(2,1)S(1)} %dynamic-slice_bitcast_fusion.refs_0_), channel_id=1, source_target_pairs={{0,8},{8,0},{4,12},{12,4},{1,9},{9,1},{5,13},{13,5},{2,10},{10,2},... | collective-permute-start | bytes 1572872 | tf_op jit(solution)/shard_map/ppermute | solution.py:566
  72.5 26.3 %collective-permute-start.22 = (bf16[256,1024]{1,0:T(8,128)(2,1)S(1)}, bf16[256,1024]{1,0:T(8,128)(2,1)S(1)}, u32[]{:S(2)}, u32[]{:S(2)}) collective-permute-start(bf16[256,1024]{1,0:T(8,128)(2,1)S(1)} %dynamic-slice_bitcast_fusion.refs_0_), channel_id=1, source_target_pairs={{0,4},{4,0},{8,12},{12,8},{1,5},{5,1},{9,13},{13,9},{2,6},{6,2},{1... | collective-permute-start | bytes 1572872 | tf_op jit(solution)/shard_map/ppermute | solution.py:566
  72.7 43.0 %collective-permute-start.28 = (bf16[256,1024]{1,0:T(8,128)(2,1)S(1)}, bf16[256,1024]{1,0:T(8,128)(2,1)S(1)}, u32[]{:S(2)}, u32[]{:S(2)}) collective-permute-start(bf16[256,1024]{1,0:T(8,128)(2,1)S(1)} %dynamic-slice_bitcast_fusion.refs_0_), channel_id=1, source_target_pairs={{4,8},{8,4},{5,9},{9,5},{6,10},{10,6},{7,11},{11,7},{20,24},{24,20... | collective-permute-start | bytes 1572872 | tf_op jit(solution)/shard_map/ppermute | solution.py:566
  119.1 25.6 %collective-permute-start.29 = (bf16[256,1024]{1,0:T(8,128)(2,1)S(1)}, bf16[256,1024]{1,0:T(8,128)(2,1)S(1)}, u32[]{:S(2)}, u32[]{:S(2)}) collective-permute-start(bf16[256,1024]{1,0:T(8,128)(2,1)S(1)} %add_convert_fusion.3), channel_id=1, source_target_pairs={{0,8},{8,0},{4,12},{12,4},{1,9},{9,1},{5,13},{13,5},{2,10},{10,2},... | collective-permute-start | bytes 1572872 | tf_op jit(solution)/shard_map/ppermute | solution.py:566
  119.3 25.9 %collective-permute-start.30 = (bf16[256,1024]{1,0:T(8,128)(2,1)S(1)}, bf16[256,1024]{1,0:T(8,128)(2,1)S(1)}, u32[]{:S(2)}, u32[]{:S(2)}) collective-permute-start(bf16[256,1024]{1,0:T(8,128)(2,1)S(1)} %get-tuple-element.385), channel_id=1, source_target_pairs={{0,4},{4,0},{8,12},{12,8},{1,5},{5,1},{9,13},{13,9},{2,6},{6,2},{1... | collective-permute-start | bytes 1572872 | tf_op jit(solution)/shard_map/ppermute | solution.py:566
  120.9 24.2 %collective-permute-start.34 = (bf16[128,3072]{1,0:T(8,128)(2,1)S(1)}, bf16[128,3072]{1,0:T(8,128)(2,1)S(1)}, u32[]{:S(2)}, u32[]{:S(2)}) collective-permute-start(bf16[128,3072]{1,0:T(8,128)(2,1)S(1)} %collective-permute-done.23.refs_1_), channel_id=1, source_target_pairs={{0,16},{16,0},{1,17},{17,1},{2,18},{18,2},{3,19},{19,3},{4,20},{20... | collective-permute-start | bytes 2359304 | tf_op jit(solution)/shard_map/ppermute | solution.py:535
  126.0 19.2 %collective-permute-start.33 = (bf16[128,3072]{1,0:T(8,128)(2,1)S(1)}, bf16[128,3072]{1,0:T(8,128)(2,1)S(1)}, u32[]{:S(2)}, u32[]{:S(2)}) collective-permute-start(bf16[128,3072]{1,0:T(8,128)(2,1)S(1)} %copy-done.59), channel_id=1, source_target_pairs={{0,16},{16,0},{1,17},{17,1},{2,18},{18,2},{3,19},{19,3},{4,20},{20... | collective-permute-start | bytes 2359304 | tf_op jit(solution)/shard_map/ppermute | solution.py:535
  148.1 25.3 %collective-permute-start.38 = (bf16[256,1024]{1,0:T(8,128)(2,1)S(1)}, bf16[256,1024]{1,0:T(8,128)(2,1)S(1)}, u32[]{:S(2)}, u32[]{:S(2)}) collective-permute-start(bf16[256,1024]{1,0:T(8,128)(2,1)S(1)} %get-tuple-element.411.refs_0_), channel_id=1, source_target_pairs={{0,8},{8,0},{4,12},{12,4},{1,9},{9,1},{5,13},{13,5},{2,10},{10,2},... | collective-permute-start | bytes 1572872 | tf_op jit(solution)/shard_map/ppermute | solution.py:566
  148.1 25.3 %collective-permute-start.39 = (bf16[256,1024]{1,0:T(8,128)(2,1)S(1)}, bf16[256,1024]{1,0:T(8,128)(2,1)S(1)}, u32[]{:S(2)}, u32[]{:S(2)}) collective-permute-start(bf16[256,1024]{1,0:T(8,128)(2,1)S(1)} %get-tuple-element.411.refs_0_), channel_id=1, source_target_pairs={{0,4},{4,0},{8,12},{12,8},{1,5},{5,1},{9,13},{13,9},{2,6},{6,2},{1... | collective-permute-start | bytes 1572872 | tf_op jit(solution)/shard_map/ppermute | solution.py:566
  241.4 28.7 %collective-permute-start.46 = (bf16[4,128,3072]{2,1,0:T(8,128)(2,1)S(1)}, bf16[4,128,3072]{2,1,0:T(8,128)(2,1)S(1)}, u32[]{:S(2)}, u32[]{:S(2)}) collective-permute-start(bf16[4,128,3072]{2,1,0:T(8,128)(2,1)S(1)} %weight_grads.4), channel_id=1, source_target_pairs={{0,16},{16,0},{1,17},{17,1},{2,18},{18,2},{3,19},{19,3},{4,20},{20... | collective-permute-start | bytes 9437192 | tf_op jit(solution)/shard_map/ppermute | solution.py:535
  243.8 26.3 %collective-permute-start.44 = (bf16[256,1024]{1,0:T(8,128)(2,1)S(1)}, bf16[256,1024]{1,0:T(8,128)(2,1)S(1)}, u32[]{:S(2)}, u32[]{:S(2)}) collective-permute-start(bf16[256,1024]{1,0:T(8,128)(2,1)S(1)} %add_convert_fusion.2), channel_id=1, source_target_pairs={{0,8},{8,0},{4,12},{12,4},{1,9},{9,1},{5,13},{13,5},{2,10},{10,2},... | collective-permute-start | bytes 1572872 | tf_op jit(solution)/shard_map/ppermute | solution.py:566
  246.6 23.5 %collective-permute-start.45 = (bf16[256,1024]{1,0:T(8,128)(2,1)S(1)}, bf16[256,1024]{1,0:T(8,128)(2,1)S(1)}, u32[]{:S(2)}, u32[]{:S(2)}) collective-permute-start(bf16[256,1024]{1,0:T(8,128)(2,1)S(1)} %get-tuple-element.486), channel_id=1, source_target_pairs={{0,4},{4,0},{8,12},{12,8},{1,5},{5,1},{9,13},{13,9},{2,6},{6,2},{1... | collective-permute-start | bytes 1572872 | tf_op jit(solution)/shard_map/ppermute | solution.py:566
  272.1 25.4 %collective-permute-start.47 = (bf16[256,1024]{1,0:T(8,128)(2,1)}, bf16[256,1024]{1,0:T(8,128)(2,1)}, u32[]{:S(2)}, u32[]{:S(2)}) collective-permute-start(bf16[256,1024]{1,0:T(8,128)(2,1)} %fusion.17.refs_0_), channel_id=1, source_target_pairs={{0,8},{8,0},{4,12},{12,4},{1,9},{9,1},{5,13},{13,5},{2,10},{10,2},... | collective-permute-start | bytes 1572872 | tf_op jit(solution)/shard_map/ppermute | solution.py:566
  273.9 23.6 %collective-permute-start.48 = (bf16[256,1024]{1,0:T(8,128)(2,1)}, bf16[256,1024]{1,0:T(8,128)(2,1)}, u32[]{:S(2)}, u32[]{:S(2)}) collective-permute-start(bf16[256,1024]{1,0:T(8,128)(2,1)} %fusion.17.refs_0_), channel_id=1, source_target_pairs={{0,4},{4,0},{8,12},{12,8},{1,5},{5,1},{9,13},{13,9},{2,6},{6,2},{1... | collective-permute-start | bytes 1572872 | tf_op jit(solution)/shard_map/ppermute | solution.py:566
  277.9 32.7 %collective-permute-start.51 = (bf16[2,64,3072]{2,1,0:T(8,128)(2,1)}, bf16[2,64,3072]{2,1,0:T(8,128)(2,1)}, u32[]{:S(2)}, u32[]{:S(2)}) collective-permute-start(bf16[2,64,3072]{2,1,0:T(8,128)(2,1)} %get-tuple-element.501), channel_id=1, source_target_pairs={{0,1},{1,0},{2,3},{3,2},{4,5},{5,4},{6,7},{7,6},{8,9},{9,8},{10,11... | collective-permute-start | bytes 2359304 | tf_op jit(solution)/shard_map/ppermute | solution.py:535
  279.0 31.6 %collective-permute-start.52 = (bf16[2,64,3072]{2,1,0:T(8,128)(2,1)}, bf16[2,64,3072]{2,1,0:T(8,128)(2,1)}, u32[]{:S(2)}, u32[]{:S(2)}) collective-permute-start(bf16[2,64,3072]{2,1,0:T(8,128)(2,1)} %get-tuple-element.502), channel_id=1, source_target_pairs={{0,2},{1,3},{2,0},{3,1},{4,6},{5,7},{6,4},{7,5},{8,10},{9,11},{10,... | collective-permute-start | bytes 2359304 | tf_op jit(solution)/shard_map/ppermute | solution.py:535
  314.9 24.7 %collective-permute-start.56 = (bf16[256,1024]{1,0:T(8,128)(2,1)S(1)}, bf16[256,1024]{1,0:T(8,128)(2,1)S(1)}, u32[]{:S(2)}, u32[]{:S(2)}) collective-permute-start(bf16[256,1024]{1,0:T(8,128)(2,1)S(1)} %add_convert_fusion.1), channel_id=1, source_target_pairs={{0,8},{8,0},{4,12},{12,4},{1,9},{9,1},{5,13},{13,5},{2,10},{10,2},... | collective-permute-start | bytes 1572872 | tf_op jit(solution)/shard_map/ppermute | solution.py:566
  318.9 18.1 %collective-permute-start.54 = (bf16[64,3072]{1,0:T(8,128)(2,1)S(1)}, bf16[64,3072]{1,0:T(8,128)(2,1)S(1)}, u32[]{:S(2)}, u32[]{:S(2)}) collective-permute-start(bf16[64,3072]{1,0:T(8,128)(2,1)S(1)} %get-tuple-element.633), channel_id=1, source_target_pairs={{0,2},{1,3},{2,0},{3,1},{4,6},{5,7},{6,4},{7,5},{8,10},{9,11},{10,... | collective-permute-start | bytes 1179656 | tf_op jit(solution)/shard_map/ppermute | solution.py:535
  360.5 25.7 %collective-permute-start.63 = (bf16[256,1024]{1,0:T(8,128)(2,1)S(1)}, bf16[256,1024]{1,0:T(8,128)(2,1)S(1)}, u32[]{:S(2)}, u32[]{:S(2)}) collective-permute-start(bf16[256,1024]{1,0:T(8,128)(2,1)S(1)} %add_convert_fusion), channel_id=1, source_target_pairs={{0,8},{8,0},{4,12},{12,4},{1,9},{9,1},{5,13},{13,5},{2,10},{10,2},... | collective-permute-start | bytes 1572872 | tf_op jit(solution)/shard_map/ppermute | solution.py:566
  362.3 23.9 %collective-permute-start.64 = (bf16[256,1024]{1,0:T(8,128)(2,1)S(1)}, bf16[256,1024]{1,0:T(8,128)(2,1)S(1)}, u32[]{:S(2)}, u32[]{:S(2)}) collective-permute-start(bf16[256,1024]{1,0:T(8,128)(2,1)S(1)} %get-tuple-element.547), channel_id=1, source_target_pairs={{0,4},{4,0},{8,12},{12,8},{1,5},{5,1},{9,13},{13,9},{2,6},{6,2},{1... | collective-permute-start | bytes 1572872 | tf_op jit(solution)/shard_map/ppermute | solution.py:566
  390.6 21.9 %collective-permute-start.66 = (bf16[2,64,3072]{2,1,0:T(8,128)(2,1)}, bf16[2,64,3072]{2,1,0:T(8,128)(2,1)}, u32[]{:S(2)}, u32[]{:S(2)}) collective-permute-start(bf16[2,64,3072]{2,1,0:T(8,128)(2,1)} %get-tuple-element.557), channel_id=1, source_target_pairs={{0,1},{1,0},{2,3},{3,2},{4,5},{5,4},{6,7},{7,6},{8,9},{9,8},{10,11... | collective-permute-start | bytes 2359304 | tf_op jit(solution)/shard_map/ppermute | solution.py:535
  392.3 20.2 %collective-permute-start.67 = (bf16[2,64,3072]{2,1,0:T(8,128)(2,1)S(1)}, bf16[2,64,3072]{2,1,0:T(8,128)(2,1)}, u32[]{:S(2)}, u32[]{:S(2)}) collective-permute-start(bf16[2,64,3072]{2,1,0:T(8,128)(2,1)S(1)} %get-tuple-element.558), channel_id=1, source_target_pairs={{0,2},{1,3},{2,0},{3,1},{4,6},{5,7},{6,4},{7,5},{8,10},{9,11},{10,... | collective-permute-start | bytes 2359304 | tf_op jit(solution)/shard_map/ppermute | solution.py:535
  (130 other events, 1306.1 us)
